TPU v7x, 32 devices: a whole 2x2x4 slice. The times are simulated.
32 devices in a mesh: grp: 8 (over z, x), tp: 4 (over y, core).
Axes of the slice: x: 2, y: 2, z: 4, core: 2. Of those that a mesh axis runs over, the one named last changes fastest.
Arguments:
- latents: bfloat16 [128, 128, 1024], P('grp', None, 'tp'), may hold values from -6 to 6
- skip_latents: bfloat16 [128, 128, 1024], P('grp', None, 'tp'), may hold values from -24 to 24
- points: bfloat16 [16384, 1024], P('grp'), may hold values from -6 to 6
- neighbours: int32 [128, 4], P('grp'), may hold values from 0 to 127, as said below
- block_lengths: int32 [128], replicated, may hold values from 32 to 128
- latent_embed: float32 [128, 1024], P(None, 'tp'), may hold values from -4 to 4
- gain_cross: float32 [1024], replicated, may hold values from 0.2 to 3
- query_cross: bfloat16 [1024, 1024], P(None, 'tp'), may hold values from -0.1875 to 0.1875
- key_cross: bfloat16 [1024, 1024], P(None, 'tp'), may hold values from -0.1875 to 0.1875
- value_cross: bfloat16 [1024, 1024], P(None, 'tp'), may hold values from -0.1875 to 0.1875
- output_cross: bfloat16 [1024, 1024], P('tp'), may hold values from -0.75 to 0.75
- bias_cross: float32 [1024], P('tp'), may hold values from -2 to 2
- gain_self: float32 [1024], replicated, may hold values from 0.2 to 3
- query_self: bfloat16 [1024, 1024], P(None, 'tp'), may hold values from -0.1875 to 0.1875
- key_self: bfloat16 [1024, 1024], P(None, 'tp'), may hold values from -0.1875 to 0.1875
- value_self: bfloat16 [1024, 1024], P(None, 'tp'), may hold values from -0.1875 to 0.1875
- output_self: bfloat16 [1024, 1024], P('tp'), may hold values from -0.75 to 0.75
- bias_self: float32 [1024], P('tp'), may hold values from -2 to 2
- gain_mlp: float32 [1024], replicated, may hold values from 0.2 to 3
- hidden_weight: bfloat16 [1024, 4096], P(None, 'tp'), may hold values from -0.1875 to 0.1875
- hidden_bias: float32 [4096], P('tp'), may hold values from -3 to 3
- output_weight: bfloat16 [4096, 1024], P('tp'), may hold values from -0.09375 to 0.09375
- output_bias: float32 [1024], P('tp'), may hold values from -2 to 2
- cotangent: bfloat16 [128, 128, 1024], P('grp', None, 'tp'), may hold values from -6 to 6
Outputs:
- block_out: float32 [128, 128, 1024], P('grp', None, 'tp')
- group_norms: float32 [128], replicated
- latents_grad: float32 [128, 128, 1024], P('grp', None, 'tp')
- embed_grad: float32 [128, 1024], P(None, 'tp')
- gain_cross_grad: float32 [1024], P('tp')
- query_cross_grad: float32 [1024, 1024], P(None, 'tp')
- key_cross_grad: float32 [1024, 1024], P(None, 'tp')
- value_cross_grad: float32 [1024, 1024], P(None, 'tp')
- output_cross_grad: float32 [1024, 1024], P('tp')
- bias_cross_grad: float32 [1024], P('tp')
- gain_self_grad: float32 [1024], P('tp')
- query_self_grad: float32 [1024, 1024], P(None, 'tp')
- key_self_grad: float32 [1024, 1024], P(None, 'tp')
- value_self_grad: float32 [1024, 1024], P(None, 'tp')
- output_self_grad: float32 [1024, 1024], P('tp')
- bias_self_grad: float32 [1024], P('tp')
- gain_mlp_grad: float32 [1024], P('tp')
- hidden_weight_grad: float32 [1024, 4096], P(None, 'tp')
- hidden_bias_grad: float32 [4096], P('tp')
- output_weight_grad: float32 [4096, 1024], P('tp')
- output_bias_grad: float32 [1024], P('tp')
Inputs may be any that keep to these rules, and one draw needn't show every extreme that they name: The neighbours of group g lie among the 16 blocks that start at block (g // 16) * 16 - 16 // 2, counted cyclically modulo 128; the first of them lies among the first 8 of these.
All inputs are finite; a program needn't handle non-finite values.
Results may differ from a plain program's by a relative error of at most 0.025.
Values may be sent and summed in bfloat16 or wider, within the bound.
No kernel may reach another device: no remote copies, remote signals or barrier semaphores. Data moves between devices by JAX's collectives and lax.ppermute only.
A program may use at most 192 MiB of HBM per device.

v0:
```python
import jax
import jax.numpy as jnp
from jax import lax
from jax.sharding import PartitionSpec as P

HD = 128
PB = 128
NB = 4


EPS = 1e-05
NEG = -1e30


def passed_along(x, axis, by):
    devices = lax.axis_size(axis)
    return lax.ppermute(x, axis, [(i, (i + by) % devices) for i in range(devices)])


def widen(value):
    return lax.all_gather(value, "tp", axis=1, tiled=True)


def narrow(value):
    return lax.psum_scatter(value, "tp", scatter_dimension=1, tiled=True)


def regroup(value):
    return lax.all_to_all(value, "grp", split_axis=1, concat_axis=0, tiled=True)


def restore(value):
    return lax.all_to_all(value, "grp", split_axis=0, concat_axis=1, tiled=True)


def cross_dot(left, right):
    return lax.dot_general(
        left, right, (((0,), (0,)), ((), ())), preferred_element_type=jnp.float32
    )


def back_dot(left, right):
    return lax.dot_general(
        left, right, (((1,), (1,)), ((), ())), preferred_element_type=jnp.float32
    )


def plain_dot(left, right):
    return jnp.dot(left, right, preferred_element_type=jnp.float32)


def slice_part(value, width):
    return lax.dynamic_slice_in_dim(value, lax.axis_index("tp") * width, width, 0)


def norm_forward(stream, gain):
    full = widen(stream)
    centre = jnp.mean(full, axis=1, keepdims=True)
    spread = jnp.mean(jnp.square(full - centre), axis=1, keepdims=True)
    scaled = lax.rsqrt(spread + EPS)
    centred = (full - centre) * scaled
    normed = (centred * gain).astype(jnp.bfloat16)
    width = stream.shape[1]
    local = lax.dynamic_slice_in_dim(centred, lax.axis_index("tp") * width, width, 1)
    return (normed, local, scaled)


def norm_backward(upstream, local, scaled, gain_part):
    full_width = local.shape[1] * lax.axis_size("tp")
    weighted = upstream * gain_part
    total_plain, total_mixed = lax.psum(
        (jnp.sum(weighted, axis=1), jnp.sum(weighted * local, axis=1)), "tp"
    )
    grad = scaled * (
        weighted - total_plain[:, None] / full_width - local * (total_mixed[:, None] / full_width)
    )
    return (grad, jnp.sum(upstream * local, axis=0))


def attend(queries, keys, values, live):
    scores = jnp.einsum(
        "gqhd,gkhd->ghqk", queries, keys, preferred_element_type=jnp.float32
    ) * HD ** (-0.5)
    scores = jnp.where(live[:, None, None, :], scores, NEG)
    highest = jnp.max(scores, axis=-1, keepdims=True)
    expo = jnp.exp(scores - highest)
    probs = expo / jnp.sum(expo, axis=-1, keepdims=True)
    weights = probs.astype(jnp.bfloat16)
    result = jnp.einsum(
        "ghqk,gkhd->gqhd", weights, values, preferred_element_type=jnp.float32
    ).astype(jnp.bfloat16)
    return (result, probs, weights)


def attend_back(grad_out, queries, keys, values, probs, weights):
    grad_weights = jnp.einsum(
        "gqhd,gkhd->ghqk", grad_out, values, preferred_element_type=jnp.float32
    )
    grad_values = jnp.einsum(
        "ghqk,gqhd->gkhd", weights, grad_out, preferred_element_type=jnp.float32
    )
    grad_scores = (
        probs * (grad_weights - jnp.sum(grad_weights * probs, axis=-1, keepdims=True))
    ).astype(jnp.bfloat16)
    grad_queries = jnp.einsum(
        "ghqk,gkhd->gqhd", grad_scores, keys, preferred_element_type=jnp.float32
    ) * HD ** (-0.5)
    grad_keys = jnp.einsum(
        "ghqk,gqhd->gkhd", grad_scores, queries, preferred_element_type=jnp.float32
    ) * HD ** (-0.5)
    return (grad_queries, grad_keys, grad_values)


def per_device(
    latents,
    skip_latents,
    points,
    neighbours,
    block_lengths,
    latent_embed,
    gain_cross,
    query_cross,
    key_cross,
    value_cross,
    output_cross,
    bias_cross,
    gain_self,
    query_self,
    key_self,
    value_self,
    output_self,
    bias_self,
    gain_mlp,
    hidden_weight,
    hidden_bias,
    output_weight,
    output_bias,
    cotangent,
):
    groups_here = neighbours.shape[0]
    lat_rows = latent_embed.shape[0]
    width_part = latent_embed.shape[1]
    model_width = query_cross.shape[0]
    heads_here = width_part // HD
    rows = groups_here * lat_rows
    grp_count = lax.axis_size("grp")
    grp_rank = lax.axis_index("grp")
    blocks_here = points.shape[0] // PB
    half_rows = points.shape[0] // 2
    all_blocks = blocks_here * grp_count
    first_block = grp_rank * blocks_here - blocks_here // 2
    local_index = (neighbours - first_block) % all_blocks
    ext_ids = (first_block + jnp.arange(blocks_here, dtype=jnp.int32)) % all_blocks
    ext_lengths = block_lengths[ext_ids]
    key_live = (
        jnp.arange(PB, dtype=jnp.int32)[None, None, :] < ext_lengths[local_index][:, :, None]
    ).reshape(groups_here, NB * PB)
    attn_shape = (groups_here, lat_rows, heads_here, HD)
    arrived = regroup(latents)
    stream_zero = (jnp.transpose(arrived, (1, 0, 2)).astype(jnp.float32) + latent_embed).reshape(
        rows, width_part
    )
    normed_cross, local_cross, scale_cross = norm_forward(stream_zero, gain_cross)
    cross_queries = plain_dot(normed_cross, query_cross).astype(jnp.bfloat16)
    own_keys = plain_dot(points, key_cross).astype(jnp.bfloat16)
    own_values = plain_dot(points, value_cross).astype(jnp.bfloat16)
    came_keys, came_values = passed_along((own_keys[half_rows:], own_values[half_rows:]), "grp", 1)
    ext_keys = jnp.concatenate([came_keys, own_keys[:half_rows]], axis=0)
    ext_values = jnp.concatenate([came_values, own_values[:half_rows]], axis=0)
    gathered_keys = ext_keys.reshape(blocks_here, PB, width_part)[local_index].reshape(
        groups_here, NB * PB, heads_here, HD
    )
    gathered_values = ext_values.reshape(blocks_here, PB, width_part)[local_index].reshape(
        groups_here, NB * PB, heads_here, HD
    )
    cross_heads = cross_queries.reshape(attn_shape)
    cross_out, cross_probs, cross_weights = attend(
        cross_heads, gathered_keys, gathered_values, key_live
    )
    cross_flat = cross_out.reshape(rows, width_part)
    stream_one = stream_zero + narrow(plain_dot(cross_flat, output_cross)) + bias_cross
    normed_self, local_self, scale_self = norm_forward(stream_one, gain_self)
    self_queries = plain_dot(normed_self, query_self).astype(jnp.bfloat16).reshape(attn_shape)
    self_keys = plain_dot(normed_self, key_self).astype(jnp.bfloat16).reshape(attn_shape)
    self_values = plain_dot(normed_self, value_self).astype(jnp.bfloat16).reshape(attn_shape)
    all_live = jnp.ones((groups_here, lat_rows), dtype=bool)
    self_out, self_probs, self_weights = attend(self_queries, self_keys, self_values, all_live)
    self_flat = self_out.reshape(rows, width_part)
    stream_two = stream_one + narrow(plain_dot(self_flat, output_self)) + bias_self
    normed_mlp, local_mlp, scale_mlp = norm_forward(stream_two, gain_mlp)
    before = plain_dot(normed_mlp, hidden_weight) + hidden_bias
    activation = jax.nn.gelu(before).astype(jnp.bfloat16)
    stream_three = stream_two + narrow(plain_dot(activation, output_weight)) + output_bias
    leaving = restore(
        jnp.transpose(stream_three.reshape(groups_here, lat_rows, width_part), (1, 0, 2))
    )
    block_out = leaving + skip_latents.astype(jnp.float32)
    square_sums = lax.psum(jnp.sum(jnp.square(block_out), axis=(0, 2)), ("grp", "tp"))
    group_norms = jnp.sqrt(square_sums / (lat_rows * model_width))
    grad_three = (
        jnp.transpose(regroup(cotangent), (1, 0, 2)).astype(jnp.float32).reshape(rows, width_part)
    )
    output_bias_grad = jnp.sum(grad_three, axis=0)
    branch_three = widen(grad_three).astype(jnp.bfloat16)
    output_weight_grad = cross_dot(activation, branch_three)
    grad_act = back_dot(branch_three, output_weight)
    gelu_value, gelu_pull = jax.vjp(jax.nn.gelu, before)
    grad_before = gelu_pull(grad_act)[0].astype(jnp.bfloat16)
    hidden_bias_grad = jnp.sum(grad_before.astype(jnp.float32), axis=0)
    hidden_weight_grad = cross_dot(normed_mlp, grad_before)
    grad_mlp_norm = narrow(back_dot(grad_before, hidden_weight))
    back_mlp, gain_mlp_grad = norm_backward(
        grad_mlp_norm, local_mlp, scale_mlp, slice_part(gain_mlp, width_part)
    )
    grad_two = grad_three + back_mlp
    bias_self_grad = jnp.sum(grad_two, axis=0)
    branch_two = widen(grad_two).astype(jnp.bfloat16)
    output_self_grad = cross_dot(self_flat, branch_two)
    grad_self_out = back_dot(branch_two, output_self).astype(jnp.bfloat16).reshape(attn_shape)
    grad_sq, grad_sk, grad_sv = attend_back(
        grad_self_out, self_queries, self_keys, self_values, self_probs, self_weights
    )
    grad_sq = grad_sq.astype(jnp.bfloat16).reshape(rows, width_part)
    grad_sk = grad_sk.astype(jnp.bfloat16).reshape(rows, width_part)
    grad_sv = grad_sv.astype(jnp.bfloat16).reshape(rows, width_part)
    query_self_grad = cross_dot(normed_self, grad_sq)
    key_self_grad = cross_dot(normed_self, grad_sk)
    value_self_grad = cross_dot(normed_self, grad_sv)
    grad_self_norm = narrow(
        back_dot(grad_sq, query_self) + back_dot(grad_sk, key_self) + back_dot(grad_sv, value_self)
    )
    back_self, gain_self_grad = norm_backward(
        grad_self_norm, local_self, scale_self, slice_part(gain_self, width_part)
    )
    grad_one = grad_two + back_self
    bias_cross_grad = jnp.sum(grad_one, axis=0)
    branch_one = widen(grad_one).astype(jnp.bfloat16)
    output_cross_grad = cross_dot(cross_flat, branch_one)
    grad_cross_out = back_dot(branch_one, output_cross).astype(jnp.bfloat16).reshape(attn_shape)
    grad_cq, grad_ck, grad_cv = attend_back(
        grad_cross_out, cross_heads, gathered_keys, gathered_values, cross_probs, cross_weights
    )
    grad_cq = grad_cq.astype(jnp.bfloat16).reshape(rows, width_part)
    flat_index = local_index.reshape(groups_here * NB)
    ext_grad_keys = (
        jnp.zeros((blocks_here, PB, width_part), jnp.float32)
        .at[flat_index]
        .add(grad_ck.reshape(groups_here * NB, PB, width_part))
        .reshape(blocks_here * PB, width_part)
    )
    ext_grad_values = (
        jnp.zeros((blocks_here, PB, width_part), jnp.float32)
        .at[flat_index]
        .add(grad_cv.reshape(groups_here * NB, PB, width_part))
        .reshape(blocks_here * PB, width_part)
    )
    back_keys, back_values = passed_along(
        (ext_grad_keys[:half_rows], ext_grad_values[:half_rows]), "grp", -1
    )
    own_grad_keys = jnp.concatenate([ext_grad_keys[half_rows:], back_keys], axis=0).astype(
        jnp.bfloat16
    )
    own_grad_values = jnp.concatenate([ext_grad_values[half_rows:], back_values], axis=0).astype(
        jnp.bfloat16
    )
    key_cross_grad = cross_dot(points, own_grad_keys)
    value_cross_grad = cross_dot(points, own_grad_values)
    query_cross_grad = cross_dot(normed_cross, grad_cq)
    grad_cross_norm = narrow(back_dot(grad_cq, query_cross))
    back_cross, gain_cross_grad = norm_backward(
        grad_cross_norm, local_cross, scale_cross, slice_part(gain_cross, width_part)
    )
    grad_zero = grad_one + back_cross
    grad_groups = grad_zero.reshape(groups_here, lat_rows, width_part)
    latents_grad = restore(jnp.transpose(grad_groups, (1, 0, 2)))
    embed_local = jnp.sum(grad_groups, axis=0)
    summed = lax.psum(
        (
            embed_local,
            gain_cross_grad,
            query_cross_grad,
            key_cross_grad,
            value_cross_grad,
            output_cross_grad,
            bias_cross_grad,
            gain_self_grad,
            query_self_grad,
            key_self_grad,
            value_self_grad,
            output_self_grad,
            bias_self_grad,
            gain_mlp_grad,
            hidden_weight_grad,
            hidden_bias_grad,
            output_weight_grad,
            output_bias_grad,
        ),
        "grp",
    )
    return (block_out, group_norms, latents_grad) + tuple(summed)


def solution(mesh):
    placed = (
        P("grp", None, "tp"),
        P("grp", None, "tp"),
        P("grp", None),
        P("grp", None),
        P(),
        P(None, "tp"),
        P(),
        P(None, "tp"),
        P(None, "tp"),
        P(None, "tp"),
        P("tp", None),
        P("tp"),
        P(),
        P(None, "tp"),
        P(None, "tp"),
        P(None, "tp"),
        P("tp", None),
        P("tp"),
        P(),
        P(None, "tp"),
        P("tp"),
        P("tp", None),
        P("tp"),
        P("grp", None, "tp"),
    )
    return jax.shard_map(
        per_device,
        mesh=mesh,
        in_specs=placed,
        out_specs=(
            P("grp", None, "tp"),
            P(),
            P("grp", None, "tp"),
            P(None, "tp"),
            P("tp"),
            P(None, "tp"),
            P(None, "tp"),
            P(None, "tp"),
            P("tp", None),
            P("tp"),
            P("tp"),
            P(None, "tp"),
            P(None, "tp"),
            P(None, "tp"),
            P("tp", None),
            P("tp"),
            P("tp"),
            P(None, "tp"),
            P("tp"),
            P("tp", None),
            P("tp"),
        ),
        check_vma=False,
    )
```

profile of v0, /device:TPU:0, one launch (start us, length us, event | category | flops | bytes accessed | tf_op | source)
XLA Modules:
  0.0 1688.0 jit_solution(14869327532852302948)
XLA Ops:
  9.2 32.8 %all_to_all.54 = bf16[16,128,256]{2,0,1:T(8,128)(2,1)S(1)} all-to-all(bf16[16,128,256]{2,0,1:T(8,128)(2,1)S(1)} %copy.156), channel_id=1, replica_groups=mesh['grp'=8,'tp'=4] {'grp'}, dimensions={1} | all-to-all | bytes 2097152 | tf_op jit(solution)/shard_map/all_to_all | solution.py:29
  56.6 19.3 %collective-permute-done = bf16[1024,256]{1,0:T(8,128)(2,1)S(1)} collective-permute-done((bf16[1024,256]{1,0:T(8,128)(2,1)S(1)}, bf16[1024,256]{1,0:T(8,128)(2,1)S(1)}, u32[]{:S(2)}, u32[]{:S(2)}) %collective-permute-start) | collective-permute-done | bytes 524320 | tf_op jit(solution)/shard_map/ppermute | solution.py:17
  98.7 11.2 copy.189
  128.6 8.9 fusion.114
  150.9 68.7 %reduce-scatter.7.cloned.1.call-done = f32[2048,256]{1,0:T(8,128)} async-done(((f32[2048,1024]{1,0:T(8,128)}), f32[2048,256]{1,0:T(8,128)}) %reduce-scatter.7.cloned.1.call-update) | async-done | bytes 2097168 | tf_op jit(solution)/shard_map/reduce_scatter | solution.py:25
  223.5 58.4 %all-gather.9.cloned.1.call-done = f32[2048,1024]{1,0:T(8,128)} async-done(((f32[2048,256]{1,0:T(8,128)}), f32[2048,1024]{1,0:T(8,128)}) %all-gather.9.cloned.1.call-update) | async-done | bytes 8388624 | tf_op jit(solution)/shard_map/all_gather | solution.py:21
  331.6 71.8 %reduce-scatter.9.cloned.1.call-done = f32[2048,256]{1,0:T(8,128)} async-done(((f32[2048,1024]{1,0:T(8,128)}), f32[2048,256]{1,0:T(8,128)}) %reduce-scatter.9.cloned.1.call-update) | async-done | bytes 2097168 | tf_op jit(solution)/shard_map/reduce_scatter | solution.py:25
  409.1 31.1 %all_to_all.55 = bf16[16,128,256]{2,0,1:T(8,128)(2,1)S(1)} all-to-all(bf16[16,128,256]{2,0,1:T(8,128)(2,1)S(1)} %copy.172), channel_id=1, replica_groups=mesh['grp'=8,'tp'=4] {'grp'}, dimensions={1} | all-to-all | bytes 2097152 | tf_op jit(solution)/shard_map/all_to_all | solution.py:29
  444.1 21.6 %all-gather.11.cloned.1.call-done = f32[2048,1024]{1,0:T(8,128)} async-done(((f32[2048,256]{1,0:T(8,128)}), f32[2048,1024]{1,0:T(8,128)}) %all-gather.11.cloned.1.call-update) | async-done | bytes 8388624 | tf_op jit(solution)/shard_map/all_gather | solution.py:21
  486.8 15.9 all-gather.13.cloned.1.call-done
  502.7 13.4 convert_reduce_fusion
  525.2 71.7 %reduce-scatter.13.cloned.1.call-done = f32[2048,256]{1,0:T(8,128)} async-done(((f32[2048,1024]{1,0:T(8,128)}), f32[2048,256]{1,0:T(8,128)}) %reduce-scatter.13.cloned.1.call-update) | async-done | bytes 2097168 | tf_op jit(solution)/shard_map/reduce_scatter | solution.py:25
  600.4 10.1 all-reduce.4
  617.1 36.0 %all-gather.15.cloned.1.call-done = bf16[2048,1024]{1,0:T(8,128)(2,1)} async-done(((bf16[2048,256]{1,0:T(8,128)(2,1)}), bf16[2048,1024]{1,0:T(8,128)(2,1)}) %all-gather.15.cloned.1.call-update) | async-done | bytes 4194320 | tf_op jit(solution)/shard_map/all_gather | solution.py:21
  687.6 71.8 %reduce-scatter.15.cloned.1.call-done = f32[2048,256]{1,0:T(8,128)} async-done(((f32[2048,1024]{1,0:T(8,128)}), f32[2048,256]{1,0:T(8,128)}) %reduce-scatter.15.cloned.1.call-update) | async-done | bytes 2097168 | tf_op jit(solution)/shard_map/reduce_scatter | solution.py:25
  762.3 10.1 all-reduce.3
  778.8 35.7 %all-gather.17.cloned.1.call-done = bf16[2048,1024]{1,0:T(8,128)(2,1)} async-done(((bf16[2048,256]{1,0:T(8,128)(2,1)}), bf16[2048,1024]{1,0:T(8,128)(2,1)}) %all-gather.17.cloned.1.call-update) | async-done | bytes 4194320 | tf_op jit(solution)/shard_map/all_gather | solution.py:21
  846.0 13.9 fusion.107
  860.9 11.5 fusion.33
  872.4 11.6 fusion.23
  898.8 13.2 copy.217
  911.9 11.5 reshape.366
  925.0 20.0 %scatter_fusion.1 = f32[16,128,256]{2,1,0:T(8,128)} fusion(f32[16,128,256]{2,1,0:T(8,128)} %broadcast.230.clone.1, s32[64]{0:T(128)S(1)} %fusion.99, f32[64,128,256]{2,1,0:T(8,128)} %reshape.366), kind=kCustom, calls=%fused_computation.5 | custom fusion | flops 2097152 | bytes 25166080 | tf_op jit(solution)/shard_map/scatter-add | solution.py:254
  959.4 13.3 copy.216
  972.7 11.6 reshape.365
  985.8 18.8 %scatter_fusion = f32[16,128,256]{2,1,0:T(8,128)} fusion(f32[16,128,256]{2,1,0:T(8,128)} %broadcast.230.clone, s32[64]{0:T(128)S(1)} %fusion.99, f32[64,128,256]{2,1,0:T(8,128)} %reshape.365), kind=kCustom, calls=%fused_computation.4 | custom fusion | flops 2097152 | bytes 25166080 | tf_op jit(solution)/shard_map/scatter-add | solution.py:248
  1016.8 7.7 collective-permute-done.2
  1029.7 10.1 all-reduce.2
  1060.9 97.9 %all-to-all-done.1 = f32[128,16,256]{2,1,0:T(8,128)} async-done(((f32[128,16,256]{2,1,0:T(8,128)}), f32[128,16,256]{2,1,0:T(8,128)}, u32[]{:S(2)}, u32[]{:S(2)}) %all-to-all-start.1) | async-done | bytes 2097184 | tf_op jit(solution)/shard_map/all_to_all | solution.py:33
  1167.0 112.6 %psum.175 = f32[128]{0:T(128)S(1)} all-reduce(f32[128]{0:T(128)S(1)} %get-tuple-element.142), channel_id=1, replica_groups=mesh['grp'=8,'tp'=4] {'grp','tp'}, use_global_device_ids=true, to_apply=%region_14.15 | all-reduce | flops 128 | bytes 1024 | tf_op jit(solution)/shard_map/psum | solution.py:198
  1280.1 38.9 %all-reduce = (f32[256]{0:T(256)}, f32[256]{0:T(256)}, f32[256]{0:T(256)}, f32[256]{0:T(256)}, f32[256]{0:T(256)}, /*index=5*/f32[1024]{0:T(1024)}, f32[256]{0:T(256)}) all-reduce(f32[256]{0:T(256)S(1)} %get-tuple-element.109, f32[256]{0:T(256)S(1)} %get-tuple-element.140, ...), channel_id=1, replica_groups=mesh['grp'=8,'tp'=4] {'grp'}, use_global_device_ids=true, to_apply=%region_35.36 | all-reduce | flops 2560 | bytes 20480 | tf_op jit(solution)/shard_map/psum | solution.py:277
  1322.2 338.6 %all-reduce.7.cloned.1.call-done = (f32[128,256]{1,0:T(8,128)}, f32[1024,256]{1,0:T(8,128)}, f32[1024,256]{0,1:T(8,128)}, f32[1024,256]{0,1:T(8,128)}, f32[256,1...) async-done(((f32[128,256]{1,0:T(8,128)}, ...) | async-done | bytes 16908304 | tf_op jit(solution)/shard_map/psum | solution.py:277
  (337 shorter events, 353.2 us)
Async XLA Ops:
  7.2 495.5 %copy-start = (bf16[1024,1024]{1,0:T(8,128)(2,1)S(1)}, bf16[1024,1024]{1,0:T(8,128)(2,1)}, u32[]{:S(2)}) copy-start(bf16[1024,1024]{1,0:T(8,128)(2,1)} %param.45) | copy-start | bytes 6291460
  7.2 102.7 %all-gather.7.cloned.1.call-start = ((), (), s32[]{:S(2)}) async-start(), calls=%async_computation.10 | async-start | bytes 10485760 | tf_op jit(solution)/shard_map/all_gather | solution.py:21
  44.5 175.1 %reduce-scatter.7.cloned.1.call-start = ((), (), s32[]{:S(2)}) async-start(), calls=%async_computation.11 | async-start | bytes 10485760 | tf_op jit(solution)/shard_map/reduce_scatter | solution.py:25
  49.2 38.5 %collective-permute-start.1 = (bf16[1024,256]{1,0:T(8,128)(2,1)}, bf16[1024,256]{1,0:T(8,128)(2,1)}, u32[]{:S(2)}, u32[]{:S(2)}) collective-permute-start(bf16[1024,256]{1,0:T(8,128)(2,1)} %get-tuple-element.152), channel_id=1, source_target_pairs={{0,4},{4,8},{8,12},{12,16},{16,20},{20,24},{24,28},{28,0},{1,5},{5... | collective-permute-start | bytes 1572872 | tf_op jit(solution)/shard_map/ppermute | solution.py:17
  52.8 23.1 %collective-permute-start = (bf16[1024,256]{1,0:T(8,128)(2,1)S(1)}, bf16[1024,256]{1,0:T(8,128)(2,1)S(1)}, u32[]{:S(2)}, u32[]{:S(2)}) collective-permute-start(bf16[1024,256]{1,0:T(8,128)(2,1)S(1)} %get-tuple-element.154), channel_id=1, source_target_pairs={{0,4},{4,8},{8,12},{12,16},{16,20},{20,24},{24,28},{28,0},{1,5},{5... | collective-permute-start | bytes 1572872 | tf_op jit(solution)/shard_map/ppermute | solution.py:17
  150.5 69.1 %copy-start.63 = (f32[256]{0:T(256)S(1)}, f32[256]{0:T(256)}, u32[]{:S(2)}) copy-start(f32[256]{0:T(256)} %param.35) | copy-start | bytes 3076
  150.5 131.4 %all-gather.9.cloned.1.call-start = ((), (), s32[]{:S(2)}) async-start(), calls=%async_computation.12 | async-start | bytes 10485760 | tf_op jit(solution)/shard_map/all_gather | solution.py:21
  223.4 180.0 %reduce-scatter.9.cloned.1.call-start = ((), (), s32[]{:S(2)}) async-start(), calls=%async_computation.13 | async-start | bytes 10485760 | tf_op jit(solution)/shard_map/reduce_scatter | solution.py:25
  331.5 71.9 %copy-start.64 = (f32[256]{0:T(256)S(1)}, f32[256]{0:T(256)}, u32[]{:S(2)}) copy-start(f32[256]{0:T(256)} %param.41) | copy-start | bytes 3076
  331.5 134.2 %all-gather.11.cloned.1.call-start = ((), (), s32[]{:S(2)}) async-start(), calls=%async_computation.14 | async-start | bytes 10485760 | tf_op jit(solution)/shard_map/all_gather | solution.py:21
  407.2 95.5 %all-gather.13.cloned.1.call-start = ((), (), s32[]{:S(2)}) async-start(), calls=%async_computation.16 | async-start | bytes 5242880 | tf_op jit(solution)/shard_map/all_gather | solution.py:21
  443.8 153.1 %reduce-scatter.13.cloned.1.call-start = ((), (), s32[]{:S(2)}) async-start(), calls=%async_computation.17 | async-start | bytes 10485760 | tf_op jit(solution)/shard_map/reduce_scatter | solution.py:25
  480.1 22.6 %copy-start.75 = (f32[1024]{0:T(1024)S(1)}, f32[1024]{0:T(1024)}, u32[]{:S(2)}) copy-start(f32[1024]{0:T(1024)} %param.44) | copy-start | bytes 12292
  502.7 15.4 copy-start.72
  525.0 128.0 %all-gather.15.cloned.1.call-start = ((), (), s32[]{:S(2)}) async-start(), calls=%async_computation.18 | async-start | bytes 5242880 | tf_op jit(solution)/shard_map/all_gather | solution.py:21
  616.9 142.5 %reduce-scatter.15.cloned.1.call-start = ((), (), s32[]{:S(2)}) async-start(), calls=%async_computation.19 | async-start | bytes 10485760 | tf_op jit(solution)/shard_map/reduce_scatter | solution.py:25
  687.5 127.0 %all-gather.17.cloned.1.call-start = ((), (), s32[]{:S(2)}) async-start(), calls=%async_computation.20 | async-start | bytes 5242880 | tf_op jit(solution)/shard_map/all_gather | solution.py:21
  775.8 38.6 %copy-start.47 = (bf16[256,1024]{1,0:T(8,128)(2,1)S(1)}, bf16[256,1024]{1,0:T(8,128)(2,1)}, u32[]{:S(2)}) copy-start(bf16[256,1024]{1,0:T(8,128)(2,1)} %param.34) | copy-start | bytes 1572868
  778.3 248.5 %reduce-scatter.17.cloned.1.call-start = ((), (), s32[]{:S(2)}) async-start(), calls=%async_computation.21 | async-start | bytes 10485760 | tf_op jit(solution)/shard_map/reduce_scatter | solution.py:25
  846.0 200.6 %reduce-scatter.11.cloned.1.call-start = ((), (), s32[]{:S(2)}) async-start(), calls=%async_computation.15 | async-start | bytes 10485760 | tf_op jit(solution)/shard_map/reduce_scatter | solution.py:25
  860.0 800.9 %all-reduce.7.cloned.1.call-start = ((), (), s32[]{:S(2)}) async-start(), calls=%async_computation.22 | async-start | bytes 33816576 | tf_op jit(solution)/shard_map/psum | solution.py:277
  872.4 11.6 copy-start.21
  872.4 11.6 copy-start.69
  947.6 65.9 %collective-permute-start.3 = (bf16[1024,256]{1,0:T(8,128)(2,1)}, bf16[1024,256]{1,0:T(8,128)(2,1)}, u32[]{:S(2)}, u32[]{:S(2)}) collective-permute-start(bf16[1024,256]{1,0:T(8,128)(2,1)} %bitcast.40), channel_id=1, source_target_pairs={{0,28},{4,0},{8,4},{12,8},{16,12},{20,16},{24,20},{28,24},{1,29},{... | collective-permute-start | bytes 1572872 | tf_op jit(solution)/shard_map/ppermute | solution.py:17
  1010.6 13.9 collective-permute-start.2
  1024.5 15.4 copy-start.56
  1052.3 106.5 %all-to-all-start.1 = ((f32[128,16,256]{2,1,0:T(8,128)}), f32[128,16,256]{2,1,0:T(8,128)}, u32[]{:S(2)}, u32[]{:S(2)}) async-start(f32[128,16,256]{2,1,0:T(8,128)} %bitcast.192), calls=%async_computation.4 | async-start | bytes 4194304 | tf_op jit(solution)/shard_map/all_to_all | solution.py:33
  1056.7 106.5 %copy-start.14 = (bf16[16,128,256]{2,0,1:T(8,128)(2,1)S(1)}, bf16[16,128,256]{2,0,1:T(8,128)(2,1)}, u32[]{:S(2)}) copy-start(bf16[16,128,256]{2,0,1:T(8,128)(2,1)} %copy-done.13) | copy-start | bytes 3145732
  1158.8 160.2 %all-to-all-start.3 = ((f32[128,16,256]{2,1,0:T(8,128)}), f32[128,16,256]{2,1,0:T(8,128)}, u32[]{:S(2)}, u32[]{:S(2)}) async-start(f32[128,16,256]{2,1,0:T(8,128)} %bitcast.191), calls=%async_computation.9 | async-start | bytes 4194304 | tf_op jit(solution)/shard_map/all_to_all | solution.py:33
  1163.5 116.7 %copy-start.59 = (f32[256]{0:T(256)S(1)}, f32[256]{0:T(256)}, u32[]{:S(2)}) copy-start(f32[256]{0:T(256)} %get-tuple-element.138) | copy-start | bytes 3076
  1163.5 116.7 %copy-start.60 = (f32[1024]{0:T(1024)S(1)}, f32[1024]{0:T(1024)}, u32[]{:S(2)}) copy-start(f32[1024]{0:T(1024)} %get-tuple-element.164) | copy-start | bytes 12292
  1163.5 116.6 %copy-start.61 = (f32[256]{0:T(256)S(1)}, f32[256]{0:T(256)}, u32[]{:S(2)}) copy-start(f32[256]{0:T(256)} %get-tuple-element.105) | copy-start | bytes 3076
  (65 other events, 244.6 us)
Sparse Core Ops, SparseCore 0:
  44.6 57.3 all-gather.6
  150.6 68.9 reduce-scatter.6
  223.6 58.2 all-gather.8
  331.6 71.7 reduce-scatter.8
  407.4 58.2 all-gather.10
  467.7 35.0 all-gather.12
  525.2 71.7 reduce-scatter.12
  617.0 36.0 all-gather.14
  687.6 71.7 reduce-scatter.14
  778.4 36.0 all-gather.16
  846.1 71.7 reduce-scatter.16
  920.5 71.6 reduce-scatter.10
  1046.7 614.1 all-reduce.6
where the time goes:
time: 1700 us; the launch traced here: 1690 us
  waiting for transfers between devices  915 us (54%)
  blocking collectives  246 us (14%)
  local copies, waits for them, and re-layouts  190 us (11%)
  matrix products  186 us (11%)
  other arithmetic  118 us (7%)
  starting transfers between devices  18.7 us (1%)
    psum x1, waiting for transfers between devices, per_device(): lax.psum((embed_local, gain_cross_grad, query_cross_grad, key_cross_grad,...  339 us
    reduce_scatter x6, waiting for transfers between devices, narrow(): return lax.psum_scatter(value, 'tp', scatter_dimension=1, tiled=True)  284 us
    all_gather x6, waiting for transfers between devices, widen(): return lax.all_gather(value, 'tp', axis=1, tiled=True)  168 us
    psum x1, blocking collectives, per_device(): lax.psum(jnp.sum(jnp.square(block_out), axis=(0, 2)), ('grp', 'tp'))  113 us
    all_to_all x2, waiting for transfers between devices, restore(): return lax.all_to_all(value, 'grp', split_axis=0, concat_axis=1, tiled=True)  97.9 us
    all_to_all x2, blocking collectives, regroup(): return lax.all_to_all(value, 'grp', split_axis=1, concat_axis=0, tiled=True)  63.9 us
    unnamed x169, local copies, waits for them, and re-layouts  53.3 us
    dot_general x10, matrix products, plain_dot(): return jnp.dot(left, right, preferred_element_type=jnp.float32)  46.2 us
  transfers between devices with their start and end apart: 19, of which 13 were waited for; matrix products, arithmetic and copies ran while one was open for 15% of the time, Pallas kernels for 0%

commit v1 on v0

v1 whole, which is shorter than its diff:
```python
import functools

import jax
import jax.numpy as jnp
from jax import lax
from jax.experimental import pallas as pl
from jax.experimental.pallas import tpu as pltpu
from jax.sharding import PartitionSpec as P

HD = 128
PB = 128
NB = 4
EPS = 1e-05
NEG = -1e30
SCALE = HD ** (-0.5)
BF = jnp.bfloat16
F32 = jnp.float32
VMEM_BYTES = 58 * 2**20

ANY = pl.BlockSpec(memory_space=pl.ANY)
VM = pl.BlockSpec(memory_space=pltpu.VMEM)
SM = pl.BlockSpec(memory_space=pltpu.SMEM)


def shape(dims, kind):
    return jax.ShapeDtypeStruct(dims, kind)


def params():
    return pltpu.CompilerParams(vmem_limit_bytes=VMEM_BYTES)


def nn(left, right):
    return lax.dot_general(left, right, (((1,), (0,)), ((), ())), preferred_element_type=F32)


def nt(left, right):
    return lax.dot_general(left, right, (((1,), (1,)), ((), ())), preferred_element_type=F32)


def tn(left, right):
    return lax.dot_general(left, right, (((0,), (0,)), ((), ())), preferred_element_type=F32)


def rows_at(i, n):
    return pl.ds(pl.multiple_of(i * n, n), n)


def normalise(x):
    d = x - jnp.mean(x, axis=1, keepdims=True)
    r = lax.rsqrt(jnp.mean(d * d, axis=1, keepdims=True) + EPS)
    return d * r, r


def norm_back(u, xhat, r, gain):
    w = u * gain
    a = jnp.mean(w, axis=1, keepdims=True)
    b = jnp.mean(w * xhat, axis=1, keepdims=True)
    return r * (w - a - xhat * b)


def colsum(x):
    return jnp.sum(x, axis=0, keepdims=True)


def begin(copies):
    for c in copies:
        c.start()


def finish(copies):
    for c in copies:
        c.wait()


def row_copies(pieces, buf, sem):
    n = pieces[0].shape[0]
    return [pltpu.make_async_copy(s, buf.at[pl.ds(p * n, n), :], sem) for p, s in enumerate(pieces)]


def col_copies(pieces, buf, sem):
    n = pieces[0].shape[1]
    return [pltpu.make_async_copy(s, buf.at[:, pl.ds(p * n, n)], sem) for p, s in enumerate(pieces)]


def cross_probs(q, ks, lens):
    lane = lax.broadcasted_iota(jnp.int32, (1, PB), 1)
    ss = [jnp.where(lane < n, nt(q, k) * SCALE, NEG) for k, n in zip(ks, lens)]
    top = functools.reduce(jnp.maximum, ss)
    top = jnp.max(top, axis=1, keepdims=True)
    es = [jnp.exp(s - top) for s in ss]
    total = jnp.sum(functools.reduce(jnp.add, es), axis=1, keepdims=True)
    inv = 1.0 / total
    return [e * inv for e in es]


def cross_forward_body(tp, idx, lens, x0, gain_c, gain_s, bias, *refs):
    came, refs = refs[:tp], refs[tp:]
    points, refs = refs[0], refs[1:]
    wkv, wq, wo = refs[:tp], refs[tp : 2 * tp], refs[2 * tp : 3 * tp]
    (kv, q, o, x1, nc, ns, ext_b, wkv_b, wq_b, wo_b, acc, sems) = refs[3 * tp :]
    rows, d = x0.shape
    w = d // tp
    half = ext_b.shape[0] // 2
    ext_c = row_copies(came, ext_b, sems.at[0]) + [
        pltpu.make_async_copy(points.at[pl.ds(0, half), :], ext_b.at[pl.ds(half, half), :], sems.at[0])
    ]
    wkv_c = col_copies(wkv, wkv_b, sems.at[1])
    wq_c = col_copies(wq, wq_b, sems.at[2])
    wo_c = row_copies(wo, wo_b, sems.at[3])
    for c in (wq_c, wkv_c, ext_c, wo_c):
        begin(c)

    @pl.loop(0, rows // PB)
    def _(i):
        s = rows_at(i, PB)
        xhat, _ = normalise(x0[s, :])
        nc[s, :] = (xhat * gain_c[...]).astype(BF)

    finish(wq_c)
    q[...] = nn(nc[...], wq_b[...]).astype(BF)
    finish(wkv_c)
    finish(ext_c)
    span = 512

    @pl.loop(0, ext_b.shape[0] // span)
    def _(i):
        s = rows_at(i, span)
        kv[s, :] = nn(ext_b[s, :], wkv_b[...]).astype(BF)

    @pl.loop(0, rows // PB)
    def _(g):
        s = rows_at(g, PB)
        at = [rows_at(idx[g * NB + n], PB) for n in range(NB)]
        ln = [lens[g * NB + n] for n in range(NB)]
        for p in range(tp):
            for h in range(w // HD):
                c = p * w + h * HD
                k0 = p * 2 * w + h * HD
                ks = [kv[a, k0 : k0 + HD] for a in at]
                vs = [kv[a, k0 + w : k0 + w + HD] for a in at]
                ps = cross_probs(q[s, c : c + HD], ks, ln)
                out = functools.reduce(jnp.add, [nn(pr.astype(BF), v) for pr, v in zip(ps, vs)])
                o[s, c : c + HD] = out.astype(BF)

    finish(wo_c)
    acc[...] = nn(o[...], wo_b[...])

    @pl.loop(0, rows // PB)
    def _(i):
        s = rows_at(i, PB)
        y = x0[s, :] + acc[s, :] + bias[...]
        x1[s, :] = y
        xhat, _ = normalise(y)
        ns[s, :] = (xhat * gain_s[...]).astype(BF)


def cross_forward(idx, lens, x0, gain_c, gain_s, bias, came, points, wkv, wq, wo):
    tp = len(wq)
    rows, d = x0.shape
    w = d // tp
    ext = points.shape[0]
    return pl.pallas_call(
        functools.partial(cross_forward_body, tp),
        out_shape=(
            shape((ext, 2 * d), BF),
            shape((rows, d), BF),
            shape((rows, d), BF),
            shape((rows, d), F32),
            shape((rows, d), BF),
            shape((rows, d), BF),
        ),
        in_specs=[SM, SM] + [VM] * 4 + [ANY] * (4 * tp + 1),
        out_specs=[VM] * 6,
        scratch_shapes=[
            pltpu.VMEM((ext, d), BF),
            pltpu.VMEM((d, 2 * d), BF),
            pltpu.VMEM((d, d), BF),
            pltpu.VMEM((d, d), BF),
            pltpu.VMEM((rows, d), F32),
            pltpu.SemaphoreType.DMA((4,)),
        ],
        compiler_params=params(),
        name="cross_forward",
    )(idx, lens, x0, gain_c, gain_s, bias, *came, points, *wkv, *wq, *wo)


def self_probs(q, k):
    s = nt(q, k) * SCALE
    e = jnp.exp(s - jnp.max(s, axis=1, keepdims=True))
    return e * (1.0 / jnp.sum(e, axis=1, keepdims=True))


def self_forward_body(tp, ns, x1, gain_m, bias, *refs):
    wqkv, wo = refs[:tp], refs[tp : 2 * tp]
    qkv, o, x2, nm, wqkv_b, wo_b, acc, sems = refs[2 * tp :]
    rows, d = x1.shape
    w = d // tp
    wqkv_c = col_copies(wqkv, wqkv_b, sems.at[0])
    wo_c = row_copies(wo, wo_b, sems.at[1])
    begin(wqkv_c)
    begin(wo_c)
    finish(wqkv_c)
    qkv[...] = nn(ns[...], wqkv_b[...]).astype(BF)

    @pl.loop(0, rows // PB)
    def _(g):
        s = rows_at(g, PB)
        for p in range(tp):
            for h in range(w // HD):
                c = p * w + h * HD
                k0 = p * 3 * w + h * HD
                pr = self_probs(qkv[s, k0 : k0 + HD], qkv[s, k0 + w : k0 + w + HD])
                v = qkv[s, k0 + 2 * w : k0 + 2 * w + HD]
                o[s, c : c + HD] = nn(pr.astype(BF), v).astype(BF)

    finish(wo_c)
    acc[...] = nn(o[...], wo_b[...])

    @pl.loop(0, rows // PB)
    def _(i):
        s = rows_at(i, PB)
        y = x1[s, :] + acc[s, :] + bias[...]
        x2[s, :] = y
        xhat, _ = normalise(y)
        nm[s, :] = (xhat * gain_m[...]).astype(BF)


def self_forward(ns, x1, gain_m, bias, wqkv, wo):
    tp = len(wo)
    rows, d = x1.shape
    return pl.pallas_call(
        functools.partial(self_forward_body, tp),
        out_shape=(
            shape((rows, 3 * d), BF),
            shape((rows, d), BF),
            shape((rows, d), F32),
            shape((rows, d), BF),
        ),
        in_specs=[VM] * 4 + [ANY] * (2 * tp),
        out_specs=[VM] * 4,
        scratch_shapes=[
            pltpu.VMEM((d, 3 * d), BF),
            pltpu.VMEM((d, d), BF),
            pltpu.VMEM((rows, d), F32),
            pltpu.SemaphoreType.DMA((2,)),
        ],
        compiler_params=params(),
        name="self_forward",
    )(ns, x1, gain_m, bias, *wqkv, *wo)


ROOT = 0.7978845608028654
CUBE = 0.044715


def feed_body(nm, cot, hb, wh0, wh1, wo0, wo1, act, gb, out, gnm, hbg):
    rows, d = nm.shape
    ff = wh0.shape[1]
    span = min(512, ff)
    for p, (wh, wo) in enumerate(((wh0, wo0), (wh1, wo1))):
        for j in range(ff // span):
            s = slice(j * span, (j + 1) * span)
            x = nn(nm[...], wh[:, s]) + hb[p : p + 1, s]
            ga = nt(cot[...], wo[s, :])
            sq = x * x
            t = jnp.tanh(ROOT * x * (1.0 + CUBE * sq))
            half = 0.5 * (1.0 + t)
            act[p, :, s] = (x * half).astype(BF)
            slope = half + 0.5 * x * (1.0 - t * t) * (ROOT + (3.0 * ROOT * CUBE) * sq)
            g = (ga * slope).astype(BF)
            gb[p, :, s] = g
            hbg[p : p + 1, s] = colsum(g.astype(F32))
    gnm[...] = (nt(gb[0], wh0[...]) + nt(gb[1], wh1[...])).astype(gnm.dtype)
    out[...] = (nn(act[0], wo0[...]) + nn(act[1], wo1[...])).astype(out.dtype)


def feed(nm, cot, hb, wh, wo, kind):
    rows, d = nm.shape
    ff = wh[0].shape[1]
    return pl.pallas_call(
        feed_body,
        out_shape=(
            shape((2, rows, ff), BF),
            shape((2, rows, ff), BF),
            shape((rows, d), kind),
            shape((rows, d), kind),
            shape((2, ff), F32),
        ),
        in_specs=[VM] * 7,
        out_specs=[VM] * 5,
        compiler_params=params(),
        name="feed",
    )(nm, cot, hb, *wh, *wo)


def feed_weights_body(sets, p, *refs):
    acts, cots, nms, gbs = (refs[k * sets : (k + 1) * sets] for k in range(4))
    rest = refs[4 * sets :]
    (came_o, came_h, do, dh) = rest if len(rest) == 4 else (None, None) + tuple(rest)
    tile = 256
    ff, d = do.shape

    @pl.loop(0, ff // tile)
    def _(i):
        s = rows_at(i, tile)
        y = functools.reduce(jnp.add, [tn(a[0, :, s], c[...]) for a, c in zip(acts, cots)])
        if came_o is not None:
            y = y + came_o[s, :].astype(F32)
        do[s, :] = y.astype(BF)

    @pl.loop(0, d // tile)
    def _(i):
        s = rows_at(i, tile)
        y = functools.reduce(jnp.add, [tn(a[:, s], g[0]) for a, g in zip(nms, gbs)])
        if came_h is not None:
            y = y + came_h[s, :].astype(F32)
        dh[s, :] = y.astype(BF)


def feed_weights(p, acts, cots, nms, gbs, came):
    sets = len(acts)
    _, rows, ff = acts[0].shape
    d = cots[0].shape[1]
    one = pl.BlockSpec((1, rows, ff), lambda i: (p, 0, 0))
    whole = pl.BlockSpec((rows, d), lambda i: (0, 0))
    fo = pl.BlockSpec((ff, d), lambda i: (0, 0))
    fh = pl.BlockSpec((d, ff), lambda i: (0, 0))
    return pl.pallas_call(
        functools.partial(feed_weights_body, sets, p),
        grid=(1,),
        out_shape=(shape((ff, d), BF), shape((d, ff), BF)),
        in_specs=[one] * sets + [whole] * sets + [whole] * sets + [one] * sets + ([fo, fh] if came else []),
        out_specs=[fo, fh],
        compiler_params=params(),
        name="feed_weights",
    )(*acts, *cots, *nms, *gbs, *came)


def self_backward_body(tp, others, cot, gnm, x2, x1, gain_m, gain_s, qkv, *refs):
    gots, refs = refs[:others], refs[others:]
    wo, wqkv, refs = refs[:tp], refs[tp : 2 * tp], refs[2 * tp :]
    b2, dqkv, g1, b1, vec, wo_b, wqkv_b, g2, gso, gns, sems = refs
    rows, d = cot.shape
    w = d // tp
    wo_c = row_copies(wo, wo_b, sems.at[0])
    wqkv_c = col_copies(wqkv, wqkv_b, sems.at[1])
    begin(wo_c)
    begin(wqkv_c)
    vec[...] = jnp.zeros_like(vec)

    @pl.loop(0, rows // PB)
    def _(i):
        s = rows_at(i, PB)
        u = functools.reduce(jnp.add, [r[s, :].astype(F32) for r in gots], gnm[s, :])
        xhat, r = normalise(x2[s, :])
        g3 = cot[s, :].astype(F32)
        y = g3 + norm_back(u, xhat, r, gain_m[...])
        g2[s, :] = y
        b2[s, :] = y.astype(BF)
        vec[0:1, :] += colsum(g3)
        vec[1:2, :] += colsum(u * xhat)
        vec[2:3, :] += colsum(y)

    finish(wo_c)
    gso[...] = nt(b2[...], wo_b[...]).astype(BF)

    @pl.loop(0, rows // PB)
    def _(g):
        s = rows_at(g, PB)
        for p in range(tp):
            for h in range(w // HD):
                c = p * w + h * HD
                k0 = p * 3 * w + h * HD
                k1, k2 = k0 + w, k0 + 2 * w
                q, k, v = qkv[s, k0 : k0 + HD], qkv[s, k1 : k1 + HD], qkv[s, k2 : k2 + HD]
                pr = self_probs(q, k)
                do = gso[s, c : c + HD]
                dp = nt(do, v)
                ds = (pr * (dp - jnp.sum(dp * pr, axis=1, keepdims=True))).astype(BF)
                dqkv[s, k0 : k0 + HD] = (nn(ds, k) * SCALE).astype(BF)
                dqkv[s, k1 : k1 + HD] = (tn(ds, q) * SCALE).astype(BF)
                dqkv[s, k2 : k2 + HD] = tn(pr.astype(BF), do).astype(BF)

    finish(wqkv_c)
    gns[...] = nt(dqkv[...], wqkv_b[...])

    @pl.loop(0, rows // PB)
    def _(i):
        s = rows_at(i, PB)
        u = gns[s, :]
        xhat, r = normalise(x1[s, :])
        y = g2[s, :] + norm_back(u, xhat, r, gain_s[...])
        g1[s, :] = y
        b1[s, :] = y.astype(BF)
        vec[3:4, :] += colsum(u * xhat)
        vec[4:5, :] += colsum(y)


def self_backward(cot, gnm, gots, x2, x1, gain_m, gain_s, qkv, wo, wqkv):
    tp = len(wo)
    rows, d = cot.shape
    return pl.pallas_call(
        functools.partial(self_backward_body, tp, len(gots)),
        out_shape=(
            shape((rows, d), BF),
            shape((rows, 3 * d), BF),
            shape((rows, d), F32),
            shape((rows, d), BF),
            shape((8, d), F32),
        ),
        in_specs=[VM] * (7 + len(gots)) + [ANY] * (2 * tp),
        out_specs=[VM] * 5,
        scratch_shapes=[
            pltpu.VMEM((d, d), BF),
            pltpu.VMEM((d, 3 * d), BF),
            pltpu.VMEM((rows, d), F32),
            pltpu.VMEM((rows, d), BF),
            pltpu.VMEM((rows, d), F32),
            pltpu.SemaphoreType.DMA((2,)),
        ],
        compiler_params=params(),
        name="self_backward",
    )(cot, gnm, x2, x1, gain_m, gain_s, qkv, *gots, *wo, *wqkv)


def cross_backward_body(tp, idx, lens, b1, g1, x0, gain_c, q, kv, *refs):
    wo, wq, refs = refs[:tp], refs[tp : 2 * tp], refs[2 * tp :]
    dq, dkv, g0, emb, vec, wo_b, wq_b, gco, gnc, dacc, sems = refs
    rows, d = b1.shape
    w = d // tp
    wo_c = row_copies(wo, wo_b, sems.at[0])
    wq_c = col_copies(wq, wq_b, sems.at[1])
    begin(wo_c)
    begin(wq_c)
    vec[...] = jnp.zeros_like(vec)
    emb[...] = jnp.zeros_like(emb)
    ext = kv.shape[0]

    @pl.loop(0, ext // PB)
    def _(i):
        dacc[rows_at(i, PB), :] = jnp.zeros((PB, dacc.shape[1]), F32)

    finish(wo_c)
    gco[...] = nt(b1[...], wo_b[...]).astype(BF)

    @pl.loop(0, rows // PB)
    def _(g):
        s = rows_at(g, PB)
        at = [rows_at(idx[g * NB + n], PB) for n in range(NB)]
        ln = [lens[g * NB + n] for n in range(NB)]
        for p in range(tp):
            for h in range(w // HD):
                c = p * w + h * HD
                k0 = p * 2 * w + h * HD
                v0 = k0 + w
                ks = [kv[a, k0 : k0 + HD] for a in at]
                vs = [kv[a, v0 : v0 + HD] for a in at]
                qh = q[s, c : c + HD]
                do = gco[s, c : c + HD]
                ps = cross_probs(qh, ks, ln)
                dps = [nt(do, v) for v in vs]
                mixed = functools.reduce(jnp.add, [a * b for a, b in zip(ps, dps)])
                mixed = jnp.sum(mixed, axis=1, keepdims=True)
                dss = [(a * (b - mixed)).astype(BF) for a, b in zip(ps, dps)]
                dqh = functools.reduce(jnp.add, [nn(ds, k) for ds, k in zip(dss, ks)])
                dq[s, c : c + HD] = (dqh * SCALE).astype(BF)
                for a, ds, pr in zip(at, dss, ps):
                    dacc[a, k0 : k0 + HD] += tn(ds, qh) * SCALE
                    dacc[a, v0 : v0 + HD] += tn(pr.astype(BF), do)

    @pl.loop(0, ext // PB)
    def _(i):
        s = rows_at(i, PB)
        dkv[s, :] = dacc[s, :].astype(BF)

    finish(wq_c)
    gnc[...] = nt(dq[...], wq_b[...])

    @pl.loop(0, rows // PB)
    def _(i):
        s = rows_at(i, PB)
        u = gnc[s, :]
        xhat, r = normalise(x0[s, :])
        y = g1[s, :] + norm_back(u, xhat, r, gain_c[...])
        g0[s, :] = y.astype(BF)
        emb[...] += y
        vec[0:1, :] += colsum(u * xhat)


def cross_backward(idx, lens, b1, g1, x0, gain_c, q, kv, wo, wq):
    tp = len(wo)
    rows, d = b1.shape
    ext = kv.shape[0]
    return pl.pallas_call(
        functools.partial(cross_backward_body, tp),
        out_shape=(
            shape((rows, d), BF),
            shape((ext, 2 * d), BF),
            shape((rows, d), BF),
            shape((PB, d), F32),
            shape((8, d), F32),
        ),
        in_specs=[SM, SM] + [VM] * 6 + [ANY] * (2 * tp),
        out_specs=[VM] * 5,
        scratch_shapes=[
            pltpu.VMEM((d, d), BF),
            pltpu.VMEM((d, d), BF),
            pltpu.VMEM((rows, d), BF),
            pltpu.VMEM((rows, d), F32),
            pltpu.VMEM((ext, 2 * d), F32),
            pltpu.SemaphoreType.DMA((2,)),
        ],
        compiler_params=params(),
        name="cross_backward",
    )(idx, lens, b1, g1, x0, gain_c, q, kv, *wo, *wq)


def tn_into(out, at, left, right, extra):
    tile = 256
    lead, lo, n = at

    @pl.loop(0, left.shape[1] // tile)
    def _(i):
        s = rows_at(i, tile)
        y = tn(left[:, s], right())
        if extra is not None:
            y = y + extra[lead, s, lo : lo + n].astype(F32)
        out[lead, s, lo : lo + n] = y.astype(BF)


def self_weights_body(tp, odd, ns, dqkv, o, b2, *refs):
    extra, out = (None, refs[0]) if odd else (refs[0], refs[1])
    w = ns.shape[1] // tp
    for j in range(tp // 2):
        p = 2 * j + (1 if odd else 0)
        tn_into(out, (j, 0, 3 * w), ns, lambda: dqkv[:, p * 3 * w : (p + 1) * 3 * w], extra)
        tn_into(out, (j, 3 * w, w), b2, lambda: o[:, p * w : (p + 1) * w], extra)


def self_weights(tp, odd, ns, dqkv, o, b2, came):
    d = ns.shape[1]
    ins = [ns, dqkv, o, b2] + list(came)
    return pl.pallas_call(
        functools.partial(self_weights_body, tp, odd),
        out_shape=shape((tp // 2, d, 4 * d // tp), BF),
        in_specs=[VM] * len(ins),
        out_specs=VM,
        compiler_params=params(),
        name="self_weights",
    )(*ins)


def cross_weights_body(tp, odd, nc, dq, o, b1, dkv, points, *refs):
    came, refs = refs[:tp], refs[tp:]
    extra, refs = (None, refs) if odd else (refs[0], refs[1:])
    out, ext_b, sem = refs
    half = ext_b.shape[0] // 2
    copies = row_copies(came, ext_b, sem) + [
        pltpu.make_async_copy(points.at[pl.ds(0, half), :], ext_b.at[pl.ds(half, half), :], sem)
    ]
    begin(copies)
    w = nc.shape[1] // tp
    for j in range(tp // 2):
        p = 2 * j + (1 if odd else 0)
        tn_into(out, (j, 0, w), nc, lambda: dq[:, p * w : (p + 1) * w], extra)
        tn_into(out, (j, 3 * w, w), b1, lambda: o[:, p * w : (p + 1) * w], extra)
    finish(copies)
    for j in range(tp // 2):
        p = 2 * j + (1 if odd else 0)
        tn_into(out, (j, w, 2 * w), ext_b, lambda: dkv[:, p * 2 * w : (p + 1) * 2 * w], extra)


def cross_weights(tp, odd, nc, dq, o, b1, dkv, points, came_points, came):
    d = nc.shape[1]
    ins = [nc, dq, o, b1, dkv, points] + list(came_points) + list(came)
    return pl.pallas_call(
        functools.partial(cross_weights_body, tp, odd),
        out_shape=shape((tp // 2, d, 4 * d // tp), BF),
        in_specs=[VM] * 5 + [ANY] * (1 + tp) + [VM] * len(came),
        out_specs=VM,
        scratch_shapes=[pltpu.VMEM((dkv.shape[0], d), BF), pltpu.SemaphoreType.DMA],
        compiler_params=params(),
        name="cross_weights",
    )(*ins)


def flip(x, axis, bit):
    n = lax.axis_size(axis)
    return lax.ppermute(x, axis, [(i, i ^ (1 << bit)) for i in range(n)])


def bits_of(axis):
    return (lax.axis_size(axis) - 1).bit_length()


def bit_at(axis, bit):
    return (lax.axis_index(axis) >> bit) & 1


def gather_pieces(own):
    have = {0: own}
    for bit in reversed(range(bits_of("tp"))):
        for p in list(have):
            have[p | (1 << bit)] = flip(have[p], "tp", bit)
    return [have[p] for p in range(len(have))]


def in_order(pieces):
    x = jnp.stack(pieces)
    for bit in range(bits_of("tp")):
        y = x.reshape((-1, 2, 1 << bit) + x.shape[1:])
        x = jnp.where(bit_at("tp", bit) == 1, y[:, ::-1], y).reshape(x.shape)
    return x


def add(*xs):
    return functools.reduce(jnp.add, [x.astype(F32) for x in xs]).astype(BF)


def halves(x, axis, bit):
    n = x.shape[0] // 2
    mine = bit_at(axis, bit)
    return (
        lax.dynamic_slice_in_dim(x, mine * n, n, 0),
        lax.dynamic_slice_in_dim(x, (1 - mine) * n, n, 0),
    )


def sum_half(x, axis, bit):
    keep, send = halves(x, axis, bit)
    return keep, flip(send, axis, bit)


def both(x, axis, bit):
    other = flip(x, axis, bit)
    low = bit_at(axis, bit) == 0
    return jnp.where(low, jnp.concatenate([x, other]), jnp.concatenate([other, x]))


def sum_over_grp(x):
    order = list(range(bits_of("grp")))
    for bit in order:
        x = add(*sum_half(x, "grp", bit))
    for bit in reversed(order):
        x = both(x, "grp", bit)
    return x.astype(F32)


def sum_pieces(even):
    have = {2 * j: even[j] for j in range(even.shape[0])}
    for bit in reversed(range(1, bits_of("tp"))):
        send = [p for p in have if p >> bit & 1]
        for p in send:
            got = flip(have[p], "tp", bit)
            have[p ^ (1 << bit)] = add(have[p ^ (1 << bit)], got)
        have = {p: v for p, v in have.items() if not p >> bit & 1}
    return have[0]


def sum_small(x):
    for bit in reversed(range(bits_of("tp"))):
        keep, got = sum_half(x, "tp", bit)
        x = keep + got
    x = x[0]
    for bit in range(bits_of("grp")):
        x = x + flip(x, "grp", bit)
    return x


def to_groups(x, per):
    lat, groups, w = x.shape
    n = groups // per
    tp = lax.axis_size("tp")
    y = jnp.transpose(x.reshape(lat, n, per, w), (1, 2, 0, 3))
    y = lax.all_to_all(y, ("grp", "tp"), split_axis=0, concat_axis=0, tiled=True)
    y = jnp.transpose(y.reshape(n // tp, tp, per, lat, w), (2, 0, 3, 1, 4))
    return y.reshape(per * lat * (n // tp), tp * w)


def from_groups(x, per):
    tp = lax.axis_size("tp")
    n = lax.axis_size("grp") * tp
    rows, d = x.shape
    lat, w = rows // per // (n // tp), d // tp
    y = jnp.transpose(x.reshape(per, n // tp, lat, tp, w), (1, 3, 0, 2, 4)).reshape(n, per, lat, w)
    y = lax.all_to_all(y, ("grp", "tp"), split_axis=0, concat_axis=0, tiled=True)
    return jnp.transpose(y, (2, 0, 1, 3)).reshape(lat, n * per, w)


def per_device(
    latents,
    skip_latents,
    points,
    neighbours,
    block_lengths,
    latent_embed,
    gain_cross,
    query_cross,
    key_cross,
    value_cross,
    output_cross,
    bias_cross,
    gain_self,
    query_self,
    key_self,
    value_self,
    output_self,
    bias_self,
    gain_mlp,
    hidden_weight,
    hidden_bias,
    output_weight,
    output_bias,
    cotangent,
):
    tp, grp = lax.axis_size("tp"), lax.axis_size("grp")
    t, i = lax.axis_index("tp"), lax.axis_index("grp")
    d = query_cross.shape[0]
    w = latent_embed.shape[1]
    lat_rows = latent_embed.shape[0]
    ff = hidden_weight.shape[1]
    groups_here = neighbours.shape[0]
    groups = groups_here * grp
    per = groups_here // tp
    blocks_here = points.shape[0] // PB
    all_blocks = blocks_here * grp
    half_rows = points.shape[0] // 2

    small = jnp.concatenate(
        [
            latent_embed,
            bias_cross[None],
            bias_self[None],
            output_bias[None],
            hidden_bias.reshape(ff // w, w),
        ]
    )
    small_pieces = gather_pieces(small)
    small_all = in_order(small_pieces)
    by_rows = jnp.transpose(small_all, (1, 0, 2)).reshape(small.shape[0], d)
    embed = by_rows[:lat_rows]
    bias_c, bias_s, bias_o = (by_rows[lat_rows + k : lat_rows + k + 1] for k in range(3))
    hid_bias = jnp.stack([piece[lat_rows + 3 :].reshape(ff) for piece in small_pieces[:2]])

    wkv = gather_pieces(jnp.concatenate([key_cross, value_cross], axis=1))
    wq = gather_pieces(query_cross)
    woc = gather_pieces(output_cross)
    wqkv = gather_pieces(jnp.concatenate([query_self, key_self, value_self], axis=1))
    wos = gather_pieces(output_self)
    whid = [hidden_weight, flip(hidden_weight, "tp", 0)]
    wout = [output_weight, flip(output_weight, "tp", 0)]

    share = half_rows // tp
    sent = lax.dynamic_slice_in_dim(points, half_rows + t * share, share, 0)
    first = lax.ppermute(sent, "grp", [(k, (k + 1) % grp) for k in range(grp)])
    came_points = gather_pieces(first)
    near = lax.dynamic_slice_in_dim(neighbours, t * per, per, 0).reshape(per * NB)
    block = (near - (i * blocks_here - blocks_here // 2)) % all_blocks
    share_blocks = share // PB
    moved = ((block // share_blocks) ^ t) * share_blocks + block % share_blocks
    idx = jnp.where(block < blocks_here // 2, moved, block).astype(jnp.int32)
    lens = block_lengths[near]

    gain_c, gain_s, gain_m = gain_cross[None], gain_self[None], gain_mlp[None]
    rows = per * lat_rows
    x0 = (
        to_groups(latents, per).astype(F32).reshape(per, lat_rows, d) + embed[None]
    ).reshape(rows, d)
    kv, q, oc, x1, nc, ns = cross_forward(
        idx, lens, x0, gain_c, gain_s, bias_c, came_points, points, wkv, wq, woc
    )
    qkv, os, x2, nm = self_forward(ns, x1, gain_m, bias_s, wqkv, wos)
    cot = to_groups(cotangent, per)

    steps = list(range(2, tp, 2))

    def swap(x, k):
        return lax.ppermute(x, "tp", [(j, j ^ k) for j in range(tp)])

    other_cot = [swap(cot, k) for k in steps]
    other_nm = [swap(nm, k) for k in steps]
    acts, gbs, hbgs = [], [], []
    act, gb, out, gnm, hbg = feed(nm, cot, hid_bias, whid, wout, F32)
    acts.append(act)
    gbs.append(gb)
    hbgs.append(hbg)
    back_out, back_gnm = [], []
    for k, n_k, c_k in zip(steps, other_nm, other_cot):
        act, gb, o_k, g_k, hbg = feed(n_k, c_k, hid_bias, whid, wout, BF)
        acts.append(act)
        gbs.append(gb)
        hbgs.append(hbg)
        back_gnm.append(swap(g_k, k))
        back_out.append(swap(o_k, k))
    nms, cots = [nm] + other_nm, [cot] + other_cot
    sent_o, sent_h = feed_weights(1, acts, cots, nms, gbs, [])
    got = [flip(sent_o, "tp", 0), flip(sent_h, "tp", 0)]
    own_o, own_h = feed_weights(0, acts, cots, nms, gbs, got)
    output_weight_grad = sum_over_grp(own_o)
    hidden_weight_grad = sum_over_grp(own_h)

    x3 = functools.reduce(jnp.add, [r.astype(F32) for r in back_out], x2 + out + bias_o)
    block_out = from_groups(x3.astype(BF), per).astype(F32) + skip_latents.astype(F32)
    squares = jnp.sum(jnp.square(block_out), axis=(0, 2))

    b2, dqkv, g1, b1, vec_s = self_backward(
        cot, gnm, back_gnm, x2, x1, gain_m, gain_s, qkv, wos, wqkv
    )
    odd = self_weights(tp, True, ns, dqkv, os, b2, [])
    even = self_weights(tp, False, ns, dqkv, os, b2, [flip(odd, "tp", 0)])
    self_grads = sum_over_grp(sum_pieces(even))

    dq, dkv, g0, emb, vec_c = cross_backward(idx, lens, b1, g1, x0, gain_c, q, kv, woc, wq)
    odd = cross_weights(tp, True, nc, dq, oc, b1, dkv, points, came_points, [])
    even = cross_weights(
        tp, False, nc, dq, oc, b1, dkv, points, came_points, [flip(odd, "tp", 0)]
    )
    cross_grads = sum_over_grp(sum_pieces(even))
    latents_grad = from_groups(g0, per).astype(F32)

    by_share = jnp.transpose(
        jnp.concatenate([emb, vec_s[:5], vec_c[:1]]).reshape(lat_rows + 6, tp, w), (1, 0, 2)
    )
    hb_all = functools.reduce(jnp.add, hbgs).reshape(2, ff // w, w)
    place = lax.broadcasted_iota(jnp.int32, (tp, 1, 1), 0)
    hb_share = jnp.where(place == t, hb_all[0][None], 0.0) + jnp.where(
        place == (t ^ 1), hb_all[1][None], 0.0
    )
    norm_rows = -(-groups // w)
    sq_rows = jnp.pad(squares, (0, norm_rows * w - groups)).reshape(1, norm_rows, w)
    packed = jnp.concatenate(
        [by_share, hb_share, jnp.broadcast_to(sq_rows, (tp, norm_rows, w))], axis=1
    )
    pad = -packed.shape[1] % 8
    packed = jnp.pad(packed, ((0, 0), (0, pad), (0, 0)))
    total = sum_small(packed)
    embed_grad = total[:lat_rows]
    (
        output_bias_grad,
        gain_mlp_grad,
        bias_self_grad,
        gain_self_grad,
        bias_cross_grad,
        gain_cross_grad,
    ) = (total[lat_rows + k] for k in range(6))
    at = lat_rows + 6
    hidden_bias_grad = total[at : at + ff // w].reshape(ff)
    at += ff // w
    square_sums = total[at : at + norm_rows].reshape(norm_rows * w)[:groups]
    group_norms = jnp.sqrt(square_sums / (lat_rows * d))

    def four(u):
        return u[:, :w], u[:, w : 2 * w], u[:, 2 * w : 3 * w], u[:, 3 * w :].T

    query_cross_grad, key_cross_grad, value_cross_grad, output_cross_grad = four(cross_grads)
    query_self_grad, key_self_grad, value_self_grad, output_self_grad = four(self_grads)
    return (
        block_out,
        group_norms,
        latents_grad,
        embed_grad,
        gain_cross_grad,
        query_cross_grad,
        key_cross_grad,
        value_cross_grad,
        output_cross_grad,
        bias_cross_grad,
        gain_self_grad,
        query_self_grad,
        key_self_grad,
        value_self_grad,
        output_self_grad,
        bias_self_grad,
        gain_mlp_grad,
        hidden_weight_grad,
        hidden_bias_grad,
        output_weight_grad,
        output_bias_grad,
    )


def solution(mesh):
    lay = P("grp", None, "tp")
    cols, rows, part = P(None, "tp"), P("tp", None), P("tp")
    attn = (P(), cols, cols, cols, rows, part)
    return jax.shard_map(
        per_device,
        mesh=mesh,
        in_specs=(lay, lay, P("grp", None), P("grp", None), P(), cols)
        + attn
        + attn
        + (P(), cols, part, rows, part, lay),
        out_specs=(lay, P(), lay, cols)
        + (part, cols, cols, cols, rows, part)
        + (part, cols, cols, cols, rows, part)
        + (part, cols, part, rows, part),
        check_vma=False,
    )
```

time: 1700 us -> 768 us (0.45)
  waiting for transfers between devices: 915 us -> 359 us
  blocking collectives: 246 us -> 0 us
  Pallas kernels: 0 us -> 240 us
  matrix products: 186 us -> 0 us
  local copies, waits for them, and re-layouts: 190 us -> 47.7 us
  other arithmetic: 118 us -> 35.2 us
  starting transfers between devices: 18.7 us -> 78.2 us
    psum x1 -> x0, waiting for transfers between devices: 339 us -> none  [per_device(): lax.psum((embed_local, gain_cross_grad, query_cross_grad, key_cross_grad,...]
    ppermute x4 -> x63, waiting for transfers between devices: 27 us -> 355 us  [the longest x58 306 us: flip(): return lax.ppermute(x, axis, [(i, i ^ 1 << bit) for i in range(n)])]
    reduce_scatter x6 -> x0, waiting for transfers between devices: 284 us -> none  [narrow(): return lax.psum_scatter(value, 'tp', scatter_dimension=1, tiled=True)]
    pallas_call x0 -> x12, Pallas kernels: none -> 240 us  [the longest x1 36.9 us: cross_backward(): pl.pallas_call(functools.partial(cross_backward_body, tp), out_shape=(sha...]
    psum x5 -> x0, blocking collectives: 182 us -> none  [the longest x1 113 us: per_device(): lax.psum(jnp.sum(jnp.square(block_out), axis=(0, 2)), ('grp', 'tp'))]
    dot_general x38 -> x0, matrix products: 173 us -> none  [the longest x10 46.2 us: plain_dot(): return jnp.dot(left, right, preferred_element_type=jnp.float32)]
    all_gather x6 -> x0, waiting for transfers between devices: 168 us -> none  [widen(): return lax.all_gather(value, 'tp', axis=1, tiled=True)]
    reshape x21 -> x9, local copies, waits for them, and re-layouts: 106 us -> 5.69 us  [the longest x4 5.01 us: from_groups(): x.reshape(per, n // tp, lat, tp, w)]
  transfers between devices with their start and end apart: 19 -> 67, of which waited for: 13 -> 28; matrix products, arithmetic and copies ran while one was open for 15% -> 10% of each run, Pallas kernels for 0% -> 18%
where the time goes in v1:
time: 768 us; the launch traced here: 762 us
  waiting for transfers between devices  359 us (47%)
  Pallas kernels  240 us (31%)
  starting transfers between devices  78.2 us (10%)
  local copies, waits for them, and re-layouts  47.7 us (6%)
  other arithmetic  35.2 us (5%)
    ppermute x58, waiting for transfers between devices, flip(): return lax.ppermute(x, axis, [(i, i ^ 1 << bit) for i in range(n)])  306 us
    ppermute x58, starting transfers between devices, flip(): return lax.ppermute(x, axis, [(i, i ^ 1 << bit) for i in range(n)])  50.3 us
    pallas_call x1, Pallas kernels, cross_backward(): pl.pallas_call(functools.partial(cross_backward_body, tp), out_shape=(sha...  36.9 us
    pallas_call x1, Pallas kernels, cross_forward(): pl.pallas_call(functools.partial(cross_forward_body, tp), out_shape=(shap...  36.2 us
    pallas_call x2, Pallas kernels, cross_weights(): pl.pallas_call(functools.partial(cross_weights_body, tp, odd), out_shape=...  36.1 us
    ppermute x4, waiting for transfers between devices, swap(): return lax.ppermute(x, 'tp', [(j, j ^ k) for j in range(tp)])  32.3 us
    pallas_call x2, Pallas kernels, feed(): pl.pallas_call(feed_body, out_shape=(shape((2, rows, ff), BF), shape((2,...  31.1 us
    pallas_call x1, Pallas kernels, self_backward(): pl.pallas_call(functools.partial(self_backward_body, tp, len(gots)), out_...  30.5 us
  transfers between devices with their start and end apart: 67, of which 28 were waited for; matrix products, arithmetic and copies ran while one was open for 10% of the time, Pallas kernels for 18%

profile of v1, /device:TPU:0, one launch (start us, length us, event | category | flops | bytes accessed | tf_op | source)
XLA Modules:
  0.0 762.3 jit_solution(13722533916496779990)
XLA Ops:
  3.5 7.4 all-to-all-start
  17.0 8.8 %collective-permute-done.1 = f32[135,256]{1,0:T(8,128)S(1)} collective-permute-done((f32[135,256]{1,0:T(8,128)S(1)}, f32[135,256]{1,0:T(8,128)S(1)}, u32[]{:S(2)}, u32[]{:S(2)}) %collective-permute-start.1) | collective-permute-done | bytes 138272 | tf_op jit(solution)/shard_map/ppermute | solution.py:590
  28.0 16.7 %collective-permute-done.3.refs_0_ = bf16[256,1024]{1,0:T(8,128)(2,1)} collective-permute-done((bf16[256,1024]{1,0:T(8,128)(2,1)}, bf16[256,1024]{1,0:T(8,128)(2,1)}, u32[]{:S(2)}, u32[]{:S(2)}) %collective-permute-start.3) | collective-permute-done | bytes 524320 | tf_op jit(solution)/shard_map/ppermute | solution.py:756
  52.0 44.3 %collective-permute-done.20.refs_6_.refs_3_ = bf16[256,1024]{1,0:T(8,128)(2,1)} collective-permute-done((bf16[256,1024]{1,0:T(8,128)(2,1)}, bf16[256,1024]{1,0:T(8,128)(2,1)}, u32[]{:S(2)}, u32[]{:S(2)}) %collective-permute-start.20) | collective-permute-done | bytes 524320 | tf_op jit(solution)/shard_map/ppermute | solution.py:590
  103.8 36.0 %collective-permute-done.5.refs_2_ = bf16[256,1024]{1,0:T(8,128)(2,1)} collective-permute-done((bf16[256,1024]{1,0:T(8,128)(2,1)}, bf16[256,1024]{1,0:T(8,128)(2,1)}, u32[]{:S(2)}, u32[]{:S(2)}) %collective-permute-start.5) | collective-permute-done | bytes 524320 | tf_op jit(solution)/shard_map/ppermute | solution.py:590
  159.5 36.2 %cross_forward.1 = (bf16[2048,2048]{1,0:T(8,128)(2,1)}, bf16[512,1024]{1,0:T(8,128)(2,1)}, bf16[512,1024]{1,0:T(8,128)(2,1)}, f32[512,1024]{1,0:T(8,128)}, bf16[...) custom-call(s32[16]{0:T(128)} %compare_select_fusion.1.idx, s32[16]{0:T(128)} %gather_fusion, ...), custom_call_target="tpu_custom_call" | custom-call | tf_op jit(solution)/shard_map/cross_forward/pallas_call | solution.py:163
  196.4 23.9 %self_forward.1 = (bf16[512,3072]{1,0:T(8,128)(2,1)}, bf16[512,1024]{1,0:T(8,128)(2,1)}, f32[512,1024]{1,0:T(8,128)}, bf16[512,1024]{1,0:T(8,128)(2,1)}) custom-call(bf16[512,1024]{1,0:T(8,128)(2,1)} %get-tuple-element.55.ns, f32[512,1024]{1,0:T(8,128)} %get-tuple-element.56.x1, f32[1,1024]{1,0:T(1,128)} %bitcast.126, f32[1,1024]{1,0:T(1,128)} %bitcast.128, ...), custom_call_target="tpu_custom_call" | custom-call | tf_op jit(solution)/shard_map/self_forward/pallas_call | solution.py:232
  222.5 23.2 %collective-permute-done.24.nm.refs_5_ = bf16[512,1024]{1,0:T(8,128)(2,1)S(1)} collective-permute-done((bf16[512,1024]{1,0:T(8,128)(2,1)}, bf16[512,1024]{1,0:T(8,128)(2,1)S(1)}, u32[]{:S(2)}, u32[]{:S(2)}) %collective-permute-start.24) | collective-permute-done | bytes 1048608 | tf_op jit(solution)/shard_map/ppermute | solution.py:779
  246.7 15.3 %feed.3 = (bf16[2,512,1024]{2,1,0:T(8,128)(2,1)}, bf16[2,512,1024]{2,1,0:T(8,128)(2,1)}, bf16[512,1024]{1,0:T(8,128)(2,1)}, bf16[512,1024]{1,0:T(8,128)(2,1)}, f32[2,1024]{1,0:T(2,128)}) custom-call(bf16[512,1024]{1,0:T(8,128)(2,1)} %copy-done.6, bf16[512,1024]{1,0:T(8,128)(2,1)} %copy-done.5, f32[2,1024]{1,0:T(2,128)} %pad_maximum_fusion.2.hb, ...), custom_call_target="tpu_custom_call" | custom-call | tf_op jit(solution)/shard_map/feed/pallas_call | solution.py:281
  263.4 15.8 %feed.2 = (bf16[2,512,1024]{2,1,0:T(8,128)(2,1)}, bf16[2,512,1024]{2,1,0:T(8,128)(2,1)}, f32[512,1024]{1,0:T(8,128)}, f32[512,1024]{1,0:T(8,128)}, f32[2,1024]{1,0:T(2,128)}) custom-call(bf16[512,1024]{1,0:T(8,128)(2,1)} %get-tuple-element.58.nm.refs_4_, bf16[512,1024]{1,0:T(8,128)(2,1)} %bitcast.104, f32[2,1024]{1,0:T(2,128)} %pad_maximum_fusion.2.hb, ...), custom_call_target="tpu_custom_call" | custom-call | tf_op jit(solution)/shard_map/feed/pallas_call | solution.py:281
  279.2 7.2 collective-permute-done.27.refs_0_
  287.5 30.5 %self_backward.1 = (bf16[512,1024]{1,0:T(8,128)(2,1)}, bf16[512,3072]{1,0:T(8,128)(2,1)}, f32[512,1024]{1,0:T(8,128)}, bf16[512,1024]{1,0:T(8,128)(2,1)}, f32[8,1024]{1,0:T(8,128)}) custom-call(bf16[512,1024]{1,0:T(8,128)(2,1)} %bitcast.105, f32[512,1024]{1,0:T(8,128)} %get-tuple-element.61.gnm, f32[512,1024]{1,0:T(8,128)} %get-tuple-element.57.x2, ...), custom_call_target="tpu_custom_call" | custom-call | tf_op jit(solution)/shard_map/self_backward/pallas_call | solution.py:403
  318.0 36.9 %cross_backward.1 = (bf16[512,1024]{1,0:T(8,128)(2,1)}, bf16[2048,2048]{1,0:T(8,128)(2,1)}, bf16[512,1024]{1,0:T(8,128)(2,1)}, f32[128,1024]{1,0:T(8,128)}, f32[8,1024]{1,0:T(8,128)}) custom-call(s32[16]{0:T(128)} %compare_select_fusion.1.idx, s32[16]{0:T(128)} %gather_fusion, bf16[512,1024]{1,0:T(8,128)(2,1)} %get-tuple-element.64.b1, ...), custom_call_target="tpu_custom_call" | custom-call | tf_op jit(solution)/shard_map/cross_backward/pallas_call | solution.py:495
  354.9 17.6 %cross_weights.2 = bf16[2,1024,1024]{2,1,0:T(8,128)(2,1)} custom-call(bf16[512,1024]{1,0:T(8,128)(2,1)} %get-tuple-element.74.nc, bf16[512,1024]{1,0:T(8,128)(2,1)} %get-tuple-element.75.dq, bf16[512,1024]{1,0:T(8,128)(2,1)} %get-tuple-element.76.o, bf16[512,1024]{1,0:T(8,128)(2,1)} %get-tuple-element.64.b1, bf16[2048,2048]{1,0:T(8,128)(2,1)} %get-tuple-element.77.dkv, ...), custom_call_target="tpu_custom_call" | custom-call | tf_op jit(solution)/shard_map/cross_weights/pallas_call | solution.py:577
  374.2 10.7 %self_weights.2 = bf16[2,1024,1024]{2,1,0:T(8,128)(2,1)} custom-call(bf16[512,1024]{1,0:T(8,128)(2,1)} %get-tuple-element.55.ns, bf16[512,3072]{1,0:T(8,128)(2,1)} %get-tuple-element.78.dqkv, bf16[512,1024]{1,0:T(8,128)(2,1)} %get-tuple-element.79.o, bf16[512,1024]{1,0:T(8,128)(2,1)} %get-tuple-element.80.b2), custom_call_target="tpu_custom_call" | custom-call | tf_op jit(solution)/shard_map/self_weights/pallas_call | solution.py:544
  385.0 10.9 %feed_weights.2 = (bf16[1024,1024]{1,0:T(8,128)(2,1)}, bf16[1024,1024]{1,0:T(8,128)(2,1)}) custom-call(bf16[2,512,1024]{2,1,0:T(8,128)(2,1)} %get-tuple-element.81.refs_0_, bf16[2,512,1024]{2,1,0:T(8,128)(2,1)} %get-tuple-element.82.refs_1_, bf16[512,1024]{1,0:T(8,128)(2,1)} %bitcast.106, bf16[512,1024]{1,0:T(8,128)(2,1)} %copy-done.5, ...), custom_call_target="tpu_custom_call" | custom-call | tf_op jit(solution)/shard_map/feed_weights/pallas_call | solution.py:329
  411.9 12.0 %feed_weights.3 = (bf16[1024,1024]{1,0:T(8,128)(2,1)}, bf16[1024,1024]{1,0:T(8,128)(2,1)}) custom-call(bf16[2,512,1024]{2,1,0:T(8,128)(2,1)} %get-tuple-element.81.refs_0_, bf16[2,512,1024]{2,1,0:T(8,128)(2,1)} %get-tuple-element.82.refs_1_, bf16[512,1024]{1,0:T(8,128)(2,1)} %bitcast.107, bf16[512,1024]{1,0:T(8,128)(2,1)} %copy-done.5, ...), custom_call_target="tpu_custom_call" | custom-call | tf_op jit(solution)/shard_map/feed_weights/pallas_call | solution.py:329
  441.1 18.5 %cross_weights.3 = bf16[2,1024,1024]{2,1,0:T(8,128)(2,1)} custom-call(bf16[512,1024]{1,0:T(8,128)(2,1)} %get-tuple-element.74.nc, bf16[512,1024]{1,0:T(8,128)(2,1)} %get-tuple-element.75.dq, bf16[512,1024]{1,0:T(8,128)(2,1)} %get-tuple-element.76.o, bf16[512,1024]{1,0:T(8,128)(2,1)} %get-tuple-element.64.b1, bf16[2048,2048]{1,0:T(8,128)(2,1)} %get-tuple-element.77.dkv, ...), custom_call_target="tpu_custom_call" | custom-call | tf_op jit(solution)/shard_map/cross_weights/pallas_call | solution.py:577
  464.8 11.9 %self_weights.3 = bf16[2,1024,1024]{2,1,0:T(8,128)(2,1)} custom-call(bf16[512,1024]{1,0:T(8,128)(2,1)} %get-tuple-element.55.ns, bf16[512,3072]{1,0:T(8,128)(2,1)} %get-tuple-element.78.dqkv, bf16[512,1024]{1,0:T(8,128)(2,1)} %get-tuple-element.79.o, bf16[512,1024]{1,0:T(8,128)(2,1)} %get-tuple-element.80.b2, ...), custom_call_target="tpu_custom_call" | custom-call | tf_op jit(solution)/shard_map/self_weights/pallas_call | solution.py:544
  480.5 38.5 %collective-permute-done.28 = f32[2,144,256]{2,1,0:T(8,128)S(1)} collective-permute-done((f32[2,144,256]{2,1,0:T(8,128)S(1)}, f32[2,144,256]{2,1,0:T(8,128)S(1)}, u32[]{:S(2)}, u32[]{:S(2)}) %collective-permute-start.28) | collective-permute-done | bytes 294944 | tf_op jit(solution)/shard_map/ppermute | solution.py:590
  529.2 6.6 collective-permute-done.52
  540.7 22.6 %collective-permute-done.42 = bf16[1024,1024]{1,0:T(8,128)(2,1)S(1)} collective-permute-done((bf16[1024,1024]{1,0:T(8,128)(2,1)S(1)}, bf16[1024,1024]{1,0:T(8,128)(2,1)S(1)}, u32[]{:S(2)}, u32[]{:S(2)}) %collective-permute-start.42) | collective-permute-done | bytes 2097184 | tf_op jit(solution)/shard_map/ppermute | solution.py:590
  571.9 17.9 %collective-permute-done.53 = bf16[128,1024]{1,0:T(8,128)(2,1)S(1)} collective-permute-done((bf16[128,1024]{1,0:T(8,128)(2,1)S(1)}, bf16[128,1024]{1,0:T(8,128)(2,1)S(1)}, u32[]{:S(2)}, u32[]{:S(2)}) %collective-permute-start.53) | collective-permute-done | bytes 262176 | tf_op jit(solution)/shard_map/ppermute | solution.py:590
  593.9 7.2 collective-permute-done.59
  601.3 20.5 %collective-permute-done.36 = bf16[256,1024]{1,0:T(8,128)(2,1)S(1)} collective-permute-done((bf16[256,1024]{1,0:T(8,128)(2,1)S(1)}, bf16[256,1024]{1,0:T(8,128)(2,1)S(1)}, u32[]{:S(2)}, u32[]{:S(2)}) %collective-permute-start.36) | collective-permute-done | bytes 524320 | tf_op jit(solution)/shard_map/ppermute | solution.py:590
  628.0 10.7 %collective-permute-done.44 = bf16[256,1024]{1,0:T(8,128)(2,1)S(1)} collective-permute-done((bf16[256,1024]{1,0:T(8,128)(2,1)S(1)}, bf16[256,1024]{1,0:T(8,128)(2,1)S(1)}, u32[]{:S(2)}, u32[]{:S(2)}) %collective-permute-start.44) | collective-permute-done | bytes 524320 | tf_op jit(solution)/shard_map/ppermute | solution.py:590
  647.8 12.6 %collective-permute-done.38 = bf16[128,1024]{1,0:T(8,128)(2,1)} collective-permute-done((bf16[128,1024]{1,0:T(8,128)(2,1)S(1)}, bf16[128,1024]{1,0:T(8,128)(2,1)}, u32[]{:S(2)}, u32[]{:S(2)}) %collective-permute-start.38) | collective-permute-done | bytes 262176 | tf_op jit(solution)/shard_map/ppermute | solution.py:590
  667.8 10.2 %collective-permute-done.61 = bf16[256,1024]{1,0:T(8,128)(2,1)} collective-permute-done((bf16[256,1024]{1,0:T(8,128)(2,1)S(1)}, bf16[256,1024]{1,0:T(8,128)(2,1)}, u32[]{:S(2)}, u32[]{:S(2)}) %collective-permute-start.61) | collective-permute-done | bytes 524320 | tf_op jit(solution)/shard_map/ppermute | solution.py:590
  690.8 8.6 %collective-permute-done.47 = bf16[256,1024]{1,0:T(8,128)(2,1)S(1)} collective-permute-done((bf16[256,1024]{1,0:T(8,128)(2,1)S(1)}, bf16[256,1024]{1,0:T(8,128)(2,1)S(1)}, u32[]{:S(2)}, u32[]{:S(2)}) %collective-permute-start.47) | collective-permute-done | bytes 524320 | tf_op jit(solution)/shard_map/ppermute | solution.py:590
  705.0 10.8 %collective-permute-done.62 = bf16[512,1024]{1,0:T(8,128)(2,1)S(1)} collective-permute-done((bf16[512,1024]{1,0:T(8,128)(2,1)S(1)}, bf16[512,1024]{1,0:T(8,128)(2,1)S(1)}, u32[]{:S(2)}, u32[]{:S(2)}) %collective-permute-start.62) | collective-permute-done | bytes 1048608 | tf_op jit(solution)/shard_map/ppermute | solution.py:590
  718.7 19.6 %collective-permute-done.40 = bf16[512,1024]{1,0:T(8,128)(2,1)S(1)} collective-permute-done((bf16[512,1024]{1,0:T(8,128)(2,1)S(1)}, bf16[512,1024]{1,0:T(8,128)(2,1)S(1)}, u32[]{:S(2)}, u32[]{:S(2)}) %collective-permute-start.40) | collective-permute-done | bytes 1048608 | tf_op jit(solution)/shard_map/ppermute | solution.py:590
  742.4 15.7 %collective-permute-done.48 = bf16[512,1024]{1,0:T(8,128)(2,1)S(1)} collective-permute-done((bf16[512,1024]{1,0:T(8,128)(2,1)S(1)}, bf16[512,1024]{1,0:T(8,128)(2,1)S(1)}, u32[]{:S(2)}, u32[]{:S(2)}) %collective-permute-start.48) | collective-permute-done | bytes 1048608 | tf_op jit(solution)/shard_map/ppermute | solution.py:590
  (301 shorter events, 175.0 us)
Async XLA Ops:
  3.5 95.0 %all-to-all-start = ((bf16[32,4,16,256]{3,2,1,0:T(8,128)(2,1)}), bf16[32,4,16,256]{3,2,1,0:T(8,128)(2,1)}, u32[]{:S(2)}, u32[]{:S(2)}) async-start(bf16[32,4,16,256]{3,2,1,0:T(8,128)(2,1)} %bitcast.2), calls=%async_computation | async-start | bytes 2097152 | tf_op jit(solution)/shard_map/all_to_all | solution.py:676
  44.7 96.1 %collective-permute-start.17 = (bf16[1024,768]{1,0:T(8,128)(2,1)S(1)}, bf16[1024,768]{1,0:T(8,128)(2,1)S(1)}, u32[]{:S(2)}, u32[]{:S(2)}) collective-permute-start(bf16[1024,768]{1,0:T(8,128)(2,1)S(1)} %constant_dynamic-update-slice_fusion.2.refs_0_.refs_5_), channel_id=1, source_target_pairs={{0,2},{1,3},{2,0},{3,1},{4,6},{5,7},{6,4},{7,5},{8,10},{9,11},{10,... | collective-permute-start | bytes 4718600 | tf_op jit(solution)/shard_map/ppermute | solution.py:590
  49.0 47.3 %collective-permute-start.20 = (bf16[256,1024]{1,0:T(8,128)(2,1)}, bf16[256,1024]{1,0:T(8,128)(2,1)}, u32[]{:S(2)}, u32[]{:S(2)}) collective-permute-start(bf16[256,1024]{1,0:T(8,128)(2,1)} %refs_1_.1), channel_id=1, source_target_pairs={{0,2},{1,3},{2,0},{3,1},{4,6},{5,7},{6,4},{7,5},{8,10},{9,11},{10,... | collective-permute-start | bytes 1572872 | tf_op jit(solution)/shard_map/ppermute | solution.py:590
  49.6 90.4 %collective-permute-start.7 = (bf16[1024,512]{1,0:T(8,128)(2,1)}, bf16[1024,512]{1,0:T(8,128)(2,1)}, u32[]{:S(2)}, u32[]{:S(2)}) collective-permute-start(bf16[1024,512]{1,0:T(8,128)(2,1)} %constant_dynamic-update-slice_fusion.refs_5_), channel_id=1, source_target_pairs={{0,1},{1,0},{2,3},{3,2},{4,5},{5,4},{6,7},{7,6},{8,9},{9,8},{10,11... | collective-permute-start | bytes 3145736 | tf_op jit(solution)/shard_map/ppermute | solution.py:590
  51.3 89.0 %collective-permute-start.8 = (bf16[1024,512]{1,0:T(8,128)(2,1)}, bf16[1024,512]{1,0:T(8,128)(2,1)}, u32[]{:S(2)}, u32[]{:S(2)}) collective-permute-start(bf16[1024,512]{1,0:T(8,128)(2,1)} %constant_dynamic-update-slice_fusion.refs_5_), channel_id=1, source_target_pairs={{0,2},{1,3},{2,0},{3,1},{4,6},{5,7},{6,4},{7,5},{8,10},{9,11},{10,... | collective-permute-start | bytes 3145736 | tf_op jit(solution)/shard_map/ppermute | solution.py:590
  52.0 44.9 %collective-permute-start.4 = (bf16[256,1024]{1,0:T(8,128)(2,1)}, bf16[256,1024]{1,0:T(8,128)(2,1)}, u32[]{:S(2)}, u32[]{:S(2)}) collective-permute-start(bf16[256,1024]{1,0:T(8,128)(2,1)} %collective-permute-done.3.refs_0_), channel_id=1, source_target_pairs={{0,1},{1,0},{2,3},{3,2},{4,5},{5,4},{6,7},{7,6},{8,9},{9,8},{10,11... | collective-permute-start | bytes 1572872 | tf_op jit(solution)/shard_map/ppermute | solution.py:590
  96.3 43.5 %collective-permute-start.5 = (bf16[256,1024]{1,0:T(8,128)(2,1)}, bf16[256,1024]{1,0:T(8,128)(2,1)}, u32[]{:S(2)}, u32[]{:S(2)}) collective-permute-start(bf16[256,1024]{1,0:T(8,128)(2,1)} %collective-permute-done.3.refs_0_), channel_id=1, source_target_pairs={{0,2},{1,3},{2,0},{3,1},{4,6},{5,7},{6,4},{7,5},{8,10},{9,11},{10,... | collective-permute-start | bytes 1572872 | tf_op jit(solution)/shard_map/ppermute | solution.py:590
  96.9 43.5 %collective-permute-start.12 = (bf16[1024,256]{1,0:T(8,128)(2,1)}, bf16[1024,256]{1,0:T(8,128)(2,1)}, u32[]{:S(2)}, u32[]{:S(2)}) collective-permute-start(bf16[1024,256]{1,0:T(8,128)(2,1)} %collective-permute-done.11.refs_11_.refs_6_), channel_id=1, source_target_pairs={{0,1},{1,0},{2,3},{3,2},{4,5},{5,4},{6,7},{7,6},{8,9},{9,8},{10,11... | collective-permute-start | bytes 1572872 | tf_op jit(solution)/shard_map/ppermute | solution.py:590
  98.5 56.9 %all-to-all-start.1 = ((bf16[32,4,16,256]{3,2,1,0:T(8,128)(2,1)}), bf16[32,4,16,256]{3,2,1,0:T(8,128)(2,1)}, u32[]{:S(2)}, u32[]{:S(2)}) async-start(bf16[32,4,16,256]{3,2,1,0:T(8,128)(2,1)} %bitcast.112), calls=%async_computation.1 | async-start | bytes 2097152 | tf_op jit(solution)/shard_map/all_to_all | solution.py:676
  139.8 56.6 %collective-permute-start.16 = (bf16[1024,768]{1,0:T(8,128)(2,1)S(1)}, bf16[1024,768]{1,0:T(8,128)(2,1)}, u32[]{:S(2)}, u32[]{:S(2)}) collective-permute-start(bf16[1024,768]{1,0:T(8,128)(2,1)S(1)} %constant_dynamic-update-slice_fusion.2.refs_0_.refs_5_), channel_id=1, source_target_pairs={{0,1},{1,0},{2,3},{3,2},{4,5},{5,4},{6,7},{7,6},{8,9},{9,8},{10,11... | collective-permute-start | bytes 4718600 | tf_op jit(solution)/shard_map/ppermute | solution.py:590
  140.9 55.5 %collective-permute-start.18 = (bf16[1024,768]{1,0:T(8,128)(2,1)S(1)}, bf16[1024,768]{1,0:T(8,128)(2,1)}, u32[]{:S(2)}, u32[]{:S(2)}) collective-permute-start(bf16[1024,768]{1,0:T(8,128)(2,1)S(1)} %collective-permute-done.17.refs_2_.refs_7_), channel_id=1, source_target_pairs={{0,1},{1,0},{2,3},{3,2},{4,5},{5,4},{6,7},{7,6},{8,9},{9,8},{10,11... | collective-permute-start | bytes 4718600 | tf_op jit(solution)/shard_map/ppermute | solution.py:590
  144.8 77.6 %collective-permute-start.22 = (bf16[1024,1024]{1,0:T(8,128)(2,1)}, bf16[1024,1024]{1,0:T(8,128)(2,1)}, u32[]{:S(2)}, u32[]{:S(2)}) collective-permute-start(bf16[1024,1024]{1,0:T(8,128)(2,1)} %wh0.3), channel_id=1, source_target_pairs={{0,1},{1,0},{2,3},{3,2},{4,5},{5,4},{6,7},{7,6},{8,9},{9,8},{10,11... | collective-permute-start | bytes 6291464 | tf_op jit(solution)/shard_map/ppermute | solution.py:590
  146.3 76.1 %collective-permute-start.23 = (bf16[1024,1024]{1,0:T(8,128)(2,1)}, bf16[1024,1024]{1,0:T(8,128)(2,1)}, u32[]{:S(2)}, u32[]{:S(2)}) collective-permute-start(bf16[1024,1024]{1,0:T(8,128)(2,1)} %wo0.3), channel_id=1, source_target_pairs={{0,1},{1,0},{2,3},{3,2},{4,5},{5,4},{6,7},{7,6},{8,9},{9,8},{10,11... | collective-permute-start | bytes 6291464 | tf_op jit(solution)/shard_map/ppermute | solution.py:590
  149.0 46.7 %collective-permute-start.21 = (bf16[256,1024]{1,0:T(8,128)(2,1)}, bf16[256,1024]{1,0:T(8,128)(2,1)}, u32[]{:S(2)}, u32[]{:S(2)}) collective-permute-start(bf16[256,1024]{1,0:T(8,128)(2,1)} %collective-permute-done.20.refs_6_.refs_3_), channel_id=1, source_target_pairs={{0,1},{1,0},{2,3},{3,2},{4,5},{5,4},{6,7},{7,6},{8,9},{9,8},{10,11... | collective-permute-start | bytes 1572872 | tf_op jit(solution)/shard_map/ppermute | solution.py:590
  372.5 68.5 %collective-permute-start.33 = (bf16[2,1024,1024]{2,1,0:T(8,128)(2,1)}, bf16[2,1024,1024]{2,1,0:T(8,128)(2,1)}, u32[]{:S(2)}, u32[]{:S(2)}) collective-permute-start(bf16[2,1024,1024]{2,1,0:T(8,128)(2,1)} %cross_weights.2), channel_id=1, source_target_pairs={{0,1},{1,0},{2,3},{3,2},{4,5},{5,4},{6,7},{7,6},{8,9},{9,8},{10,11... | collective-permute-start | bytes 12582920 | tf_op jit(solution)/shard_map/ppermute | solution.py:590
  384.9 80.0 %collective-permute-start.41 = (bf16[2,1024,1024]{2,1,0:T(8,128)(2,1)}, bf16[2,1024,1024]{2,1,0:T(8,128)(2,1)}, u32[]{:S(2)}, u32[]{:S(2)}) collective-permute-start(bf16[2,1024,1024]{2,1,0:T(8,128)(2,1)} %self_weights.2), channel_id=1, source_target_pairs={{0,1},{1,0},{2,3},{3,2},{4,5},{5,4},{6,7},{7,6},{8,9},{9,8},{10,11... | collective-permute-start | bytes 12582920 | tf_op jit(solution)/shard_map/ppermute | solution.py:590
  426.3 92.8 %collective-permute-start.51 = (bf16[512,1024]{1,0:T(8,128)(2,1)}, bf16[512,1024]{1,0:T(8,128)(2,1)}, u32[]{:S(2)}, u32[]{:S(2)}) collective-permute-start(bf16[512,1024]{1,0:T(8,128)(2,1)} %constant_dynamic-slice_fusion.5), channel_id=1, source_target_pairs={{0,4},{4,0},{8,12},{12,8},{16,20},{20,16},{24,28},{28,24},{1,5},{5... | collective-permute-start | bytes 3145736 | tf_op jit(solution)/shard_map/ppermute | solution.py:590
  429.3 95.2 %collective-permute-start.57 = (bf16[512,1024]{1,0:T(8,128)(2,1)}, bf16[512,1024]{1,0:T(8,128)(2,1)}, u32[]{:S(2)}, u32[]{:S(2)}) collective-permute-start(bf16[512,1024]{1,0:T(8,128)(2,1)} %constant_dynamic-slice_fusion.2), channel_id=1, source_target_pairs={{0,4},{4,0},{8,12},{12,8},{16,20},{20,16},{24,28},{28,24},{1,5},{5... | collective-permute-start | bytes 3145736 | tf_op jit(solution)/shard_map/ppermute | solution.py:590
  433.6 211.4 %all-to-all-start.3 = ((bf16[32,4,16,256]{3,2,1,0:T(8,128)(2,1)}), bf16[32,4,16,256]{3,2,1,0:T(8,128)(2,1)S(1)}, u32[]{:S(2)}, u32[]{:S(2)}) async-start(bf16[32,4,16,256]{3,2,1,0:T(8,128)(2,1)} %bitcast.33), calls=%async_computation.3 | async-start | bytes 2097152 | tf_op jit(solution)/shard_map/all_to_all | solution.py:687
  462.6 73.4 %collective-permute-start.34 = (bf16[1024,1024]{1,0:T(8,128)(2,1)}, bf16[1024,1024]{1,0:T(8,128)(2,1)}, u32[]{:S(2)}, u32[]{:S(2)}) collective-permute-start(bf16[1024,1024]{1,0:T(8,128)(2,1)} %slice_bitcast_fusion.2), channel_id=1, source_target_pairs={{0,2},{1,3},{2,0},{3,1},{4,6},{5,7},{6,4},{7,5},{8,10},{9,11},{10,... | collective-permute-start | bytes 6291464 | tf_op jit(solution)/shard_map/ppermute | solution.py:590
  464.5 54.5 %collective-permute-start.28 = (f32[2,144,256]{2,1,0:T(8,128)S(1)}, f32[2,144,256]{2,1,0:T(8,128)S(1)}, u32[]{:S(2)}, u32[]{:S(2)}) collective-permute-start(f32[2,144,256]{2,1,0:T(8,128)S(1)} %constant_dynamic-slice_fusion.13), channel_id=1, source_target_pairs={{0,2},{1,3},{2,0},{3,1},{4,6},{5,7},{6,4},{7,5},{8,10},{9,11},{10,... | collective-permute-start | bytes 884744 | tf_op jit(solution)/shard_map/ppermute | solution.py:590
  478.6 84.6 %collective-permute-start.42 = (bf16[1024,1024]{1,0:T(8,128)(2,1)S(1)}, bf16[1024,1024]{1,0:T(8,128)(2,1)S(1)}, u32[]{:S(2)}, u32[]{:S(2)}) collective-permute-start(bf16[1024,1024]{1,0:T(8,128)(2,1)S(1)} %slice_bitcast_fusion), channel_id=1, source_target_pairs={{0,2},{1,3},{2,0},{3,1},{4,6},{5,7},{6,4},{7,5},{8,10},{9,11},{10,... | collective-permute-start | bytes 6291464 | tf_op jit(solution)/shard_map/ppermute | solution.py:590
  526.3 42.3 %collective-permute-start.58 = (bf16[256,1024]{1,0:T(8,128)(2,1)S(1)}, bf16[256,1024]{1,0:T(8,128)(2,1)S(1)}, u32[]{:S(2)}, u32[]{:S(2)}) collective-permute-start(bf16[256,1024]{1,0:T(8,128)(2,1)S(1)} %constant_dynamic-slice_fusion.1), channel_id=1, source_target_pairs={{0,8},{4,12},{8,0},{12,4},{16,24},{20,28},{24,16},{28,20},{1,9},{5... | collective-permute-start | bytes 1572872 | tf_op jit(solution)/shard_map/ppermute | solution.py:590
  528.8 40.6 %collective-permute-start.31 = (f32[144,256]{1,0:T(8,128)S(1)}, f32[144,256]{1,0:T(8,128)S(1)}, u32[]{:S(2)}, u32[]{:S(2)}) collective-permute-start(f32[144,256]{1,0:T(8,128)S(1)} %add.209), channel_id=1, source_target_pairs={{0,8},{4,12},{8,0},{12,4},{16,24},{20,28},{24,16},{28,20},{1,9},{5... | collective-permute-start | bytes 442376 | tf_op jit(solution)/shard_map/ppermute | solution.py:590
  538.9 51.1 %collective-permute-start.35 = (bf16[512,1024]{1,0:T(8,128)(2,1)S(1)}, bf16[512,1024]{1,0:T(8,128)(2,1)S(1)}, u32[]{:S(2)}, u32[]{:S(2)}) collective-permute-start(bf16[512,1024]{1,0:T(8,128)(2,1)S(1)} %constant_dynamic-slice_fusion.11), channel_id=1, source_target_pairs={{0,4},{4,0},{8,12},{12,8},{16,20},{20,16},{24,28},{28,24},{1,5},{5... | collective-permute-start | bytes 3145736 | tf_op jit(solution)/shard_map/ppermute | solution.py:590
  569.5 78.3 %collective-permute-start.32 = (f32[144,256]{1,0:T(8,128)S(1)}, f32[144,256]{1,0:T(8,128)S(1)}, u32[]{:S(2)}, u32[]{:S(2)}) collective-permute-start(f32[144,256]{1,0:T(8,128)S(1)} %add.210), channel_id=1, source_target_pairs={{0,16},{4,20},{8,24},{12,28},{16,0},{20,4},{24,8},{28,12},{1,17},{... | collective-permute-start | bytes 442376 | tf_op jit(solution)/shard_map/ppermute | solution.py:590
  593.8 44.8 %collective-permute-start.44 = (bf16[256,1024]{1,0:T(8,128)(2,1)S(1)}, bf16[256,1024]{1,0:T(8,128)(2,1)S(1)}, u32[]{:S(2)}, u32[]{:S(2)}) collective-permute-start(bf16[256,1024]{1,0:T(8,128)(2,1)S(1)} %constant_dynamic-slice_fusion.7), channel_id=1, source_target_pairs={{0,8},{4,12},{8,0},{12,4},{16,24},{20,28},{24,16},{28,20},{1,9},{5... | collective-permute-start | bytes 1572872 | tf_op jit(solution)/shard_map/ppermute | solution.py:590
  601.2 41.1 %collective-permute-start.60 = (bf16[128,1024]{1,0:T(8,128)(2,1)S(1)}, bf16[128,1024]{1,0:T(8,128)(2,1)S(1)}, u32[]{:S(2)}, u32[]{:S(2)}) collective-permute-start(bf16[128,1024]{1,0:T(8,128)(2,1)S(1)} %add_convert_fusion.9), channel_id=1, source_target_pairs={{0,16},{4,20},{8,24},{12,28},{16,0},{20,4},{24,8},{28,12},{1,17},{... | collective-permute-start | bytes 786440 | tf_op jit(solution)/shard_map/ppermute | solution.py:590
  625.4 40.1 %collective-permute-start.55 = (bf16[256,1024]{1,0:T(8,128)(2,1)S(1)}, bf16[256,1024]{1,0:T(8,128)(2,1)}, u32[]{:S(2)}, u32[]{:S(2)}) collective-permute-start(bf16[256,1024]{1,0:T(8,128)(2,1)S(1)} %maximum_select_fusion.10), channel_id=1, source_target_pairs={{0,8},{4,12},{8,0},{12,4},{16,24},{20,28},{24,16},{28,20},{1,9},{5... | collective-permute-start | bytes 1572872 | tf_op jit(solution)/shard_map/ppermute | solution.py:590
  679.7 36.1 %collective-permute-start.62 = (bf16[512,1024]{1,0:T(8,128)(2,1)S(1)}, bf16[512,1024]{1,0:T(8,128)(2,1)S(1)}, u32[]{:S(2)}, u32[]{:S(2)}) collective-permute-start(bf16[512,1024]{1,0:T(8,128)(2,1)S(1)} %maximum_select_fusion.7), channel_id=1, source_target_pairs={{0,4},{4,0},{8,12},{12,8},{16,20},{20,16},{24,28},{28,24},{1,5},{5... | collective-permute-start | bytes 3145736 | tf_op jit(solution)/shard_map/ppermute | solution.py:590
  689.7 48.6 %collective-permute-start.40 = (bf16[512,1024]{1,0:T(8,128)(2,1)S(1)}, bf16[512,1024]{1,0:T(8,128)(2,1)S(1)}, u32[]{:S(2)}, u32[]{:S(2)}) collective-permute-start(bf16[512,1024]{1,0:T(8,128)(2,1)S(1)} %maximum_select_fusion.4), channel_id=1, source_target_pairs={{0,4},{4,0},{8,12},{12,8},{16,20},{20,16},{24,28},{28,24},{1,5},{5... | collective-permute-start | bytes 3145736 | tf_op jit(solution)/shard_map/ppermute | solution.py:590
  699.9 58.3 %collective-permute-start.48 = (bf16[512,1024]{1,0:T(8,128)(2,1)S(1)}, bf16[512,1024]{1,0:T(8,128)(2,1)S(1)}, u32[]{:S(2)}, u32[]{:S(2)}) collective-permute-start(bf16[512,1024]{1,0:T(8,128)(2,1)S(1)} %maximum_select_fusion.5), channel_id=1, source_target_pairs={{0,4},{4,0},{8,12},{12,8},{16,20},{20,16},{24,28},{28,24},{1,5},{5... | collective-permute-start | bytes 3145736 | tf_op jit(solution)/shard_map/ppermute | solution.py:590
  (70 other events, 1526.0 us)

commit v2 on v1

v2 whole, which is shorter than its diff:
```python
import functools

import jax
import jax.numpy as jnp
from jax import lax
from jax.experimental import pallas as pl
from jax.experimental.pallas import tpu as pltpu
from jax.sharding import PartitionSpec as P

HD = 128
PB = 128
NB = 4
EPS = 1e-05
NEG = -1e30
SCALE = HD ** (-0.5)
BF = jnp.bfloat16
F32 = jnp.float32
VMEM_BYTES = 58 * 2**20
GRP = ("z", "x")

ANY = pl.BlockSpec(memory_space=pl.ANY)
VM = pl.BlockSpec(memory_space=pltpu.VMEM)
SM = pl.BlockSpec(memory_space=pltpu.SMEM)


def shape(dims, kind):
    return jax.ShapeDtypeStruct(dims, kind)


def params():
    return pltpu.CompilerParams(vmem_limit_bytes=VMEM_BYTES)


def cost(us):
    return pl.CostEstimate(flops=int(us * 1.1e9), bytes_accessed=int(us * 1e6), transcendentals=0)


def nn(left, right):
    return lax.dot_general(left, right, (((1,), (0,)), ((), ())), preferred_element_type=F32)


def nt(left, right):
    return lax.dot_general(left, right, (((1,), (1,)), ((), ())), preferred_element_type=F32)


def tn(left, right):
    return lax.dot_general(left, right, (((0,), (0,)), ((), ())), preferred_element_type=F32)


def rows_at(i, n):
    return pl.ds(pl.multiple_of(i * n, n), n)


def normalise(x):
    d = x - jnp.mean(x, axis=1, keepdims=True)
    r = lax.rsqrt(jnp.mean(d * d, axis=1, keepdims=True) + EPS)
    return d * r, r


def norm_back(u, xhat, r, gain):
    w = u * gain
    a = jnp.mean(w, axis=1, keepdims=True)
    b = jnp.mean(w * xhat, axis=1, keepdims=True)
    return r * (w - a - xhat * b)


def colsum(x):
    return jnp.sum(x, axis=0, keepdims=True)


def begin(copies):
    for c in copies:
        c.start()


def finish(copies):
    for c in copies:
        c.wait()


def row_copies(pieces, buf, sem):
    n = pieces[0].shape[0]
    return [pltpu.make_async_copy(s, buf.at[pl.ds(p * n, n), :], sem) for p, s in enumerate(pieces)]


def pack_parts(refs, tp, place):
    if len(refs) == tp:
        return [(p, None, r) for p, r in enumerate(refs)]
    parts = [(0, None, refs[0]), (1, None, refs[1])]
    for p in range(2, tp):
        parts.append((p, place[0], refs[2 * p - 2]))
        parts.append((p, 1 - place[0], refs[2 * p - 1]))
    return parts


def col_copies(parts, at, n, buf, sem):
    out = []
    for p, h, r in parts:
        to = pl.ds(p * n, n)
        k = r.shape[0]
        dst = buf.at[:, to] if h is None else buf.at[rows_at(h, k), to]
        out.append(pltpu.make_async_copy(r.at[:, pl.ds(at, n)], dst, sem))
    return out


def block_copies(parts, at, w, buf, sem):
    out = []
    for p, h, r in parts:
        count = r.shape[0] // w
        for k in range(count):
            col = k * w if h is None else pl.multiple_of((h * count + k) * w, 128)
            src = r.at[pl.ds(k * w, w), pl.ds(at, w)]
            out.append(pltpu.make_async_copy(src, buf.at[pl.ds(p * w, w), pl.ds(col, w)], sem))
    return out


def softmax_parts(s, axis):
    e = jnp.exp((s - jnp.max(s, axis=axis, keepdims=True)) * SCALE)
    return e * (1.0 / jnp.sum(e, axis=axis, keepdims=True))


def pack_body(counts, *refs):
    outs, at = refs[-len(counts) :], 0
    for n, out in zip(counts, outs):
        col, rows = 0, out.shape[0]
        for r in refs[at : at + n]:
            if r.shape[0] == rows:
                out[:, col : col + r.shape[1]] = r[...]
                col += r.shape[1]
            else:
                w = r.shape[0]
                for k in range(rows // w):
                    out[k * w : (k + 1) * w, col : col + w] = r[:, k * w : (k + 1) * w]
                col += w
        at += n


def packed(groups, late=()):
    counts = [len(g) for g in groups]
    ins = [x for g in groups for x in g]
    rows = groups[0][0].shape[0]
    outs = []
    for g in groups:
        cols = sum(x.shape[1] if x.shape[0] == rows else x.shape[0] for x in g)
        outs.append(shape((rows, cols), g[0].dtype))
    n = len(ins)
    return pl.pallas_call(
        lambda *refs: pack_body(counts, *refs[:n], *refs[n + len(late) :]),
        out_shape=outs,
        in_specs=[VM] * n + [ANY] * len(late),
        out_specs=[VM] * len(outs),
        compiler_params=pltpu.CompilerParams(vmem_limit_bytes=12 * 2**20),
        cost_estimate=cost(2),
        name="packed",
    )(*ins, *late)


def part_body(n, at, x, *refs):
    out, sem = refs[-2:]
    copy = pltpu.make_async_copy(x.at[pl.ds(pl.multiple_of(at[0] * n, n), n), :], out, sem)
    copy.start()
    copy.wait()


def part_of(x, at, n, late=()):
    return pl.pallas_call(
        functools.partial(part_body, n),
        out_shape=shape((n, x.shape[1]), x.dtype),
        in_specs=[SM] + [ANY] * (1 + len(late)),
        out_specs=VM,
        scratch_shapes=[pltpu.SemaphoreType.DMA],
        cost_estimate=cost(1),
        name="part_of",
    )(at, x, *late)


def share_copies(places, parts, bufs, sem):
    out = []
    for r, x in zip(parts, (places[0], 1 - places[0])):
        c = bufs[0].shape[0] // (2 * r.shape[0])
        for z in range(r.shape[0]):
            for j, buf in enumerate(bufs):
                src = r.at[z, pl.ds(j * c, c), :]
                out.append(pltpu.make_async_copy(src, buf.at[rows_at(2 * z + x, c), :], sem))
    return out


def final_body(places, own, other, *refs):
    q, k, v, o, qo_b, kv_b, sem = refs[-7:]
    copies = share_copies(places, (own, other), (qo_b, kv_b), sem)
    begin(copies)
    finish(copies)
    w = o.shape[0]
    q[...] = qo_b[0:w, :].astype(F32).T
    o[...] = qo_b[w : 2 * w, :].astype(F32)
    k[...] = kv_b[0:w, :].astype(F32).T
    v[...] = kv_b[w : 2 * w, :].astype(F32).T


def final(places, w, own, other, late=()):
    d = own.shape[2]
    tall, flat = shape((d, w), F32), shape((w, d), F32)
    return pl.pallas_call(
        final_body,
        out_shape=(tall, tall, tall, flat),
        in_specs=[SM] + [ANY] * (2 + len(late)),
        out_specs=[VM] * 4,
        scratch_shapes=[pltpu.VMEM((2 * w, d), BF)] * 2 + [pltpu.SemaphoreType.DMA],
        compiler_params=params(),
        cost_estimate=cost(5),
        name="final",
    )(places, own, other, *late)


def final_feed_body(places, own, other, out, hid, out_b, hid_b, sem):
    copies = share_copies(places, (own, other), (out_b, hid_b), sem)
    begin(copies)
    finish(copies)
    out[...] = out_b[...].astype(F32)
    hid[...] = hid_b[...].astype(F32).T


def final_feed(places, own, other):
    nz, c, d = own.shape
    ff = nz * c
    return pl.pallas_call(
        final_feed_body,
        out_shape=(shape((ff, d), F32), shape((d, ff), F32)),
        in_specs=[SM] + [ANY] * 2,
        out_specs=[VM] * 2,
        scratch_shapes=[pltpu.VMEM((ff, d), BF)] * 2 + [pltpu.SemaphoreType.DMA],
        compiler_params=params(),
        cost_estimate=cost(6),
        name="final_feed",
    )(places, own, other)


def keys_body(tp, points, came0, came1, *refs):
    packs, (kv, kv_b, ext_b, wkv_b, sems) = refs[:tp], refs[-5:]
    ext, d = ext_b.shape
    half = ext // 2
    near_c = [pltpu.make_async_copy(points.at[pl.ds(0, half), :], ext_b.at[pl.ds(half, half), :], sems.at[0])]
    far_c = row_copies([came0, came1], ext_b, sems.at[1])
    w_c = col_copies(pack_parts(packs, tp, None), 0, packs[0].shape[1], wkv_b, sems.at[2])
    for c in (w_c, near_c, far_c):
        begin(c)
    finish(w_c)
    span = 512

    def out_copy(i):
        s = rows_at(i, span)
        return pltpu.make_async_copy(kv_b.at[s, :], kv.at[s, :], sems.at[3])

    def work(i):
        s = rows_at(i, span)
        kv_b[s, :] = nn(ext_b[s, :], wkv_b[...]).astype(BF)
        out_copy(i).start()

    finish(near_c)
    pl.loop(half // span, ext // span)(work)
    finish(far_c)
    pl.loop(0, half // span)(work)

    @pl.loop(0, ext // span)
    def _(i):
        out_copy(i).wait()


def keys_values(points, came, packs, late):
    tp = len(packs)
    ext, d = points.shape
    return pl.pallas_call(
        functools.partial(keys_body, tp),
        out_shape=shape((ext, 2 * d), BF),
        in_specs=[ANY] * (3 + tp + len(late)),
        out_specs=ANY,
        scratch_shapes=[
            pltpu.VMEM((ext, 2 * d), BF),
            pltpu.VMEM((ext, d), BF),
            pltpu.VMEM((d, 2 * d), BF),
            pltpu.SemaphoreType.DMA((4,)),
        ],
        compiler_params=params(),
        cost_estimate=cost(14),
        name="keys_values",
    )(points, *came, *packs, *late)


def cross_forward_body(tp, idx, lens, x0, gain_c, gain_s, bias, kv, *refs):
    parts = pack_parts(refs[:tp], tp, None)
    (q, o, x1, nc, ns, kv_b, wq_b, wo_b, acc, sems) = refs[-10:]
    rows, d = x0.shape
    w = d // tp
    wq_c = col_copies(parts, 0, w, wq_b, sems.at[0])
    wo_c = block_copies(parts, w, w, wo_b, sems.at[1])
    kv_c = [pltpu.make_async_copy(kv, kv_b, sems.at[2])]
    for c in (wq_c, kv_c, wo_c):
        begin(c)

    @pl.loop(0, rows // PB)
    def _(i):
        s = rows_at(i, PB)
        xhat, _ = normalise(x0[s, :])
        nc[s, :] = (xhat * gain_c[...]).astype(BF)

    finish(wq_c)
    q[...] = nn(nc[...], wq_b[...]).astype(BF)
    finish(kv_c)

    @pl.loop(0, rows // PB)
    def _(g):
        s = rows_at(g, PB)
        at = [rows_at(idx[g * NB + n], PB) for n in range(NB)]
        lane = lax.broadcasted_iota(jnp.int32, (1, PB), 1)
        live = jnp.concatenate([(lane < lens[g * NB + n]).astype(jnp.int32) for n in range(NB)], axis=1) > 0
        for p in range(tp):
            for h in range(w // HD):
                c = p * w + h * HD
                k0 = p * 2 * w + h * HD
                k = jnp.concatenate([kv_b[a, k0 : k0 + HD] for a in at], axis=0)
                v = jnp.concatenate([kv_b[a, k0 + w : k0 + w + HD] for a in at], axis=0)
                pr = softmax_parts(jnp.where(live, nt(q[s, c : c + HD], k), NEG), 1)
                o[s, c : c + HD] = nn(pr.astype(BF), v).astype(BF)

    finish(wo_c)
    acc[...] = nn(o[...], wo_b[...])

    @pl.loop(0, rows // PB)
    def _(i):
        s = rows_at(i, PB)
        y = x0[s, :] + acc[s, :] + bias[...]
        x1[s, :] = y
        xhat, _ = normalise(y)
        ns[s, :] = (xhat * gain_s[...]).astype(BF)


def cross_forward(idx, lens, x0, gain_c, gain_s, bias, kv, packs):
    tp = len(packs)
    rows, d = x0.shape
    ext = kv.shape[0]
    return pl.pallas_call(
        functools.partial(cross_forward_body, tp),
        out_shape=(
            shape((rows, d), BF),
            shape((rows, d), BF),
            shape((rows, d), F32),
            shape((rows, d), BF),
            shape((rows, d), BF),
        ),
        in_specs=[SM] * 2 + [VM] * 4 + [ANY] * (1 + tp),
        out_specs=[VM] * 5,
        scratch_shapes=[
            pltpu.VMEM((ext, 2 * d), BF),
            pltpu.VMEM((d, d), BF),
            pltpu.VMEM((d, d), BF),
            pltpu.VMEM((rows, d), F32),
            pltpu.SemaphoreType.DMA((3,)),
        ],
        compiler_params=params(),
        cost_estimate=cost(20),
        name="cross_forward",
    )(idx, lens, x0, gain_c, gain_s, bias, kv, *packs)


def self_forward_body(tp, ns, x1, gain_m, bias, *refs):
    n = tp
    parts = pack_parts(refs[:n], tp, None)
    qkv, o, x2, nm, wqkv_b, wo_b, acc, sems = refs[-8:]
    rows, d = x1.shape
    w = d // tp
    wqkv_c = col_copies(parts, 0, 3 * w, wqkv_b, sems.at[0])
    wo_c = block_copies(parts, 3 * w, w, wo_b, sems.at[1])
    begin(wqkv_c)
    begin(wo_c)
    finish(wqkv_c)
    qkv[...] = nn(ns[...], wqkv_b[...]).astype(BF)

    @pl.loop(0, rows // PB)
    def _(g):
        s = rows_at(g, PB)
        for p in range(tp):
            for h in range(w // HD):
                c = p * w + h * HD
                k0 = p * 3 * w + h * HD
                pr = softmax_parts(nt(qkv[s, k0 : k0 + HD], qkv[s, k0 + w : k0 + w + HD]), 1)
                v = qkv[s, k0 + 2 * w : k0 + 2 * w + HD]
                o[s, c : c + HD] = nn(pr.astype(BF), v).astype(BF)

    finish(wo_c)
    acc[...] = nn(o[...], wo_b[...])

    @pl.loop(0, rows // PB)
    def _(i):
        s = rows_at(i, PB)
        y = x1[s, :] + acc[s, :] + bias[...]
        x2[s, :] = y
        xhat, _ = normalise(y)
        nm[s, :] = (xhat * gain_m[...]).astype(BF)


def self_forward(ns, x1, gain_m, bias, pack, late):
    rows, d = x1.shape
    tp = len(pack)
    return pl.pallas_call(
        functools.partial(self_forward_body, tp),
        out_shape=(
            shape((rows, 3 * d), BF),
            shape((rows, d), BF),
            shape((rows, d), F32),
            shape((rows, d), BF),
        ),
        in_specs=[VM] * 4 + [ANY] * (len(pack) + len(late)),
        out_specs=[VM] * 4,
        scratch_shapes=[
            pltpu.VMEM((d, 3 * d), BF),
            pltpu.VMEM((d, d), BF),
            pltpu.VMEM((rows, d), F32),
            pltpu.SemaphoreType.DMA((2,)),
        ],
        compiler_params=params(),
        cost_estimate=cost(22),
        name="self_forward",
    )(ns, x1, gain_m, bias, *pack, *late)


ROOT = 0.7978845608028654
CUBE = 0.044715


def feed_body(nm, cot, hb, wh0, wh1, wo0, wo1, *refs):
    act, gb, out, gnm, hbg = refs[-5:]
    rows, d = nm.shape
    ff = wh0.shape[1]
    span = min(512, ff)
    for p, (wh, wo) in enumerate(((wh0, wo0), (wh1, wo1))):
        for j in range(ff // span):
            s = slice(j * span, (j + 1) * span)
            x = nn(nm[...], wh[:, s]) + hb[p : p + 1, s]
            ga = nt(cot[...], wo[s, :])
            sq = x * x
            t = jnp.tanh(ROOT * x * (1.0 + CUBE * sq))
            half = 0.5 * (1.0 + t)
            act[p, :, s] = (x * half).astype(BF)
            slope = half + 0.5 * x * (1.0 - t * t) * (ROOT + (3.0 * ROOT * CUBE) * sq)
            g = (ga * slope).astype(BF)
            gb[p, :, s] = g
            hbg[p : p + 1, s] = colsum(g.astype(F32))
    gnm[...] = (nt(gb[0], wh0[...]) + nt(gb[1], wh1[...])).astype(gnm.dtype)
    out[...] = (nn(act[0], wo0[...]) + nn(act[1], wo1[...])).astype(out.dtype)


def feed(nm, cot, hb, wh, wo, kind, late=()):
    rows, d = nm.shape
    ff = wh[0].shape[1]
    return pl.pallas_call(
        feed_body,
        out_shape=(
            shape((2, rows, ff), BF),
            shape((2, rows, ff), BF),
            shape((rows, d), kind),
            shape((rows, d), kind),
            shape((2, ff), F32),
        ),
        in_specs=[VM] * 7 + [ANY] * len(late),
        out_specs=[VM] * 5,
        compiler_params=params(),
        cost_estimate=cost(15),
        name="feed",
    )(nm, cot, hb, *wh, *wo, *late)


def feed_weights_body(sets, *refs):
    lefts, rights, rest = refs[:sets], refs[sets : 2 * sets], refs[2 * sets :]
    out = rest[-1]
    came = rest[0] if len(rest) == 2 else None
    tile = 256

    @pl.loop(0, out.shape[0] // tile)
    def _(i):
        s = rows_at(i, tile)
        y = functools.reduce(jnp.add, [tn(a[0, :, s], c[...]) for a, c in zip(lefts, rights)])
        if came is not None:
            y = y + came[s, :].astype(F32)
        out[s, :] = y.astype(BF)


def feed_weights(p, lefts, rights, came):
    sets = len(lefts)

    def spec(x):
        if x.ndim == 3:
            return pl.BlockSpec((1,) + x.shape[1:], lambda i: (p, 0, 0))
        return pl.BlockSpec(x.shape, lambda i: (0, 0))

    dims = (lefts[0].shape[-1], rights[0].shape[-1])
    ins = list(lefts) + list(rights) + list(came)
    return pl.pallas_call(
        functools.partial(feed_weights_body, sets),
        grid=(1,),
        out_shape=shape(dims, BF),
        in_specs=[spec(x) for x in ins],
        out_specs=pl.BlockSpec(dims, lambda i: (0, 0)),
        compiler_params=params(),
        cost_estimate=cost(6),
        name="feed_weights",
    )(*ins)


def self_backward_body(tp, others, cot, gnm, x2, x1, gain_m, gain_s, qkv, *refs):
    gots, refs = refs[:others], refs[others:]
    n = tp
    parts = pack_parts(refs[:n], tp, None)
    b2, dqkv, g1, b1, vec, wo_b, wqkv_b, g2, gso, gns, sems = refs[-11:]
    rows, d = cot.shape
    w = d // tp
    wqkv_c = col_copies(parts, 0, 3 * w, wqkv_b, sems.at[0])
    wo_c = block_copies(parts, 3 * w, w, wo_b, sems.at[1])
    begin(wo_c)
    begin(wqkv_c)
    vec[...] = jnp.zeros_like(vec)

    @pl.loop(0, rows // PB)
    def _(i):
        s = rows_at(i, PB)
        u = functools.reduce(jnp.add, [r[s, :].astype(F32) for r in gots], gnm[s, :])
        xhat, r = normalise(x2[s, :])
        g3 = cot[s, :].astype(F32)
        y = g3 + norm_back(u, xhat, r, gain_m[...])
        g2[s, :] = y
        b2[s, :] = y.astype(BF)
        vec[0:1, :] += colsum(g3)
        vec[1:2, :] += colsum(u * xhat)
        vec[2:3, :] += colsum(y)

    finish(wo_c)
    gso[...] = nt(b2[...], wo_b[...]).astype(BF)

    @pl.loop(0, rows // PB)
    def _(g):
        s = rows_at(g, PB)
        for p in range(tp):
            for h in range(w // HD):
                c = p * w + h * HD
                k0 = p * 3 * w + h * HD
                k1, k2 = k0 + w, k0 + 2 * w
                q, k, v = qkv[s, k0 : k0 + HD], qkv[s, k1 : k1 + HD], qkv[s, k2 : k2 + HD]
                pr = softmax_parts(nt(k, q), 0)
                do = gso[s, c : c + HD]
                dp = nt(v, do)
                ds = (pr * (dp - jnp.sum(dp * pr, axis=0, keepdims=True))).astype(BF)
                dqkv[s, k0 : k0 + HD] = (tn(ds, k) * SCALE).astype(BF)
                dqkv[s, k1 : k1 + HD] = (nn(ds, q) * SCALE).astype(BF)
                dqkv[s, k2 : k2 + HD] = nn(pr.astype(BF), do).astype(BF)

    finish(wqkv_c)
    gns[...] = nt(dqkv[...], wqkv_b[...])

    @pl.loop(0, rows // PB)
    def _(i):
        s = rows_at(i, PB)
        u = gns[s, :]
        xhat, r = normalise(x1[s, :])
        y = g2[s, :] + norm_back(u, xhat, r, gain_s[...])
        g1[s, :] = y
        b1[s, :] = y.astype(BF)
        vec[3:4, :] += colsum(u * xhat)
        vec[4:5, :] += colsum(y)


def self_backward(cot, gnm, gots, x2, x1, gain_m, gain_s, qkv, pack, after):
    tp = len(pack)
    rows, d = cot.shape
    return pl.pallas_call(
        functools.partial(self_backward_body, tp, len(gots)),
        out_shape=(
            shape((rows, d), BF),
            shape((rows, 3 * d), BF),
            shape((rows, d), F32),
            shape((rows, d), BF),
            shape((8, d), F32),
        ),
        in_specs=[VM] * (7 + len(gots)) + [ANY] * (len(pack) + len(after)),
        out_specs=[VM] * 5,
        scratch_shapes=[
            pltpu.VMEM((d, d), BF),
            pltpu.VMEM((d, 3 * d), BF),
            pltpu.VMEM((rows, d), F32),
            pltpu.VMEM((rows, d), BF),
            pltpu.VMEM((rows, d), F32),
            pltpu.SemaphoreType.DMA((2,)),
        ],
        compiler_params=params(),
        cost_estimate=cost(27),
        name="self_backward",
    )(cot, gnm, x2, x1, gain_m, gain_s, qkv, *gots, *pack, *after)


def cross_backward_body(tp, idx, lens, b1, g1, x0, gain_c, q, kv, *refs):
    n = tp
    parts = pack_parts(refs[:n], tp, None)
    dq, dkv, g0, emb, vec, wo_b, wq_b, gco, gnc, dacc, kv_b, sems = refs[-12:]
    rows, d = b1.shape
    w = d // tp
    wq_c = col_copies(parts, 0, w, wq_b, sems.at[0])
    wo_c = block_copies(parts, w, w, wo_b, sems.at[1])
    kv_c = [pltpu.make_async_copy(kv, kv_b, sems.at[2])]
    begin(wo_c)
    begin(kv_c)
    begin(wq_c)
    vec[...] = jnp.zeros_like(vec)
    emb[...] = jnp.zeros_like(emb)
    ext = kv.shape[0]

    @pl.loop(0, ext // PB)
    def _(i):
        dacc[rows_at(i, PB), :] = jnp.zeros((PB, dacc.shape[1]), F32)

    finish(wo_c)
    gco[...] = nt(b1[...], wo_b[...]).astype(BF)
    finish(kv_c)

    @pl.loop(0, rows // PB)
    def _(g):
        s = rows_at(g, PB)
        at = [rows_at(idx[g * NB + n], PB) for n in range(NB)]
        row = lax.broadcasted_iota(jnp.int32, (PB, PB), 0)
        live = jnp.concatenate([(row < lens[g * NB + n]).astype(jnp.int32) for n in range(NB)], axis=0) > 0
        for p in range(tp):
            for h in range(w // HD):
                c = p * w + h * HD
                k0 = p * 2 * w + h * HD
                v0 = k0 + w
                k = jnp.concatenate([kv_b[a, k0 : k0 + HD] for a in at], axis=0)
                v = jnp.concatenate([kv_b[a, v0 : v0 + HD] for a in at], axis=0)
                qh = q[s, c : c + HD]
                do = gco[s, c : c + HD]
                pr = softmax_parts(jnp.where(live, nt(k, qh), NEG), 0)
                dp = nt(v, do)
                ds = (pr * (dp - jnp.sum(dp * pr, axis=0, keepdims=True))).astype(BF)
                dq[s, c : c + HD] = (tn(ds, k) * SCALE).astype(BF)
                dk = nn(ds, qh)
                dv = nn(pr.astype(BF), do)
                for j, a in enumerate(at):
                    dacc[a, k0 : k0 + HD] += dk[j * PB : (j + 1) * PB, :]
                    dacc[a, v0 : v0 + HD] += dv[j * PB : (j + 1) * PB, :]

    @pl.loop(0, ext // PB)
    def _(i):
        s = rows_at(i, PB)
        for p in range(tp):
            k0 = p * 2 * w
            dkv[s, k0 : k0 + w] = (dacc[s, k0 : k0 + w] * SCALE).astype(BF)
            dkv[s, k0 + w : k0 + 2 * w] = dacc[s, k0 + w : k0 + 2 * w].astype(BF)

    finish(wq_c)
    gnc[...] = nt(dq[...], wq_b[...])

    @pl.loop(0, rows // PB)
    def _(i):
        s = rows_at(i, PB)
        u = gnc[s, :]
        xhat, r = normalise(x0[s, :])
        y = g1[s, :] + norm_back(u, xhat, r, gain_c[...])
        g0[s, :] = y.astype(BF)
        emb[...] += y
        vec[0:1, :] += colsum(u * xhat)


def cross_backward(idx, lens, b1, g1, x0, gain_c, q, kv, pack, after):
    tp = len(pack)
    rows, d = b1.shape
    ext = kv.shape[0]
    return pl.pallas_call(
        functools.partial(cross_backward_body, tp),
        out_shape=(
            shape((rows, d), BF),
            shape((ext, 2 * d), BF),
            shape((rows, d), BF),
            shape((PB, d), F32),
            shape((8, d), F32),
        ),
        in_specs=[SM] * 2 + [VM] * 5 + [ANY] * (1 + len(pack) + len(after)),
        out_specs=[VM] * 5,
        scratch_shapes=[
            pltpu.VMEM((d, d), BF),
            pltpu.VMEM((d, d), BF),
            pltpu.VMEM((rows, d), BF),
            pltpu.VMEM((rows, d), F32),
            pltpu.VMEM((ext, 2 * d), F32),
            pltpu.VMEM((ext, 2 * d), BF),
            pltpu.SemaphoreType.DMA((3,)),
        ],
        compiler_params=params(),
        cost_estimate=cost(35),
        name="cross_backward",
    )(idx, lens, b1, g1, x0, gain_c, q, kv, *pack, *after)


def tn_into(out, lo, left, right, extra):
    n = left.shape[1]
    tile = min(256, n)
    for k in range(n // tile):
        r = slice(lo + k * tile, lo + (k + 1) * tile)
        y = tn(left[:, k * tile : (k + 1) * tile], right[...])
        if extra is not None:
            y = y + extra[r, :].astype(F32)
        out[r, :] = y.astype(BF)


def two(ref):
    n = ref.shape[0] // 2
    return ref.at[pl.ds(0, n), :], ref.at[pl.ds(n, n), :]


def self_weights_body(ns, dqkv, o, b2, *refs):
    ea, eb = two(refs[0]) if len(refs) > 1 else (None, None)
    a, b = two(refs[-1])
    w = o.shape[1]
    tn_into(a, 0, dqkv.at[:, pl.ds(0, w)], ns, ea)
    tn_into(b, 0, dqkv.at[:, pl.ds(w, 2 * w)], ns, eb)
    tn_into(a, w, o, b2, ea)


def column_block(x, p, n):
    return pl.BlockSpec((x.shape[0], n), lambda i: (0, p))


def whole_block(x):
    return pl.BlockSpec(x.shape, lambda i: (0, 0))


def self_weights(p, w, ns, dqkv, o, b2, came, late):
    d = ns.shape[1]
    return pl.pallas_call(
        lambda *refs: self_weights_body(*refs[: 4 + len(came)], refs[-1]),
        grid=(1,),
        out_shape=shape((4 * w, d), BF),
        in_specs=[whole_block(ns), column_block(dqkv, p, 3 * w), column_block(o, p, w), whole_block(b2)]
        + [whole_block(x) for x in came]
        + [ANY] * len(late),
        out_specs=pl.BlockSpec((4 * w, d), lambda i: (0, 0)),
        compiler_params=params(),
        cost_estimate=cost(4),
        name="self_weights",
    )(ns, dqkv, o, b2, *came, *late)


def cross_weights_body(nc, dq, o, b1, dkv, points, came0, came1, *refs):
    ext_b, sem = refs[-2:]
    came, outs = (refs[:1], refs[1:-2]) if len(refs) == 5 else ((), refs[:-2])
    ea, eb = two(came[0]) if came else (None, None)
    a, b = outs if len(outs) == 2 else two(outs[0])
    half = ext_b.shape[0] // 2
    copies = row_copies([came0, came1], ext_b, sem) + [
        pltpu.make_async_copy(points.at[pl.ds(0, half), :], ext_b.at[pl.ds(half, half), :], sem)
    ]
    begin(copies)
    w = o.shape[1]
    tn_into(a, 0, dq, nc, ea)
    tn_into(a, w, o, b1, ea)
    finish(copies)
    tn_into(b, 0, dkv, ext_b, eb)


def cross_weights(p, w, nc, dq, o, b1, dkv, points, came_points, came, late):
    d = nc.shape[1]
    rows = [4 * w] if p % 2 else [2 * w] * 2
    n, k = 8 + len(came), 2 + len(rows)
    return pl.pallas_call(
        lambda *refs: cross_weights_body(*refs[:n], *refs[-k:]),
        grid=(1,),
        out_shape=[shape((r, d), BF) for r in rows],
        in_specs=[
            whole_block(nc),
            column_block(dq, p, w),
            column_block(o, p, w),
            whole_block(b1),
            column_block(dkv, p, 2 * w),
        ]
        + [ANY] * 3
        + [whole_block(x) for x in came]
        + [ANY] * len(late),
        out_specs=[pl.BlockSpec((r, d), lambda i: (0, 0)) for r in rows],
        scratch_shapes=[pltpu.VMEM((dkv.shape[0], d), BF), pltpu.SemaphoreType.DMA],
        compiler_params=params(),
        cost_estimate=cost(8),
        name="cross_weights",
    )(nc, dq, o, b1, dkv, points, *came_points, *came, *late)


def flip(x, axis, bit):
    n = lax.axis_size(axis)
    return lax.ppermute(x, axis, [(i, i ^ (1 << bit)) for i in range(n)])


def bits_of(axis):
    return (lax.axis_size(axis) - 1).bit_length()


def bit_at(axis, bit):
    return (lax.axis_index(axis) >> bit) & 1


def gather_pieces(own, *late):
    have = {0: own}
    for bit in reversed(range(bits_of("tp"))):
        for p in list(have):
            x = have[p] if bit > 0 or p == 0 or not late else after(have[p], *late)
            have[p | (1 << bit)] = flip(x, "tp", bit)
    return [have[p] for p in range(len(have))]


def in_order(pieces):
    x = jnp.stack(pieces)
    for bit in range(bits_of("tp")):
        y = x.reshape((-1, 2, 1 << bit) + x.shape[1:])
        x = jnp.where(bit_at("tp", bit) == 1, y[:, ::-1], y).reshape(x.shape)
    return x


def add(*xs, late=()):
    return after(functools.reduce(jnp.add, [x.astype(F32) for x in xs]).astype(BF), *late)


def after(x, *deps):
    ok = True
    for v in deps:
        first = v[(0,) * v.ndim]
        ok = jnp.logical_and(ok, first == first)
    return jnp.where(ok, x, jnp.zeros_like(x))


def over_tp(have, bit, late=()):
    out = {p: v for p, v in have.items() if not p >> bit & 1}
    for p, v in have.items():
        if p >> bit & 1:
            q = p ^ (1 << bit)
            out[q] = add(out[q], flip(v, "tp", bit), late=late)
    return out


def over_y(have, late=()):
    for k in reversed(range(1, bits_of("tp"))):
        have = over_tp(have, k, late)
    return have


def flip_x(v):
    return lax.ppermute(v, "x", [(0, 1), (1, 0)])


def over_x(v, late=()):
    nz = lax.axis_size("z")
    v = v.reshape((nz, 2, v.shape[0] // (2 * nz)) + v.shape[1:])
    x = lax.axis_index("x")
    keep = lax.dynamic_index_in_dim(v, x, 1, keepdims=False)
    return add(keep, flip_x(lax.dynamic_index_in_dim(v, 1 - x, 1, keepdims=False)), late=late)


def sum_z(v):
    return lax.psum(v, "z")


def to_groups(x, per):
    lat, groups, w = x.shape
    n = groups // per
    tp = lax.axis_size("tp")
    y = jnp.transpose(x.reshape(lat, n, per, w), (1, 2, 0, 3))
    y = lax.all_to_all(y, ("z", "x", "tp"), split_axis=0, concat_axis=0, tiled=True)
    y = jnp.transpose(y.reshape(n // tp, tp, per, lat, w), (2, 0, 3, 1, 4))
    return y.reshape(per * lat * (n // tp), tp * w)


def from_groups(x, per):
    tp = lax.axis_size("tp")
    n = lax.axis_size(GRP) * tp
    rows, d = x.shape
    lat, w = rows // per // (n // tp), d // tp
    y = jnp.transpose(x.reshape(per, n // tp, lat, tp, w), (1, 3, 0, 2, 4)).reshape(n, per, lat, w)
    y = lax.all_to_all(y, ("z", "x", "tp"), split_axis=0, concat_axis=0, tiled=True)
    return jnp.transpose(y, (2, 0, 1, 3)).reshape(lat, n * per, w)


def per_device(
    latents,
    skip_latents,
    points,
    neighbours,
    block_lengths,
    latent_embed,
    gain_cross,
    query_cross,
    key_cross,
    value_cross,
    output_cross,
    bias_cross,
    gain_self,
    query_self,
    key_self,
    value_self,
    output_self,
    bias_self,
    gain_mlp,
    hidden_weight,
    hidden_bias,
    output_weight,
    output_bias,
    cotangent,
):
    tp, grp = lax.axis_size("tp"), lax.axis_size(GRP)
    t, i = lax.axis_index("tp"), lax.axis_index(GRP)
    d = query_cross.shape[0]
    w = latent_embed.shape[1]
    lat_rows = latent_embed.shape[0]
    ff = hidden_weight.shape[1]
    groups_here = neighbours.shape[0]
    groups = groups_here * grp
    per = groups_here // tp
    blocks_here = points.shape[0] // PB
    all_blocks = blocks_here * grp
    half_rows = points.shape[0] // 2

    kv_own = packed([[key_cross, value_cross]])[0]
    share = half_rows // 2
    core = bit_at("tp", 0)
    sent = part_of(points, (2 + core).astype(jnp.int32).reshape(1), share, [kv_own])
    first = lax.ppermute(sent, GRP, [(k, (k + 1) % grp) for k in range(grp)])
    came_points = [first, flip(first, "tp", 0)]
    near = lax.dynamic_slice_in_dim(neighbours, t * per, per, 0).reshape(per * NB)
    block = (near - (i * blocks_here - blocks_here // 2)) % all_blocks
    share_blocks = share // PB
    moved = ((block // share_blocks) ^ core) * share_blocks + block % share_blocks
    idx = jnp.where(block < blocks_here // 2, moved, block).astype(jnp.int32)
    lens = block_lengths[near]

    kv_pack = gather_pieces(kv_own)
    qo_own = packed([[query_cross, output_cross]], [kv_own])[0]
    qo_pack = gather_pieces(qo_own)

    small = jnp.concatenate(
        [
            after(latent_embed, kv_own),
            bias_cross[None],
            bias_self[None],
            output_bias[None],
            hidden_bias.reshape(ff // w, w),
        ]
    )
    small_pieces = gather_pieces(small)
    small_all = in_order(small_pieces)
    by_rows = jnp.transpose(small_all, (1, 0, 2)).reshape(small.shape[0], d)
    embed = by_rows[:lat_rows]
    bias_c, bias_s, bias_o = (by_rows[lat_rows + k : lat_rows + k + 1] for k in range(3))
    hid_bias = jnp.stack([piece[lat_rows + 3 :].reshape(ff) for piece in small_pieces[:2]])

    whid = [hidden_weight, flip(hidden_weight, "tp", 0)]
    wout = [output_weight, flip(output_weight, "tp", 0)]

    gain_c, gain_s, gain_m = gain_cross[None], gain_self[None], gain_mlp[None]
    rows = per * lat_rows
    x0 = (
        to_groups(after(latents, kv_own), per).astype(F32).reshape(per, lat_rows, d) + embed[None]
    ).reshape(rows, d)
    self_own = packed([[query_self, key_self, value_self, output_self]], [qo_pack[2]])[0]
    kv = keys_values(points, came_points, kv_pack, [x0, self_own])
    q, oc, x1, nc, ns = cross_forward(idx, lens, x0, gain_c, gain_s, bias_c, kv, qo_pack)
    self_pack = gather_pieces(self_own, x1)
    cot = after(to_groups(after(cotangent, x0), per), x1)
    qkv, os, x2, nm = self_forward(ns, x1, gain_m, bias_s, self_pack, [cot])

    steps = list(range(2, tp, 2))

    def swap(x, k):
        return lax.ppermute(x, "tp", [(j, j ^ k) for j in range(tp)])

    other_cot = [swap(cot, k) for k in steps]
    other_nm = [swap(nm, k) for k in steps]
    acts, gbs, hbgs = [], [], []
    act, gb, out, gnm, hbg = feed(nm, cot, hid_bias, whid, wout, F32, other_cot)
    acts.append(act)
    gbs.append(gb)
    hbgs.append(hbg)
    back_out, back_gnm = [], []
    for k, n_k, c_k in zip(steps, other_nm, other_cot):
        act, gb, o_k, g_k, hbg = feed(n_k, c_k, hid_bias, whid, wout, BF)
        acts.append(act)
        gbs.append(gb)
        hbgs.append(hbg)
        back_gnm.append(swap(g_k, k))
        back_out.append(o_k)
    nms, cots = [nm] + other_nm, [cot] + other_cot
    sent_o = feed_weights(1, acts, cots, [])
    sent_h = feed_weights(1, gbs, nms, [])
    own_o = feed_weights(0, acts, cots, [flip(sent_o, "tp", 0)])
    own_h = feed_weights(0, gbs, nms, [flip(sent_h, "tp", 0)])

    b2, dqkv, g1, b1, vec_s = self_backward(
        cot, gnm, back_gnm, x2, x1, gain_m, gain_s, qkv, self_pack, [own_o, own_h]
    )

    def pieces(weights, waits):
        got, out, late = {}, {}, []
        for p in reversed(range(1, tp, 2)):
            x = weights(p, [], waits(p, late) + late)
            late = [x]
            got[p - 1] = flip(x, "tp", 0)
        for p in reversed(range(0, tp, 2)):
            out[p] = weights(p, [got[p]], waits(p, late) + late)
            late = [out[p][0] if isinstance(out[p], (list, tuple)) else out[p]]
        return out

    x3 = x2 + out + bias_o
    for k, o_k in zip(steps, back_out):
        x3 = x3 + swap(after(o_k, own_h), k).astype(F32)
    leaving = after(x3.astype(BF), b2)
    sum_o, sum_h = over_x(own_o, [b2]), over_x(own_h, [b2])
    sum_f = jnp.concatenate([sum_o, sum_h], axis=1)
    selfs = pieces(
        lambda p, came, late: self_weights(p, w, ns, dqkv, os, b2, came, late),
        lambda p, late: [sum_f, leaving] if p == tp - 1 else [],
    )
    last = selfs[0]
    feed_z = sum_z(sum_f)
    restored = from_groups(after(leaving, selfs[tp - 2]), per)

    dq, dkv, g0, emb, vec_c = cross_backward(
        idx, lens, b1, g1, x0, gain_c, q, kv, qo_pack, [leaving, *selfs.values()]
    )
    stage = {}

    def norms_and_small(late):
        block_out = after(restored, *late).astype(F32) + skip_latents.astype(F32)
        squares = jnp.sum(jnp.square(block_out), axis=(0, 2))
        by_share = jnp.transpose(
            jnp.concatenate([emb, vec_s[:5], vec_c[:1]]).reshape(lat_rows + 6, tp, w), (1, 0, 2)
        )
        hb_all = functools.reduce(jnp.add, hbgs).reshape(2, ff // w, w)
        owner = lax.broadcasted_iota(jnp.int32, (tp, 1, 1), 0)
        hb_share = jnp.where(owner == t, hb_all[0][None], 0.0) + jnp.where(
            owner == (t ^ 1), hb_all[1][None], 0.0
        )
        sq_rows = jnp.pad(squares, (0, norm_rows * w - groups)).reshape(1, norm_rows, w)
        x = jnp.concatenate(
            [by_share, hb_share, jnp.broadcast_to(sq_rows, (tp, norm_rows, w))], axis=1
        )
        x = jnp.pad(x, ((0, 0), (0, -x.shape[1] % 8), (0, 0)))
        for bit in reversed(range(bits_of("tp"))):
            n = x.shape[0] // 2
            mine = bit_at("tp", bit)
            keep = lax.dynamic_slice_in_dim(x, mine * n, n, 0)
            x = keep + flip(lax.dynamic_slice_in_dim(x, (1 - mine) * n, n, 0), "tp", bit)
        x = x[0].reshape(-1)
        places_rows = 2 * lax.axis_size("z") * 8
        rows_all = -(-x.shape[0] // (d * places_rows)) * places_rows
        return block_out, jnp.pad(x, (0, rows_all * d - x.shape[0])).reshape(rows_all, d).astype(BF)

    norm_rows = -(-groups // w)

    def waits(p, late):
        if p == tp - 1:
            stage["self"] = over_y(selfs, [emb])[0]
            return [stage["self"], restored]
        if p == tp - 3:
            return []
        if p == tp - 2:
            n = stage["self"].shape[0] // 2
            stage["self"] = [over_x(stage["self"][:n], late), over_x(stage["self"][n:], late)]
            return stage["self"] + [feed_z]
        if p == 0:
            stage["self"] = after(jnp.concatenate(stage["self"], axis=1), *late)
            stage["out"], stage["small"] = norms_and_small(late)
            return [stage["small"]]
        return []

    def cross_piece(p, came, late):
        x = cross_weights(p, w, nc, dq, oc, b1, dkv, points, came_points, came, late)
        return x[0] if p % 2 else x

    cross = pieces(cross_piece, waits)
    late = [cross[0][0]]
    self_z = sum_z(stage["self"])
    cross_a = over_y({p: v[0] for p, v in cross.items()})[0]
    cross_b = over_y({p: over_x(v[1], [feed_z]) for p, v in cross.items()})[0]
    little = over_x(stage["small"])
    cross_z = jnp.concatenate([over_x(cross_a, [self_z]), cross_b, little], axis=1)
    feed_z, self_z = after(feed_z, cross_z), after(self_z, cross_z)
    self_x, feed_x = flip_x(self_z), flip_x(feed_z)
    returned = from_groups(after(g0, cross_z), per)
    cross_z = after(sum_z(cross_z), self_x)
    cross_x = flip_x(cross_z)
    n = little.shape[1]
    low = lax.axis_index("x") == 0
    own_n, other_n = cross_z[:, -n:], cross_x[:, -n:]
    total = jnp.where(low, jnp.stack([own_n, other_n], 1), jnp.stack([other_n, own_n], 1))
    total = total.astype(F32).reshape(-1)
    total = total[: total.shape[0] // w * w].reshape(-1, w)
    places = lax.axis_index("x").astype(jnp.int32).reshape(1)
    output_weight_grad, hidden_weight_grad = final_feed(places, feed_z, feed_x)
    query_self_grad, key_self_grad, value_self_grad, output_self_grad = final(
        places, w, self_z, self_x
    )
    block_out = stage["out"]
    latents_grad = returned.astype(F32)

    query_cross_grad, key_cross_grad, value_cross_grad, output_cross_grad = final(
        places, w, cross_z, cross_x, [output_weight_grad, hidden_weight_grad, output_self_grad]
    )
    embed_grad = total[:lat_rows]
    (
        output_bias_grad,
        gain_mlp_grad,
        bias_self_grad,
        gain_self_grad,
        bias_cross_grad,
        gain_cross_grad,
    ) = (total[lat_rows + k] for k in range(6))
    at = lat_rows + 6
    hidden_bias_grad = total[at : at + ff // w].reshape(ff)
    at += ff // w
    square_sums = total[at : at + norm_rows].reshape(norm_rows * w)[:groups]
    group_norms = jnp.sqrt(square_sums / (lat_rows * d))

    return (
        block_out,
        group_norms,
        latents_grad,
        embed_grad,
        gain_cross_grad,
        query_cross_grad,
        key_cross_grad,
        value_cross_grad,
        output_cross_grad,
        bias_cross_grad,
        gain_self_grad,
        query_self_grad,
        key_self_grad,
        value_self_grad,
        output_self_grad,
        bias_self_grad,
        gain_mlp_grad,
        hidden_weight_grad,
        hidden_bias_grad,
        output_weight_grad,
        output_bias_grad,
    )


def solution(mesh):
    grp, tp = mesh.shape["grp"], mesh.shape["tp"]
    own = jax.sharding.Mesh(mesh.devices.reshape(grp // 2, 2, tp), GRP + ("tp",))
    lay = P(GRP, None, "tp")
    cols, rows, part = P(None, "tp"), P("tp", None), P("tp")
    attn = (P(), cols, cols, cols, rows, part)
    return jax.shard_map(
        per_device,
        mesh=own,
        in_specs=(lay, lay, P(GRP, None), P(GRP, None), P(), cols)
        + attn
        + attn
        + (P(), cols, part, rows, part, lay),
        out_specs=(lay, P(), lay, cols)
        + (part, cols, cols, cols, rows, part)
        + (part, cols, cols, cols, rows, part)
        + (part, cols, part, rows, part),
        check_vma=False,
    )
```

time: 768 us -> 615 us (0.80)
  waiting for transfers between devices: 359 us -> 178 us
  between operations: 1.96 us -> 32.1 us
  starting transfers between devices: 78.2 us -> 55.2 us
  local copies, waits for them, and re-layouts: 47.7 us -> 59.7 us
  Pallas kernels: 240 us -> 248 us
    ppermute x58 -> x26, waiting for transfers between devices: 306 us -> 34.4 us  [flip(): return lax.ppermute(x, axis, [(i, i ^ 1 << bit) for i in range(n)])]
    psum x0 -> x3, waiting for transfers between devices: none -> 64.8 us  [sum_z(): return lax.psum(v, 'z')]
    ppermute x1 -> x12, waiting for transfers between devices: 16.7 us -> 63.3 us  [the longest x11 48.1 us: flip_x(): return lax.ppermute(v, 'x', [(0, 1), (1, 0)])]
    ppermute x58 -> x26, starting transfers between devices: 50.3 us -> 15.5 us  [flip(): return lax.ppermute(x, axis, [(i, i ^ 1 << bit) for i in range(n)])]
    pallas_call x6 -> x20, Pallas kernels: 81.6 us -> 112 us  [the longest x4 34.4 us: cross_weights(): pl.pallas_call(lambda *refs: cross_weights_body(*refs[:n], *refs[-k:]), g...]
    ppermute x4, waiting for transfers between devices: 32.3 us -> 7.92 us  [swap(): return lax.ppermute(x, 'tp', [(j, j ^ k) for j in range(tp)])]
    select_n x8 -> x21, other arithmetic: 5.8 us -> 25.7 us  [the longest x20 25.6 us: after(): return jnp.where(ok, x, jnp.zeros_like(x))]
    convert_element_type x22 -> x4, other arithmetic: 22 us -> 2.81 us  [the longest x3 2.55 us: add(): functools.reduce(jnp.add, [x.astype(F32) for x in xs]).astype(BF)]
  transfers between devices with their start and end apart: 67 -> 49, of which waited for: 28 -> 18; matrix products, arithmetic and copies ran while one was open for 10% -> 12% of each run, Pallas kernels for 18% -> 36%
where the time goes in v2:
time: 615 us; the launch traced here: 609 us
  Pallas kernels  248 us (40%)
  waiting for transfers between devices  178 us (29%)
  local copies, waits for them, and re-layouts  59.7 us (10%)
  starting transfers between devices  55.2 us (9%)
  other arithmetic  35.7 us (6%)
  between operations  32.1 us (5%)
    psum x3, waiting for transfers between devices, sum_z(): return lax.psum(v, 'z')  64.8 us
    ppermute x11, waiting for transfers between devices, flip_x(): return lax.ppermute(v, 'x', [(0, 1), (1, 0)])  48.1 us
    pallas_call x4, Pallas kernels, cross_weights(): pl.pallas_call(lambda *refs: cross_weights_body(*refs[:n], *refs[-k:]), g...  34.4 us
    ppermute x26, waiting for transfers between devices, flip(): return lax.ppermute(x, axis, [(i, i ^ 1 << bit) for i in range(n)])  34.4 us
    pallas_call x1, Pallas kernels, cross_backward(): pl.pallas_call(functools.partial(cross_backward_body, tp), out_shape=(sha...  32.7 us
    pallas_call x2, Pallas kernels, feed(): pl.pallas_call(feed_body, out_shape=(shape((2, rows, ff), BF), shape((2,...  31.1 us
    pallas_call x4, Pallas kernels, feed_weights(): pl.pallas_call(functools.partial(feed_weights_body, sets), grid=(1,), out...  27.3 us
    select_n x20, other arithmetic, after(): return jnp.where(ok, x, jnp.zeros_like(x))  25.6 us
  transfers between devices with their start and end apart: 49, of which 18 were waited for; matrix products, arithmetic and copies ran while one was open for 12% of the time, Pallas kernels for 36%

profile of v2, /device:TPU:0, one launch (start us, length us, event | category | flops | bytes accessed | tf_op | source)
XLA Modules:
  0.0 608.8 jit_solution(17693592676455770536)
XLA Ops:
  17.8 5.0 all-to-all-start
  30.9 20.1 %collective-permute-done.1 = f32[135,256]{1,0:T(8,128)S(1)} collective-permute-done((f32[135,256]{1,0:T(8,128)S(1)}, f32[135,256]{1,0:T(8,128)S(1)}, u32[]{:S(2)}, u32[]{:S(2)}) %collective-permute-start.1) | collective-permute-done | bytes 138272 | tf_op jit(solution)/shard_map/ppermute | solution.py:793
  52.6 15.1 %collective-permute-done.3.came0.refs_6_ = bf16[512,1024]{1,0:T(8,128)(2,1)} collective-permute-done((bf16[512,1024]{1,0:T(8,128)(2,1)}, bf16[512,1024]{1,0:T(8,128)(2,1)}, u32[]{:S(2)}, u32[]{:S(2)}) %collective-permute-start.3) | collective-permute-done | bytes 1048608 | tf_op jit(solution)/shard_map/ppermute | solution.py:927
  90.2 5.6 all-to-all-start.1
  96.4 13.7 %keys_values.1.kv = bf16[2048,2048]{1,0:T(8,128)(2,1)} custom-call(bf16[2048,1024]{1,0:T(8,128)(2,1)} %refs_5_.7, bf16[512,1024]{1,0:T(8,128)(2,1)} %collective-permute-done.3.came0.refs_6_, bf16[512,1024]{1,0:T(8,128)(2,1)} %collective-permute-done.4.came1.refs_7_, bf16[1024,512]{1,0:T(8,128)(2,1)} %packed.3.refs_0_.refs_2_, ...), custom_call_target="tpu_custom_call" | custom-call | flops 15399999488 | bytes 14000000 | tf_op jit(solution)/shard_map/keys_values/pallas_call | solution.py:272
  111.1 22.3 %cross_forward.1 = (bf16[512,1024]{1,0:T(8,128)(2,1)}, bf16[512,1024]{1,0:T(8,128)(2,1)}, f32[512,1024]{1,0:T(8,128)}, bf16[512,1024]{1,0:T(8,128)(2,1)}, bf16[512,1024]{1,0:T(8,128)(2,1)}) custom-call(s32[16]{0:T(128)} %compare_select_fusion.1.idx, s32[16]{0:T(128)} %gather_fusion, f32[512,1024]{1,0:T(8,128)} %copy-done.20, f32[1,1024]{1,0:T(1,128)} %bitcast.223, ...), custom_call_target="tpu_custom_call" | custom-call | flops 22000001024 | bytes 20000000 | tf_op jit(solution)/shard_map/cross_forward/pallas_call | solution.py:341
  145.6 23.9 %self_forward.1 = (bf16[512,3072]{1,0:T(8,128)(2,1)}, bf16[512,1024]{1,0:T(8,128)(2,1)}, f32[512,1024]{1,0:T(8,128)}, bf16[512,1024]{1,0:T(8,128)(2,1)}) custom-call(bf16[512,1024]{1,0:T(8,128)(2,1)} %get-tuple-element.66.ns.refs_0_, f32[512,1024]{1,0:T(8,128)} %get-tuple-element.65.x1, f32[1,1024]{1,0:T(1,128)} %bitcast.221, f32[1,1024]{1,0:T(1,128)} %bitcast.209, ...), custom_call_target="tpu_custom_call" | custom-call | flops 24199999488 | bytes 22000000 | tf_op jit(solution)/shard_map/self_forward/pallas_call | solution.py:404
  171.5 15.6 %feed.2 = (bf16[2,512,1024]{2,1,0:T(8,128)(2,1)}, bf16[2,512,1024]{2,1,0:T(8,128)(2,1)}, f32[512,1024]{1,0:T(8,128)}, f32[512,1024]{1,0:T(8,128)}, f32[2,1024]{1,0:T(2,128)}) custom-call(bf16[512,1024]{1,0:T(8,128)(2,1)} %get-tuple-element.67.nm.refs_2_, bf16[512,1024]{1,0:T(8,128)(2,1)} %bitcast.190, f32[2,1024]{1,0:T(2,128)} %pad_maximum_fusion.4.hb, ...), custom_call_target="tpu_custom_call" | custom-call | flops 16499999744 | bytes 15000000 | tf_op jit(solution)/shard_map/feed/pallas_call | solution.py:455
  187.1 7.8 %collective-permute-done.17.nm.refs_3_ = bf16[512,1024]{1,0:T(8,128)(2,1)S(1)} collective-permute-done((bf16[512,1024]{1,0:T(8,128)(2,1)}, bf16[512,1024]{1,0:T(8,128)(2,1)S(1)}, u32[]{:S(2)}, u32[]{:S(2)}) %collective-permute-start.17) | collective-permute-done | bytes 1048608 | tf_op jit(solution)/shard_map/ppermute | solution.py:974
  195.9 15.5 %feed.3 = (bf16[2,512,1024]{2,1,0:T(8,128)(2,1)}, bf16[2,512,1024]{2,1,0:T(8,128)(2,1)}, bf16[512,1024]{1,0:T(8,128)(2,1)}, bf16[512,1024]{1,0:T(8,128)(2,1)}, f32[2,1024]{1,0:T(2,128)}) custom-call(bf16[512,1024]{1,0:T(8,128)(2,1)} %copy-done.51, bf16[512,1024]{1,0:T(8,128)(2,1)} %copy-done.50, f32[2,1024]{1,0:T(2,128)} %pad_maximum_fusion.4.hb, ...), custom_call_target="tpu_custom_call" | custom-call | flops 16499999744 | bytes 15000000 | tf_op jit(solution)/shard_map/feed/pallas_call | solution.py:455
  211.4 6.5 %feed_weights.4 = bf16[1024,1024]{1,0:T(8,128)(2,1)} custom-call(bf16[2,512,1024]{2,1,0:T(8,128)(2,1)} %get-tuple-element.72.refs_0_, bf16[2,512,1024]{2,1,0:T(8,128)(2,1)} %get-tuple-element.73.refs_1_, bf16[512,1024]{1,0:T(8,128)(2,1)} %bitcast.191, bf16[512,1024]{1,0:T(8,128)(2,1)} %copy-done.50), custom_call_target="tpu_custom_call" | custom-call | flops 6600000000 | bytes 6000000 | tf_op jit(solution)/shard_map/feed_weights/pallas_call | solution.py:497
  217.9 6.5 %feed_weights.6 = bf16[1024,1024]{1,0:T(8,128)(2,1)} custom-call(bf16[2,512,1024]{2,1,0:T(8,128)(2,1)} %get-tuple-element.74.refs_0_, bf16[2,512,1024]{2,1,0:T(8,128)(2,1)} %get-tuple-element.75.refs_1_, bf16[512,1024]{1,0:T(8,128)(2,1)} %get-tuple-element.67.nm.refs_2_, bf16[512,1024]{1,0:T(8,128)(2,1)} %copy-done.51), custom_call_target="tpu_custom_call" | custom-call | flops 6600000000 | bytes 6000000 | tf_op jit(solution)/shard_map/feed_weights/pallas_call | solution.py:497
  226.0 7.2 %feed_weights.5.refs_5_ = bf16[1024,1024]{1,0:T(8,128)(2,1)} custom-call(bf16[2,512,1024]{2,1,0:T(8,128)(2,1)} %get-tuple-element.72.refs_0_, bf16[2,512,1024]{2,1,0:T(8,128)(2,1)} %get-tuple-element.73.refs_1_, bf16[512,1024]{1,0:T(8,128)(2,1)} %bitcast.192, bf16[512,1024]{1,0:T(8,128)(2,1)} %copy-done.50, bf16[1024,1024]{1,0:T(8,128)(2,1)} %collective-permute-done.19.refs_4_), custom_call_target="tpu_custom_call" | custom-call | flops 6600000000 | bytes 6000000 | tf_op jit(solution)/shard_map/feed_weights/pallas_call | solution.py:497
  237.3 7.2 %feed_weights.7.refs_6_ = bf16[1024,1024]{1,0:T(8,128)(2,1)} custom-call(bf16[2,512,1024]{2,1,0:T(8,128)(2,1)} %get-tuple-element.74.refs_0_, bf16[2,512,1024]{2,1,0:T(8,128)(2,1)} %get-tuple-element.75.refs_1_, bf16[512,1024]{1,0:T(8,128)(2,1)} %get-tuple-element.67.nm.refs_2_, bf16[512,1024]{1,0:T(8,128)(2,1)} %copy-done.51, bf16[1024,1024]{1,0:T(8,128)(2,1)} %copy-done.48), custom_call_target="tpu_custom_call" | custom-call | flops 6600000000 | bytes 6000000 | tf_op jit(solution)/shard_map/feed_weights/pallas_call | solution.py:497
  251.2 25.2 %self_backward.1 = (bf16[512,1024]{1,0:T(8,128)(2,1)}, bf16[512,3072]{1,0:T(8,128)(2,1)}, f32[512,1024]{1,0:T(8,128)}, bf16[512,1024]{1,0:T(8,128)(2,1)}, f32[8,1024]{1,0:T(8,128)}) custom-call(bf16[512,1024]{1,0:T(8,128)(2,1)} %bitcast.193, f32[512,1024]{1,0:T(8,128)} %get-tuple-element.68.gnm, f32[512,1024]{1,0:T(8,128)} %get-tuple-element.69.x2, ...), custom_call_target="tpu_custom_call" | custom-call | flops 29699999744 | bytes 27000000 | tf_op jit(solution)/shard_map/self_backward/pallas_call | solution.py:573
  299.1 5.2 self_weights.6.refs_5_
  310.4 5.2 all-to-all-start.2
  315.7 5.2 self_weights.7.refs_6_
  320.9 32.7 %cross_backward.1 = (bf16[512,1024]{1,0:T(8,128)(2,1)}, bf16[2048,2048]{1,0:T(8,128)(2,1)}, bf16[512,1024]{1,0:T(8,128)(2,1)}, f32[128,1024]{1,0:T(8,128)}, f32[8,1024]{1,0:T(8,128)}) custom-call(s32[16]{0:T(128)} %compare_select_fusion.1.idx, s32[16]{0:T(128)} %gather_fusion, bf16[512,1024]{1,0:T(8,128)(2,1)} %get-tuple-element.76.b1.refs_3_, ...), custom_call_target="tpu_custom_call" | custom-call | flops 38499999744 | bytes 35000000 | tf_op jit(solution)/shard_map/cross_backward/pallas_call | solution.py:673
  356.0 8.1 %all-to-all-done.2 = bf16[32,4,16,256]{3,1,2,0:T(4,128)(2,1)S(1)} async-done(((bf16[32,4,16,256]{3,1,2,0:T(4,128)(2,1)}), bf16[32,4,16,256]{3,1,2,0:T(4,128)(2,1)S(1)}, u32[]{:S(2)}, u32[]{:S(2)}) %all-to-all-start.2) | async-done | bytes 1048608 | tf_op jit(solution)/shard_map/all_to_all | solution.py:880
  370.5 8.7 %cross_weights.4.refs_8_ = bf16[1024,1024]{1,0:T(8,128)(2,1)} custom-call(bf16[512,1024]{1,0:T(8,128)(2,1)} %get-tuple-element.64.refs_0_, bf16[512,1024]{1,0:T(8,128)(2,1)} %get-tuple-element.84.refs_1_, bf16[512,1024]{1,0:T(8,128)(2,1)} %get-tuple-element.85.refs_2_, bf16[512,1024]{1,0:T(8,128)(2,1)} %get-tuple-element.76.b1.refs_3_, ...), custom_call_target="tpu_custom_call" | custom-call | flops 8800000000 | bytes 8000000 | tf_op jit(solution)/shard_map/cross_weights/pallas_call | solution.py:769
  383.2 8.4 %cross_weights.5.refs_12_ = bf16[1024,1024]{1,0:T(8,128)(2,1)} custom-call(bf16[512,1024]{1,0:T(8,128)(2,1)} %get-tuple-element.64.refs_0_, bf16[512,1024]{1,0:T(8,128)(2,1)} %get-tuple-element.84.refs_1_, bf16[512,1024]{1,0:T(8,128)(2,1)} %get-tuple-element.85.refs_2_, bf16[512,1024]{1,0:T(8,128)(2,1)} %get-tuple-element.76.b1.refs_3_, ...), custom_call_target="tpu_custom_call" | custom-call | flops 8800000000 | bytes 8000000 | tf_op jit(solution)/shard_map/cross_weights/pallas_call | solution.py:769
  396.8 9.5 %collective-permute-done.28 = bf16[4,64,1024]{2,1,0:T(8,128)(2,1)S(1)} collective-permute-done((bf16[4,64,1024]{2,1,0:T(8,128)(2,1)S(1)}, bf16[4,64,1024]{2,1,0:T(8,128)(2,1)S(1)}, u32[]{:S(2)}, u32[]{:S(2)}) %collective-permute-start.28) | collective-permute-done | bytes 524320 | tf_op jit(solution)/shard_map/ppermute | solution.py:849
  408.4 8.6 %cross_weights.6 = (bf16[512,1024]{1,0:T(8,128)(2,1)}, bf16[512,1024]{1,0:T(8,128)(2,1)}) custom-call(bf16[512,1024]{1,0:T(8,128)(2,1)} %get-tuple-element.64.refs_0_, bf16[512,1024]{1,0:T(8,128)(2,1)} %get-tuple-element.84.refs_1_, bf16[512,1024]{1,0:T(8,128)(2,1)} %get-tuple-element.85.refs_2_, bf16[512,1024]{1,0:T(8,128)(2,1)} %get-tuple-element.76.b1.refs_3_, ...), custom_call_target="tpu_custom_call" | custom-call | flops 8800000000 | bytes 8000000 | tf_op jit(solution)/shard_map/cross_weights/pallas_call | solution.py:769
  425.6 4.8 collective-permute-done.31
  437.4 8.7 %cross_weights.7 = (bf16[512,1024]{1,0:T(8,128)(2,1)}, bf16[512,1024]{1,0:T(8,128)(2,1)}) custom-call(bf16[512,1024]{1,0:T(8,128)(2,1)} %get-tuple-element.64.refs_0_, bf16[512,1024]{1,0:T(8,128)(2,1)} %get-tuple-element.84.refs_1_, bf16[512,1024]{1,0:T(8,128)(2,1)} %get-tuple-element.85.refs_2_, bf16[512,1024]{1,0:T(8,128)(2,1)} %get-tuple-element.76.b1.refs_3_, ...), custom_call_target="tpu_custom_call" | custom-call | flops 8800000000 | bytes 8000000 | tf_op jit(solution)/shard_map/cross_weights/pallas_call | solution.py:769
  452.3 5.9 collective-permute-done.33
  464.3 19.5 %all-reduce.9.cloned.1.call-done = bf16[4,128,1024]{2,1,0:T(8,128)(2,1)} async-done(((bf16[4,128,1024]{2,1,0:T(8,128)(2,1)}), bf16[4,128,1024]{2,1,0:T(8,128)(2,1)}) %all-reduce.9.cloned.1.call-update) | async-done | bytes 1048592 | tf_op jit(solution)/shard_map/psum | solution.py:861
  500.7 20.0 %collective-permute-done.35.other = bf16[4,128,1024]{2,1,0:T(8,128)(2,1)} collective-permute-done((bf16[4,128,1024]{2,1,0:T(8,128)(2,1)S(1)}, bf16[4,128,1024]{2,1,0:T(8,128)(2,1)}, u32[]{:S(2)}, u32[]{:S(2)}) %collective-permute-start.35) | collective-permute-done | bytes 1048608 | tf_op jit(solution)/shard_map/ppermute | solution.py:849
  523.2 44.2 %all-reduce.11.cloned.1.call-done = bf16[4,136,1024]{2,1,0:T(8,128)(2,1)} async-done(((bf16[4,136,1024]{2,1,0:T(8,128)(2,1)}), bf16[4,136,1024]{2,1,0:T(8,128)(2,1)}) %all-reduce.11.cloned.1.call-update) | async-done | bytes 1114128 | tf_op jit(solution)/shard_map/psum | solution.py:861
  577.0 6.3 %final_feed.1 = (f32[1024,1024]{1,0:T(8,128)}, f32[1024,1024]{1,0:T(8,128)}) custom-call(s32[1]{0:T(128)} %bitcast.73.places, bf16[4,256,1024]{2,1,0:T(8,128)(2,1)} %broadcast_select_fusion.own, bf16[4,256,1024]{2,1,0:T(8,128)(2,1)} %collective-permute-done.41.other), custom_call_target="tpu_custom_call" | custom-call | flops 6600000000 | bytes 6000000 | tf_op jit(solution)/shard_map/final_feed/pallas_call | solution.py:226
  583.2 12.1 %collective-permute-done.40.other = bf16[4,136,1024]{2,1,0:T(8,128)(2,1)S(1)} collective-permute-done((bf16[4,136,1024]{2,1,0:T(8,128)(2,1)S(1)}, bf16[4,136,1024]{2,1,0:T(8,128)(2,1)S(1)}, u32[]{:S(2)}, u32[]{:S(2)}) %collective-permute-start.40) | collective-permute-done | bytes 1114144 | tf_op jit(solution)/shard_map/ppermute | solution.py:849
  (322 shorter events, 166.4 us)
Async XLA Ops:
  10.4 57.4 %collective-permute-start.6 = (bf16[1024,512]{1,0:T(8,128)(2,1)}, bf16[1024,512]{1,0:T(8,128)(2,1)}, u32[]{:S(2)}, u32[]{:S(2)}) collective-permute-start(bf16[1024,512]{1,0:T(8,128)(2,1)} %packed.3.refs_0_.refs_2_), channel_id=1, source_target_pairs={{0,2},{1,3},{2,0},{3,1},{4,6},{5,7},{6,4},{7,5},{8,10},{9,11},{10,... | collective-permute-start | bytes 3145736 | tf_op jit(solution)/shard_map/ppermute | solution.py:793
  17.8 59.9 %all-to-all-start = ((bf16[32,4,16,256]{3,1,2,0:T(4,128)(2,1)}), bf16[32,4,16,256]{3,1,2,0:T(4,128)(2,1)}, u32[]{:S(2)}, u32[]{:S(2)}) async-start(bf16[32,4,16,256]{3,1,2,0:T(4,128)(2,1)} %bitcast.160), calls=%async_computation | async-start | bytes 2097152 | tf_op jit(solution)/shard_map/all_to_all | solution.py:869
  25.2 42.5 %collective-permute-start.3 = (bf16[512,1024]{1,0:T(8,128)(2,1)}, bf16[512,1024]{1,0:T(8,128)(2,1)}, u32[]{:S(2)}, u32[]{:S(2)}) collective-permute-start(bf16[512,1024]{1,0:T(8,128)(2,1)} %part_of.1), channel_id=1, source_target_pairs={{0,4},{4,8},{8,12},{12,16},{16,20},{20,24},{24,28},{28,0},{1,5},{5... | collective-permute-start | bytes 3145736 | tf_op jit(solution)/shard_map/ppermute | solution.py:927
  28.7 44.7 %collective-permute-start.8 = (bf16[1024,512]{1,0:T(8,128)(2,1)S(1)}, bf16[1024,512]{1,0:T(8,128)(2,1)S(1)}, u32[]{:S(2)}, u32[]{:S(2)}) collective-permute-start(bf16[1024,512]{1,0:T(8,128)(2,1)S(1)} %packed.4.refs_0_), channel_id=1, source_target_pairs={{0,2},{1,3},{2,0},{3,1},{4,6},{5,7},{6,4},{7,5},{8,10},{9,11},{10,... | collective-permute-start | bytes 3145736 | tf_op jit(solution)/shard_map/ppermute | solution.py:793
  51.6 44.2 %collective-permute-start.5 = (bf16[1024,512]{1,0:T(8,128)(2,1)}, bf16[1024,512]{1,0:T(8,128)(2,1)}, u32[]{:S(2)}, u32[]{:S(2)}) collective-permute-start(bf16[1024,512]{1,0:T(8,128)(2,1)} %packed.3.refs_0_.refs_2_), channel_id=1, source_target_pairs={{0,1},{1,0},{2,3},{3,2},{4,5},{5,4},{6,7},{7,6},{8,9},{9,8},{10,11... | collective-permute-start | bytes 3145736 | tf_op jit(solution)/shard_map/ppermute | solution.py:793
  52.4 57.7 %collective-permute-start.9 = (bf16[1024,512]{1,0:T(8,128)(2,1)S(1)}, bf16[1024,512]{1,0:T(8,128)(2,1)}, u32[]{:S(2)}, u32[]{:S(2)}) collective-permute-start(bf16[1024,512]{1,0:T(8,128)(2,1)S(1)} %packed.4.refs_0_), channel_id=1, source_target_pairs={{0,1},{1,0},{2,3},{3,2},{4,5},{5,4},{6,7},{7,6},{8,9},{9,8},{10,11... | collective-permute-start | bytes 3145736 | tf_op jit(solution)/shard_map/ppermute | solution.py:793
  67.7 28.6 %collective-permute-start.4 = (bf16[512,1024]{1,0:T(8,128)(2,1)}, bf16[512,1024]{1,0:T(8,128)(2,1)}, u32[]{:S(2)}, u32[]{:S(2)}) collective-permute-start(bf16[512,1024]{1,0:T(8,128)(2,1)} %collective-permute-done.3.came0.refs_6_), channel_id=1, source_target_pairs={{0,1},{1,0},{2,3},{3,2},{4,5},{5,4},{6,7},{7,6},{8,9},{9,8},{10,11... | collective-permute-start | bytes 3145736 | tf_op jit(solution)/shard_map/ppermute | solution.py:793
  67.7 28.7 %collective-permute-start.7 = (bf16[1024,512]{1,0:T(8,128)(2,1)}, bf16[1024,512]{1,0:T(8,128)(2,1)}, u32[]{:S(2)}, u32[]{:S(2)}) collective-permute-start(bf16[1024,512]{1,0:T(8,128)(2,1)} %collective-permute-done.6.refs_2_), channel_id=1, source_target_pairs={{0,1},{1,0},{2,3},{3,2},{4,5},{5,4},{6,7},{7,6},{8,9},{9,8},{10,11... | collective-permute-start | bytes 3145736 | tf_op jit(solution)/shard_map/ppermute | solution.py:793
  75.9 60.0 %collective-permute-start.12 = (bf16[1024,1024]{1,0:T(8,128)(2,1)S(1)}, bf16[1024,1024]{1,0:T(8,128)(2,1)}, u32[]{:S(2)}, u32[]{:S(2)}) collective-permute-start(bf16[1024,1024]{1,0:T(8,128)(2,1)S(1)} %packed.5.refs_5_.refs_0_.refs_1_), channel_id=1, source_target_pairs={{0,2},{1,3},{2,0},{3,1},{4,6},{5,7},{6,4},{7,5},{8,10},{9,11},{10,... | collective-permute-start | bytes 6291464 | tf_op jit(solution)/shard_map/ppermute | solution.py:793
  90.2 50.8 %all-to-all-start.1 = ((bf16[32,4,16,256]{3,1,2,0:T(4,128)(2,1)}), bf16[32,4,16,256]{3,1,2,0:T(4,128)(2,1)}, u32[]{:S(2)}, u32[]{:S(2)}) async-start(bf16[32,4,16,256]{3,1,2,0:T(4,128)(2,1)} %bitcast.167), calls=%async_computation.1 | async-start | bytes 2097152 | tf_op jit(solution)/shard_map/all_to_all | solution.py:869
  95.9 49.7 %collective-permute-start.11 = (bf16[1024,1024]{1,0:T(8,128)(2,1)S(1)}, bf16[1024,1024]{1,0:T(8,128)(2,1)}, u32[]{:S(2)}, u32[]{:S(2)}) collective-permute-start(bf16[1024,1024]{1,0:T(8,128)(2,1)S(1)} %packed.5.refs_5_.refs_0_.refs_1_), channel_id=1, source_target_pairs={{0,1},{1,0},{2,3},{3,2},{4,5},{5,4},{6,7},{7,6},{8,9},{9,8},{10,11... | collective-permute-start | bytes 6291464 | tf_op jit(solution)/shard_map/ppermute | solution.py:793
  139.3 31.2 %collective-permute-start.14 = (bf16[1024,1024]{1,0:T(8,128)(2,1)}, bf16[1024,1024]{1,0:T(8,128)(2,1)}, u32[]{:S(2)}, u32[]{:S(2)}) collective-permute-start(bf16[1024,1024]{1,0:T(8,128)(2,1)} %wh0.3), channel_id=1, source_target_pairs={{0,1},{1,0},{2,3},{3,2},{4,5},{5,4},{6,7},{7,6},{8,9},{9,8},{10,11... | collective-permute-start | bytes 6291464 | tf_op jit(solution)/shard_map/ppermute | solution.py:793
  139.5 31.0 %collective-permute-start.15 = (bf16[1024,1024]{1,0:T(8,128)(2,1)}, bf16[1024,1024]{1,0:T(8,128)(2,1)}, u32[]{:S(2)}, u32[]{:S(2)}) collective-permute-start(bf16[1024,1024]{1,0:T(8,128)(2,1)} %wo0.3), channel_id=1, source_target_pairs={{0,1},{1,0},{2,3},{3,2},{4,5},{5,4},{6,7},{7,6},{8,9},{9,8},{10,11... | collective-permute-start | bytes 6291464 | tf_op jit(solution)/shard_map/ppermute | solution.py:793
  143.9 26.6 %collective-permute-start.16 = (bf16[512,1024]{1,0:T(8,128)(2,1)S(1)}, bf16[512,1024]{1,0:T(8,128)(2,1)S(1)}, u32[]{:S(2)}, u32[]{:S(2)}) collective-permute-start(bf16[512,1024]{1,0:T(8,128)(2,1)S(1)} %bitcast.188), channel_id=1, source_target_pairs={{0,2},{1,3},{2,0},{3,1},{4,6},{5,7},{6,4},{7,5},{8,10},{9,11},{10,... | collective-permute-start | bytes 3145736 | tf_op jit(solution)/shard_map/ppermute | solution.py:974
  234.5 44.5 %collective-permute-start.22 = (bf16[4,128,1024]{2,1,0:T(8,128)(2,1)S(1)}, bf16[4,128,1024]{2,1,0:T(8,128)(2,1)}, u32[]{:S(2)}, u32[]{:S(2)}) collective-permute-start(bf16[4,128,1024]{2,1,0:T(8,128)(2,1)S(1)} %dynamic-slice_bitcast_fusion.1), channel_id=1, source_target_pairs={{0,4},{4,0},{1,5},{5,1},{2,6},{6,2},{3,7},{7,3},{8,12},{12,8},{9,1... | collective-permute-start | bytes 3145736 | tf_op jit(solution)/shard_map/ppermute | solution.py:849
  247.1 34.8 %collective-permute-start.23 = (bf16[4,128,1024]{2,1,0:T(8,128)(2,1)S(1)}, bf16[4,128,1024]{2,1,0:T(8,128)(2,1)}, u32[]{:S(2)}, u32[]{:S(2)}) collective-permute-start(bf16[4,128,1024]{2,1,0:T(8,128)(2,1)S(1)} %dynamic-slice_bitcast_fusion), channel_id=1, source_target_pairs={{0,4},{4,0},{1,5},{5,1},{2,6},{6,2},{3,7},{7,3},{8,12},{12,8},{9,1... | collective-permute-start | bytes 3145736 | tf_op jit(solution)/shard_map/ppermute | solution.py:849
  249.2 35.9 %collective-permute-start.21 = (bf16[512,1024]{1,0:T(8,128)(2,1)S(1)}, bf16[512,1024]{1,0:T(8,128)(2,1)}, u32[]{:S(2)}, u32[]{:S(2)}) collective-permute-start(bf16[512,1024]{1,0:T(8,128)(2,1)S(1)} %broadcast_select_fusion.6), channel_id=1, source_target_pairs={{0,2},{1,3},{2,0},{3,1},{4,6},{5,7},{6,4},{7,5},{8,10},{9,11},{10,... | collective-permute-start | bytes 3145736 | tf_op jit(solution)/shard_map/ppermute | solution.py:974
  293.9 114.5 %all-reduce.7.cloned.1.call-start = ((), (), s32[]{:S(2)}) async-start(), calls=%async_computation.4 | async-start | bytes 4194304 | tf_op jit(solution)/shard_map/psum | solution.py:861
  304.3 61.6 %collective-permute-start.26 = (bf16[1024,1024]{1,0:T(8,128)(2,1)}, bf16[1024,1024]{1,0:T(8,128)(2,1)}, u32[]{:S(2)}, u32[]{:S(2)}) collective-permute-start(bf16[1024,1024]{1,0:T(8,128)(2,1)} %self_weights.6.refs_5_), channel_id=1, source_target_pairs={{0,2},{1,3},{2,0},{3,1},{4,6},{5,7},{6,4},{7,5},{8,10},{9,11},{10,... | collective-permute-start | bytes 6291464 | tf_op jit(solution)/shard_map/ppermute | solution.py:793
  310.4 53.7 %all-to-all-start.2 = ((bf16[32,4,16,256]{3,1,2,0:T(4,128)(2,1)}), bf16[32,4,16,256]{3,1,2,0:T(4,128)(2,1)S(1)}, u32[]{:S(2)}, u32[]{:S(2)}) async-start(bf16[32,4,16,256]{3,1,2,0:T(4,128)(2,1)} %bitcast.38), calls=%async_computation.2 | async-start | bytes 2097152 | tf_op jit(solution)/shard_map/all_to_all | solution.py:880
  315.6 168.2 %all-reduce.9.cloned.1.call-start = ((), (), s32[]{:S(2)}) async-start(), calls=%async_computation.5 | async-start | bytes 2097152 | tf_op jit(solution)/shard_map/psum | solution.py:861
  379.1 29.3 %collective-permute-start.27 = (bf16[1024,1024]{1,0:T(8,128)(2,1)}, bf16[1024,1024]{1,0:T(8,128)(2,1)}, u32[]{:S(2)}, u32[]{:S(2)}) collective-permute-start(bf16[1024,1024]{1,0:T(8,128)(2,1)} %cross_weights.4.refs_8_), channel_id=1, source_target_pairs={{0,1},{1,0},{2,3},{3,2},{4,5},{5,4},{6,7},{7,6},{8,9},{9,8},{10,11... | collective-permute-start | bytes 6291464 | tf_op jit(solution)/shard_map/ppermute | solution.py:793
  392.8 44.6 %collective-permute-start.30 = (bf16[1024,1024]{1,0:T(8,128)(2,1)}, bf16[1024,1024]{1,0:T(8,128)(2,1)}, u32[]{:S(2)}, u32[]{:S(2)}) collective-permute-start(bf16[1024,1024]{1,0:T(8,128)(2,1)} %cross_weights.5.refs_12_), channel_id=1, source_target_pairs={{0,1},{1,0},{2,3},{3,2},{4,5},{5,4},{6,7},{7,6},{8,9},{9,8},{10,11... | collective-permute-start | bytes 6291464 | tf_op jit(solution)/shard_map/ppermute | solution.py:793
  432.0 26.2 %collective-permute-start.33 = (bf16[512,1024]{1,0:T(8,128)(2,1)}, bf16[512,1024]{1,0:T(8,128)(2,1)S(1)}, u32[]{:S(2)}, u32[]{:S(2)}) collective-permute-start(bf16[512,1024]{1,0:T(8,128)(2,1)} %get-tuple-element.88.refs_10_), channel_id=1, source_target_pairs={{0,2},{1,3},{2,0},{3,1},{4,6},{5,7},{6,4},{7,5},{8,10},{9,11},{10,... | collective-permute-start | bytes 3145736 | tf_op jit(solution)/shard_map/ppermute | solution.py:793
  433.5 133.9 %all-reduce.11.cloned.1.call-start = ((), (), s32[]{:S(2)}) async-start(), calls=%async_computation.6 | async-start | bytes 2228224 | tf_op jit(solution)/shard_map/psum | solution.py:861
  447.4 38.9 %collective-permute-start.36 = (bf16[4,64,1024]{2,1,0:T(8,128)(2,1)S(1)}, bf16[4,64,1024]{2,1,0:T(8,128)(2,1)}, u32[]{:S(2)}, u32[]{:S(2)}) collective-permute-start(bf16[4,64,1024]{2,1,0:T(8,128)(2,1)S(1)} %dynamic-slice_bitcast_fusion.3), channel_id=1, source_target_pairs={{0,4},{4,0},{1,5},{5,1},{2,6},{6,2},{3,7},{7,3},{8,12},{12,8},{9,1... | collective-permute-start | bytes 1572872 | tf_op jit(solution)/shard_map/ppermute | solution.py:849
  451.6 34.8 %collective-permute-start.38 = (bf16[4,64,1024]{2,1,0:T(8,128)(2,1)}, bf16[4,64,1024]{2,1,0:T(8,128)(2,1)S(1)}, u32[]{:S(2)}, u32[]{:S(2)}) collective-permute-start(bf16[4,64,1024]{2,1,0:T(8,128)(2,1)} %fusion.16), channel_id=1, source_target_pairs={{0,2},{1,3},{2,0},{3,1},{4,6},{5,7},{6,4},{7,5},{8,10},{9,11},{10,... | collective-permute-start | bytes 1572872 | tf_op jit(solution)/shard_map/ppermute | solution.py:793
  458.7 29.2 %collective-permute-start.34 = (bf16[4,64,1024]{2,1,0:T(8,128)(2,1)S(1)}, bf16[4,64,1024]{2,1,0:T(8,128)(2,1)S(1)}, u32[]{:S(2)}, u32[]{:S(2)}) collective-permute-start(bf16[4,64,1024]{2,1,0:T(8,128)(2,1)S(1)} %dynamic-slice_bitcast_fusion.4), channel_id=1, source_target_pairs={{0,4},{4,0},{1,5},{5,1},{2,6},{6,2},{3,7},{7,3},{8,12},{12,8},{9,1... | collective-permute-start | bytes 1572872 | tf_op jit(solution)/shard_map/ppermute | solution.py:849
  490.0 30.7 %collective-permute-start.35 = (bf16[4,128,1024]{2,1,0:T(8,128)(2,1)S(1)}, bf16[4,128,1024]{2,1,0:T(8,128)(2,1)}, u32[]{:S(2)}, u32[]{:S(2)}) collective-permute-start(bf16[4,128,1024]{2,1,0:T(8,128)(2,1)S(1)} %broadcast_select_fusion.4.own), channel_id=1, source_target_pairs={{0,4},{4,0},{1,5},{5,1},{2,6},{6,2},{3,7},{7,3},{8,12},{12,8},{9,1... | collective-permute-start | bytes 3145736 | tf_op jit(solution)/shard_map/ppermute | solution.py:849
  493.0 84.0 %collective-permute-start.41 = (bf16[4,256,1024]{2,1,0:T(8,128)(2,1)}, bf16[4,256,1024]{2,1,0:T(8,128)(2,1)}, u32[]{:S(2)}, u32[]{:S(2)}) collective-permute-start(bf16[4,256,1024]{2,1,0:T(8,128)(2,1)} %broadcast_select_fusion.own), channel_id=1, source_target_pairs={{0,4},{4,0},{1,5},{5,1},{2,6},{6,2},{3,7},{7,3},{8,12},{12,8},{9,1... | collective-permute-start | bytes 6291464 | tf_op jit(solution)/shard_map/ppermute | solution.py:849
  496.7 77.4 %all-to-all-start.3 = ((bf16[32,4,16,256]{3,2,1,0:T(8,128)(2,1)}), bf16[32,4,16,256]{3,2,1,0:T(8,128)(2,1)S(1)}, u32[]{:S(2)}, u32[]{:S(2)}) async-start(bf16[32,4,16,256]{3,2,1,0:T(8,128)(2,1)} %bitcast.69), calls=%async_computation.3 | async-start | bytes 2097152 | tf_op jit(solution)/shard_map/all_to_all | solution.py:880
  568.8 26.6 %collective-permute-start.40 = (bf16[4,136,1024]{2,1,0:T(8,128)(2,1)S(1)}, bf16[4,136,1024]{2,1,0:T(8,128)(2,1)S(1)}, u32[]{:S(2)}, u32[]{:S(2)}) collective-permute-start(bf16[4,136,1024]{2,1,0:T(8,128)(2,1)S(1)} %broadcast_select_fusion.2.own), channel_id=1, source_target_pairs={{0,4},{4,0},{1,5},{5,1},{2,6},{6,2},{3,7},{7,3},{8,12},{12,8},{9,1... | collective-permute-start | bytes 3342344 | tf_op jit(solution)/shard_map/ppermute | solution.py:849
  (70 other events, 587.6 us)
Sparse Core Ops, SparseCore 0:
  299.2 109.1 all-reduce.6
  433.7 50.0 all-reduce.8
  494.8 72.6 all-reduce.10

commit v3 on v2

--- a/solution.py
+++ b/solution.py
@@ -15,7 +15,6 @@
 SCALE = HD ** (-0.5)
 BF = jnp.bfloat16
 F32 = jnp.float32
-VMEM_BYTES = 58 * 2**20
 GRP = ("z", "x")
 
 ANY = pl.BlockSpec(memory_space=pl.ANY)
@@ -27,8 +26,8 @@
     return jax.ShapeDtypeStruct(dims, kind)
 
 
-def params():
-    return pltpu.CompilerParams(vmem_limit_bytes=VMEM_BYTES)
+def params(mib):
+    return pltpu.CompilerParams(vmem_limit_bytes=mib * 2**20)
 
 
 def cost(us):
@@ -149,7 +148,7 @@
         out_shape=outs,
         in_specs=[VM] * n + [ANY] * len(late),
         out_specs=[VM] * len(outs),
-        compiler_params=pltpu.CompilerParams(vmem_limit_bytes=12 * 2**20),
+        compiler_params=params(12),
         cost_estimate=cost(2),
         name="packed",
     )(*ins, *late)
@@ -206,33 +205,40 @@
         in_specs=[SM] + [ANY] * (2 + len(late)),
         out_specs=[VM] * 4,
         scratch_shapes=[pltpu.VMEM((2 * w, d), BF)] * 2 + [pltpu.SemaphoreType.DMA],
-        compiler_params=params(),
+        compiler_params=params(58),
         cost_estimate=cost(5),
         name="final",
     )(places, own, other, *late)
 
 
-def final_feed_body(places, own, other, out, hid, out_b, hid_b, sem):
-    copies = share_copies(places, (own, other), (out_b, hid_b), sem)
+def final_feed_body(places, own, other_o, other_h, out, hid, out_b, hid_b, sem):
+    c = other_o.shape[1]
+    copies = []
+    for z in range(own.shape[0]):
+        here, there = rows_at(2 * z + places[0], c), rows_at(2 * z + 1 - places[0], c)
+        for k, (other, buf) in enumerate(((other_o, out_b), (other_h, hid_b))):
+            src = own.at[z, pl.ds(k * c, c), :]
+            copies.append(pltpu.make_async_copy(src, buf.at[here, :], sem))
+            copies.append(pltpu.make_async_copy(other.at[z], buf.at[there, :], sem))
     begin(copies)
     finish(copies)
     out[...] = out_b[...].astype(F32)
     hid[...] = hid_b[...].astype(F32).T
 
 
-def final_feed(places, own, other):
+def final_feed(places, own, other_o, other_h):
     nz, c, d = own.shape
     ff = nz * c
     return pl.pallas_call(
         final_feed_body,
         out_shape=(shape((ff, d), F32), shape((d, ff), F32)),
-        in_specs=[SM] + [ANY] * 2,
+        in_specs=[SM] + [ANY] * 3,
         out_specs=[VM] * 2,
         scratch_shapes=[pltpu.VMEM((ff, d), BF)] * 2 + [pltpu.SemaphoreType.DMA],
-        compiler_params=params(),
+        compiler_params=params(58),
         cost_estimate=cost(6),
         name="final_feed",
-    )(places, own, other)
+    )(places, own, other_o, other_h)
 
 
 def keys_body(tp, points, came0, came1, *refs):
@@ -280,7 +286,7 @@
             pltpu.VMEM((d, 2 * d), BF),
             pltpu.SemaphoreType.DMA((4,)),
         ],
-        compiler_params=params(),
+        compiler_params=params(58),
         cost_estimate=cost(14),
         name="keys_values",
     )(points, *came, *packs, *late)
@@ -356,7 +362,7 @@
             pltpu.VMEM((rows, d), F32),
             pltpu.SemaphoreType.DMA((3,)),
         ],
-        compiler_params=params(),
+        compiler_params=params(58),
         cost_estimate=cost(20),
         name="cross_forward",
     )(idx, lens, x0, gain_c, gain_s, bias, kv, *packs)
@@ -417,7 +423,7 @@
             pltpu.VMEM((rows, d), F32),
             pltpu.SemaphoreType.DMA((2,)),
         ],
-        compiler_params=params(),
+        compiler_params=params(32),
         cost_estimate=cost(22),
         name="self_forward",
     )(ns, x1, gain_m, bias, *pack, *late)
@@ -463,7 +469,7 @@
         ),
         in_specs=[VM] * 7 + [ANY] * len(late),
         out_specs=[VM] * 5,
-        compiler_params=params(),
+        compiler_params=params(32),
         cost_estimate=cost(15),
         name="feed",
     )(nm, cot, hb, *wh, *wo, *late)
@@ -500,7 +506,7 @@
         out_shape=shape(dims, BF),
         in_specs=[spec(x) for x in ins],
         out_specs=pl.BlockSpec(dims, lambda i: (0, 0)),
-        compiler_params=params(),
+        compiler_params=params(16),
         cost_estimate=cost(6),
         name="feed_weights",
     )(*ins)
@@ -589,7 +595,7 @@
             pltpu.VMEM((rows, d), F32),
             pltpu.SemaphoreType.DMA((2,)),
         ],
-        compiler_params=params(),
+        compiler_params=params(44),
         cost_estimate=cost(27),
         name="self_backward",
     )(cot, gnm, x2, x1, gain_m, gain_s, qkv, *gots, *pack, *after)
@@ -690,7 +696,7 @@
             pltpu.VMEM((ext, 2 * d), BF),
             pltpu.SemaphoreType.DMA((3,)),
         ],
-        compiler_params=params(),
+        compiler_params=params(58),
         cost_estimate=cost(35),
         name="cross_backward",
     )(idx, lens, b1, g1, x0, gain_c, q, kv, *pack, *after)
@@ -739,7 +745,7 @@
         + [whole_block(x) for x in came]
         + [ANY] * len(late),
         out_specs=pl.BlockSpec((4 * w, d), lambda i: (0, 0)),
-        compiler_params=params(),
+        compiler_params=params(58),
         cost_estimate=cost(4),
         name="self_weights",
     )(ns, dqkv, o, b2, *came, *late)
@@ -782,7 +788,7 @@
         + [ANY] * len(late),
         out_specs=[pl.BlockSpec((r, d), lambda i: (0, 0)) for r in rows],
         scratch_shapes=[pltpu.VMEM((dkv.shape[0], d), BF), pltpu.SemaphoreType.DMA],
-        compiler_params=params(),
+        compiler_params=params(58),
         cost_estimate=cost(8),
         name="cross_weights",
     )(nc, dq, o, b1, dkv, points, *came_points, *came, *late)
@@ -849,12 +855,17 @@
     return lax.ppermute(v, "x", [(0, 1), (1, 0)])
 
 
-def over_x(v, late=()):
+def shares(v):
     nz = lax.axis_size("z")
     v = v.reshape((nz, 2, v.shape[0] // (2 * nz)) + v.shape[1:])
     x = lax.axis_index("x")
     keep = lax.dynamic_index_in_dim(v, x, 1, keepdims=False)
-    return add(keep, flip_x(lax.dynamic_index_in_dim(v, 1 - x, 1, keepdims=False)), late=late)
+    return keep, lax.dynamic_index_in_dim(v, 1 - x, 1, keepdims=False)
+
+
+def over_x(v, late=()):
+    keep, send = shares(v)
+    return add(keep, flip_x(send), late=late)
 
 
 def sum_z(v):
@@ -923,7 +934,7 @@
     kv_own = packed([[key_cross, value_cross]])[0]
     share = half_rows // 2
     core = bit_at("tp", 0)
-    sent = part_of(points, (2 + core).astype(jnp.int32).reshape(1), share, [kv_own])
+    sent = part_of(points, (2 + core).astype(jnp.int32).reshape(1), share)
     first = lax.ppermute(sent, GRP, [(k, (k + 1) % grp) for k in range(grp)])
     came_points = [first, flip(first, "tp", 0)]
     near = lax.dynamic_slice_in_dim(neighbours, t * per, per, 0).reshape(per * NB)
@@ -935,7 +946,6 @@
 
     kv_pack = gather_pieces(kv_own)
     qo_own = packed([[query_cross, output_cross]], [kv_own])[0]
-    qo_pack = gather_pieces(qo_own)
 
     small = jnp.concatenate(
         [
@@ -958,11 +968,13 @@
 
     gain_c, gain_s, gain_m = gain_cross[None], gain_self[None], gain_mlp[None]
     rows = per * lat_rows
+    self_own = packed([[query_self, key_self, value_self, output_self]], [qo_own])[0]
+    kv = keys_values(points, came_points, kv_pack, [self_own])
     x0 = (
-        to_groups(after(latents, kv_own), per).astype(F32).reshape(per, lat_rows, d) + embed[None]
+        to_groups(after(latents, kv_own, sent), per).astype(F32).reshape(per, lat_rows, d) + embed[None]
     ).reshape(rows, d)
-    self_own = packed([[query_self, key_self, value_self, output_self]], [qo_pack[2]])[0]
-    kv = keys_values(points, came_points, kv_pack, [x0, self_own])
+    x0 = after(x0, kv)
+    qo_pack = gather_pieces(qo_own, kv)
     q, oc, x1, nc, ns = cross_forward(idx, lens, x0, gain_c, gain_s, bias_c, kv, qo_pack)
     self_pack = gather_pieces(self_own, x1)
     cot = after(to_groups(after(cotangent, x0), per), x1)
@@ -1059,17 +1071,19 @@
     def waits(p, late):
         if p == tp - 1:
             stage["self"] = over_y(selfs, [emb])[0]
+            stage["returned"] = from_groups(after(g0, *late), per)
             return [stage["self"], restored]
         if p == tp - 3:
             return []
         if p == tp - 2:
             n = stage["self"].shape[0] // 2
             stage["self"] = [over_x(stage["self"][:n], late), over_x(stage["self"][n:], late)]
+            stage["returned"] = from_groups(after(g0, *late), per)
             return stage["self"] + [feed_z]
         if p == 0:
             stage["self"] = after(jnp.concatenate(stage["self"], axis=1), *late)
             stage["out"], stage["small"] = norms_and_small(late)
-            return [stage["small"]]
+            return [stage["small"], stage["returned"]]
         return []
 
     def cross_piece(p, came, late):
@@ -1082,11 +1096,15 @@
     cross_a = over_y({p: v[0] for p, v in cross.items()})[0]
     cross_b = over_y({p: over_x(v[1], [feed_z]) for p, v in cross.items()})[0]
     little = over_x(stage["small"])
-    cross_z = jnp.concatenate([over_x(cross_a, [self_z]), cross_b, little], axis=1)
-    feed_z, self_z = after(feed_z, cross_z), after(self_z, cross_z)
-    self_x, feed_x = flip_x(self_z), flip_x(feed_z)
-    returned = from_groups(after(g0, cross_z), per)
+    keep, send = shares(cross_a)
+    half = feed_z.shape[1] // 2
+    feed_ox = flip_x(after(feed_z[:, :half], send))
+    cross_z = jnp.concatenate([add(keep, flip_x(send)), cross_b, little], axis=1)
+    cross_z = after(cross_z, self_z, feed_ox)
+    feed_hx = flip_x(after(feed_z[:, half:], cross_z))
+    self_x = flip_x(after(self_z, cross_z))
     cross_z = after(sum_z(cross_z), self_x)
+    returned = stage["returned"]
     cross_x = flip_x(cross_z)
     n = little.shape[1]
     low = lax.axis_index("x") == 0
@@ -1095,7 +1113,7 @@
     total = total.astype(F32).reshape(-1)
     total = total[: total.shape[0] // w * w].reshape(-1, w)
     places = lax.axis_index("x").astype(jnp.int32).reshape(1)
-    output_weight_grad, hidden_weight_grad = final_feed(places, feed_z, feed_x)
+    output_weight_grad, hidden_weight_grad = final_feed(places, feed_z, feed_ox, feed_hx)
     query_self_grad, key_self_grad, value_self_grad, output_self_grad = final(
         places, w, self_z, self_x
     )

time: 615 us -> 597 us (0.971)
  waiting for transfers between devices: 178 us -> 158 us
  Pallas kernels: 248 us -> 229 us
  other arithmetic: 35.7 us -> 43 us
  between operations: 32.1 us -> 39.4 us
    psum x3, waiting for transfers between devices: 64.8 us -> 25.5 us  [sum_z(): return lax.psum(v, 'z')]
    ppermute x11 -> x12, waiting for transfers between devices: 48.1 us -> 73.2 us  [flip_x(): return lax.ppermute(v, 'x', [(0, 1), (1, 0)])]
    pallas_call x4, Pallas kernels: 27.3 us -> 18 us  [feed_weights(): pl.pallas_call(functools.partial(feed_weights_body, sets), grid=(1,), out...]
    ppermute x26, waiting for transfers between devices: 34.4 us -> 25.6 us  [flip(): return lax.ppermute(x, axis, [(i, i ^ 1 << bit) for i in range(n)])]
    select_n x20 -> x23, other arithmetic: 25.6 us -> 29.4 us  [after(): return jnp.where(ok, x, jnp.zeros_like(x))]
    slice x13 -> x17, local copies, waits for them, and re-layouts: 14.4 us -> 16.3 us  [after(): first = v[(0,) * v.ndim]]
    unnamed x118 -> x163, local copies, waits for them, and re-layouts: 18.6 us -> 19.8 us
    ppermute x11 -> x12, starting transfers between devices: 13.1 us -> 13.3 us  [flip_x(): return lax.ppermute(v, 'x', [(0, 1), (1, 0)])]
  transfers between devices with their start and end apart: 49 -> 50, of which waited for: 18 -> 17; matrix products, arithmetic and copies ran while one was open for 12% -> 14% of each run, Pallas kernels for 36% -> 34%
where the time goes in v3:
time: 597 us; the launch traced here: 589 us
  Pallas kernels  229 us (38%)
  waiting for transfers between devices  158 us (26%)
  local copies, waits for them, and re-layouts  65.5 us (11%)
  starting transfers between devices  54.3 us (9%)
  other arithmetic  43 us (7%)
  between operations  39.4 us (7%)
    ppermute x12, waiting for transfers between devices, flip_x(): return lax.ppermute(v, 'x', [(0, 1), (1, 0)])  73.2 us
    pallas_call x4, Pallas kernels, cross_weights(): pl.pallas_call(lambda *refs: cross_weights_body(*refs[:n], *refs[-k:]), g...  34.7 us
    pallas_call x1, Pallas kernels, cross_backward(): pl.pallas_call(functools.partial(cross_backward_body, tp), out_shape=(sha...  32.7 us
    select_n x23, other arithmetic, after(): return jnp.where(ok, x, jnp.zeros_like(x))  29.4 us
    pallas_call x2, Pallas kernels, feed(): pl.pallas_call(feed_body, out_shape=(shape((2, rows, ff), BF), shape((2,...  28.5 us
    ppermute x26, waiting for transfers between devices, flip(): return lax.ppermute(x, axis, [(i, i ^ 1 << bit) for i in range(n)])  25.6 us
    psum x3, waiting for transfers between devices, sum_z(): return lax.psum(v, 'z')  25.5 us
    pallas_call x1, Pallas kernels, self_backward(): pl.pallas_call(functools.partial(self_backward_body, tp, len(gots)), out_...  22.5 us
  transfers between devices with their start and end apart: 50, of which 17 were waited for; matrix products, arithmetic and copies ran while one was open for 14% of the time, Pallas kernels for 34%

profile of v3, /device:TPU:0, one launch (start us, length us, event | category | flops | bytes accessed | tf_op | source)
XLA Modules:
  0.0 589.0 jit_solution(8566542503169366431)
XLA Ops:
  21.5 5.1 all-to-all-start
  26.5 15.9 %collective-permute-done.came0.refs_6_ = bf16[512,1024]{1,0:T(8,128)(2,1)} collective-permute-done((bf16[512,1024]{1,0:T(8,128)(2,1)}, bf16[512,1024]{1,0:T(8,128)(2,1)}, u32[]{:S(2)}, u32[]{:S(2)}) %collective-permute-start) | collective-permute-done | bytes 1048608 | tf_op jit(solution)/shard_map/ppermute | solution.py:938
  53.3 13.6 %keys_values.1.kv = bf16[2048,2048]{1,0:T(8,128)(2,1)} custom-call(bf16[2048,1024]{1,0:T(8,128)(2,1)} %refs_5_.7, bf16[512,1024]{1,0:T(8,128)(2,1)} %collective-permute-done.came0.refs_6_, bf16[512,1024]{1,0:T(8,128)(2,1)} %collective-permute-done.1.came1.refs_7_, bf16[1024,512]{1,0:T(8,128)(2,1)} %copy-done.11, ...), custom_call_target="tpu_custom_call" | custom-call | flops 15399999488 | bytes 14000000 | tf_op jit(solution)/shard_map/keys_values/pallas_call | solution.py:278
  69.5 8.2 %collective-permute-done.9.refs_2_ = bf16[1024,512]{1,0:T(8,128)(2,1)S(1)} collective-permute-done((bf16[1024,512]{1,0:T(8,128)(2,1)S(1)}, bf16[1024,512]{1,0:T(8,128)(2,1)S(1)}, u32[]{:S(2)}, u32[]{:S(2)}) %collective-permute-start.9) | collective-permute-done | bytes 1048608 | tf_op jit(solution)/shard_map/ppermute | solution.py:799
  94.7 6.1 %all-to-all-start.1 = ((bf16[32,4,16,256]{3,1,2,0:T(4,128)(2,1)}), bf16[32,4,16,256]{3,1,2,0:T(4,128)(2,1)}, u32[]{:S(2)}, u32[]{:S(2)}) async-start(bf16[32,4,16,256]{3,1,2,0:T(4,128)(2,1)} %bitcast.188), calls=%async_computation.1 | async-start | bytes 2097152 | tf_op jit(solution)/shard_map/all_to_all | solution.py:880
  100.9 22.3 %cross_forward.1 = (bf16[512,1024]{1,0:T(8,128)(2,1)}, bf16[512,1024]{1,0:T(8,128)(2,1)}, f32[512,1024]{1,0:T(8,128)}, bf16[512,1024]{1,0:T(8,128)(2,1)}, bf16[512,1024]{1,0:T(8,128)(2,1)}) custom-call(s32[16]{0:T(128)} %compare_select_fusion.1.idx, s32[16]{0:T(128)} %gather_fusion, f32[512,1024]{1,0:T(8,128)} %copy-done.55, f32[1,1024]{1,0:T(1,128)} %bitcast.225, ...), custom_call_target="tpu_custom_call" | custom-call | flops 22000001024 | bytes 20000000 | tf_op jit(solution)/shard_map/cross_forward/pallas_call | solution.py:347
  125.7 6.8 %collective-permute-done.12.refs_2_.refs_3_ = bf16[1024,1024]{1,0:T(8,128)(2,1)S(1)} collective-permute-done((bf16[1024,1024]{1,0:T(8,128)(2,1)}, bf16[1024,1024]{1,0:T(8,128)(2,1)S(1)}, u32[]{:S(2)}, u32[]{:S(2)}) %collective-permute-start.12) | collective-permute-done | bytes 2097184 | tf_op jit(solution)/shard_map/ppermute | solution.py:799
  139.1 19.0 %self_forward.1 = (bf16[512,3072]{1,0:T(8,128)(2,1)S(1)}, bf16[512,1024]{1,0:T(8,128)(2,1)S(1)}, f32[512,1024]{1,0:T(8,128)S(1)}, bf16[512,1024]{1,0:T(8,128)(2,1)S(1)}) custom-call(bf16[512,1024]{1,0:T(8,128)(2,1)S(1)} %copy-done.31, f32[512,1024]{1,0:T(8,128)S(1)} %copy-done.29, f32[1,1024]{1,0:T(1,128)S(1)} %bitcast.179, f32[1,1024]{1,0:T(1,128)S(1)} %bitcast.176, ...), custom_call_target="tpu_custom_call" | custom-call | flops 24199999488 | bytes 22000000 | tf_op jit(solution)/shard_map/self_forward/pallas_call | solution.py:410
  163.2 14.1 %feed.2 = (bf16[2,512,1024]{2,1,0:T(8,128)(2,1)S(1)}, bf16[2,512,1024]{2,1,0:T(8,128)(2,1)S(1)}, f32[512,1024]{1,0:T(8,128)S(1)}, f32[512,1024]{1,0:T(8,128)S(1)}, f32[2,1024]{1,0:T(2,128)S(1)}) custom-call(bf16[512,1024]{1,0:T(8,128)(2,1)S(1)} %get-tuple-element.67.nm.refs_2_, bf16[512,1024]{1,0:T(8,128)(2,1)S(1)} %bitcast.171, ...), custom_call_target="tpu_custom_call" | custom-call | flops 16499999744 | bytes 15000000 | tf_op jit(solution)/shard_map/feed/pallas_call | solution.py:461
  180.0 7.3 %collective-permute-done.17.nm.refs_3_ = bf16[512,1024]{1,0:T(8,128)(2,1)S(1)} collective-permute-done((bf16[512,1024]{1,0:T(8,128)(2,1)S(1)}, bf16[512,1024]{1,0:T(8,128)(2,1)S(1)}, u32[]{:S(2)}, u32[]{:S(2)}) %collective-permute-start.17) | collective-permute-done | bytes 1048608 | tf_op jit(solution)/shard_map/ppermute | solution.py:986
  187.4 14.3 %feed.3 = (bf16[2,512,1024]{2,1,0:T(8,128)(2,1)S(1)}, bf16[2,512,1024]{2,1,0:T(8,128)(2,1)S(1)}, bf16[512,1024]{1,0:T(8,128)(2,1)S(1)}, bf16[512,1024]{1,0:T(8,128)(2,1)S(1)}, f32[2,1024]{1,0:T(2,128)S(1)}) custom-call(bf16[512,1024]{1,0:T(8,128)(2,1)S(1)} %collective-permute-done.17.nm.refs_3_, ...), custom_call_target="tpu_custom_call" | custom-call | flops 16499999744 | bytes 15000000 | tf_op jit(solution)/shard_map/feed/pallas_call | solution.py:461
  215.2 4.7 feed_weights.5.refs_5_
  222.2 4.6 feed_weights.7.refs_6_
  232.0 5.2 collective-permute-done.18.refs_0_
  237.2 22.5 %self_backward.1 = (bf16[512,1024]{1,0:T(8,128)(2,1)S(1)}, bf16[512,3072]{1,0:T(8,128)(2,1)}, f32[512,1024]{1,0:T(8,128)S(1)}, bf16[512,1024]{1,0:T(8,128)(2,1)S(1)}, f32[8,1024]{1,0:T(8,128)S(1)}) custom-call(bf16[512,1024]{1,0:T(8,128)(2,1)S(1)} %bitcast.174, f32[512,1024]{1,0:T(8,128)S(1)} %copy-done.43, f32[512,1024]{1,0:T(8,128)} %copy-done.7, ...), custom_call_target="tpu_custom_call" | custom-call | flops 29699999744 | bytes 27000000 | tf_op jit(solution)/shard_map/self_backward/pallas_call | solution.py:579
  283.4 5.2 self_weights.6.refs_5_
  294.9 5.1 all-to-all-start.2
  300.0 5.2 self_weights.7.refs_6_
  305.2 32.7 %cross_backward.1 = (bf16[512,1024]{1,0:T(8,128)(2,1)}, bf16[2048,2048]{1,0:T(8,128)(2,1)}, bf16[512,1024]{1,0:T(8,128)(2,1)}, f32[128,1024]{1,0:T(8,128)}, f32[8,1024]{1,0:T(8,128)}) custom-call(s32[16]{0:T(128)} %compare_select_fusion.1.idx, s32[16]{0:T(128)} %gather_fusion, bf16[512,1024]{1,0:T(8,128)(2,1)} %copy-done.33, f32[512,1024]{1,0:T(8,128)} %copy-done.45, ...), custom_call_target="tpu_custom_call" | custom-call | flops 38499999744 | bytes 35000000 | tf_op jit(solution)/shard_map/cross_backward/pallas_call | solution.py:679
  343.3 5.2 all-to-all-done.2
  354.8 8.7 %cross_weights.4.refs_8_ = bf16[1024,1024]{1,0:T(8,128)(2,1)} custom-call(bf16[512,1024]{1,0:T(8,128)(2,1)} %get-tuple-element.64.refs_0_, bf16[512,1024]{1,0:T(8,128)(2,1)} %get-tuple-element.84.refs_1_, bf16[512,1024]{1,0:T(8,128)(2,1)} %get-tuple-element.85.refs_2_, bf16[512,1024]{1,0:T(8,128)(2,1)} %copy-done.33, ...), custom_call_target="tpu_custom_call" | custom-call | flops 8800000000 | bytes 8000000 | tf_op jit(solution)/shard_map/cross_weights/pallas_call | solution.py:775
  366.2 8.4 %cross_weights.5.refs_12_ = bf16[1024,1024]{1,0:T(8,128)(2,1)} custom-call(bf16[512,1024]{1,0:T(8,128)(2,1)} %get-tuple-element.64.refs_0_, bf16[512,1024]{1,0:T(8,128)(2,1)} %get-tuple-element.84.refs_1_, bf16[512,1024]{1,0:T(8,128)(2,1)} %get-tuple-element.85.refs_2_, bf16[512,1024]{1,0:T(8,128)(2,1)} %copy-done.33, ...), custom_call_target="tpu_custom_call" | custom-call | flops 8800000000 | bytes 8000000 | tf_op jit(solution)/shard_map/cross_weights/pallas_call | solution.py:775
  387.3 7.9 %collective-permute-done.28 = bf16[4,64,1024]{2,1,0:T(8,128)(2,1)} collective-permute-done((bf16[4,64,1024]{2,1,0:T(8,128)(2,1)}, bf16[4,64,1024]{2,1,0:T(8,128)(2,1)}, u32[]{:S(2)}, u32[]{:S(2)}) %collective-permute-start.28) | collective-permute-done | bytes 524320 | tf_op jit(solution)/shard_map/ppermute | solution.py:855
  397.2 8.8 %cross_weights.6 = (bf16[512,1024]{1,0:T(8,128)(2,1)}, bf16[512,1024]{1,0:T(8,128)(2,1)}) custom-call(bf16[512,1024]{1,0:T(8,128)(2,1)} %get-tuple-element.64.refs_0_, bf16[512,1024]{1,0:T(8,128)(2,1)} %get-tuple-element.84.refs_1_, bf16[512,1024]{1,0:T(8,128)(2,1)} %get-tuple-element.85.refs_2_, bf16[512,1024]{1,0:T(8,128)(2,1)} %copy-done.33, ...), custom_call_target="tpu_custom_call" | custom-call | flops 8800000000 | bytes 8000000 | tf_op jit(solution)/shard_map/cross_weights/pallas_call | solution.py:775
  423.8 8.8 %cross_weights.7 = (bf16[512,1024]{1,0:T(8,128)(2,1)}, bf16[512,1024]{1,0:T(8,128)(2,1)}) custom-call(bf16[512,1024]{1,0:T(8,128)(2,1)} %get-tuple-element.64.refs_0_, bf16[512,1024]{1,0:T(8,128)(2,1)} %get-tuple-element.84.refs_1_, bf16[512,1024]{1,0:T(8,128)(2,1)} %get-tuple-element.85.refs_2_, bf16[512,1024]{1,0:T(8,128)(2,1)} %copy-done.33, ...), custom_call_target="tpu_custom_call" | custom-call | flops 8800000000 | bytes 8000000 | tf_op jit(solution)/shard_map/cross_weights/pallas_call | solution.py:775
  434.8 7.2 %collective-permute-done.33 = bf16[512,1024]{1,0:T(8,128)(2,1)} collective-permute-done((bf16[512,1024]{1,0:T(8,128)(2,1)}, bf16[512,1024]{1,0:T(8,128)(2,1)}, u32[]{:S(2)}, u32[]{:S(2)}) %collective-permute-start.33) | collective-permute-done | bytes 1048608 | tf_op jit(solution)/shard_map/ppermute | solution.py:799
  454.9 20.6 %collective-permute-done.39 = bf16[4,8,1024]{2,1,0:T(8,128)(2,1)S(1)} collective-permute-done((bf16[4,8,1024]{2,1,0:T(8,128)(2,1)S(1)}, bf16[4,8,1024]{2,1,0:T(8,128)(2,1)S(1)}, u32[]{:S(2)}, u32[]{:S(2)}) %collective-permute-start.39) | collective-permute-done | bytes 65568 | tf_op jit(solution)/shard_map/ppermute | solution.py:855
  479.7 5.2 collective-permute-done.35
  497.8 21.8 %collective-permute-done.40.other = bf16[4,128,1024]{2,1,0:T(8,128)(2,1)} collective-permute-done((bf16[4,128,1024]{2,1,0:T(8,128)(2,1)}, bf16[4,128,1024]{2,1,0:T(8,128)(2,1)}, u32[]{:S(2)}, u32[]{:S(2)}) %collective-permute-start.40) | collective-permute-done | bytes 1048608 | tf_op jit(solution)/shard_map/ppermute | solution.py:855
  522.1 25.4 %all-reduce.11.cloned.1.call-done = bf16[4,136,1024]{2,1,0:T(8,128)(2,1)} async-done(((bf16[4,136,1024]{2,1,0:T(8,128)(2,1)}), bf16[4,136,1024]{2,1,0:T(8,128)(2,1)}) %all-reduce.11.cloned.1.call-update) | async-done | bytes 1114128 | tf_op jit(solution)/shard_map/psum | solution.py:872
  555.2 6.3 %final_feed.1 = (f32[1024,1024]{1,0:T(8,128)}, f32[1024,1024]{1,0:T(8,128)}) custom-call(s32[1]{0:T(128)} %bitcast.75.places, bf16[4,256,1024]{2,1,0:T(8,128)(2,1)} %all-reduce.7.cloned.1.call-done.refs_11_.own, bf16[4,128,1024]{2,1,0:T(8,128)(2,1)} %collective-permute-done.34.other_o, bf16[4,128,1024]{2,1,0:T(8,128)(2,1)} %copy-done.75), custom_call_target="tpu_custom_call" | custom-call | flops 6600000000 | bytes 6000000 | tf_op jit(solution)/shard_map/final_feed/pallas_call | solution.py:232
  561.5 14.0 %collective-permute-done.41.other = bf16[4,136,1024]{2,1,0:T(8,128)(2,1)S(1)} collective-permute-done((bf16[4,136,1024]{2,1,0:T(8,128)(2,1)S(1)}, bf16[4,136,1024]{2,1,0:T(8,128)(2,1)S(1)}, u32[]{:S(2)}, u32[]{:S(2)}) %collective-permute-start.41) | collective-permute-done | bytes 1114144 | tf_op jit(solution)/shard_map/ppermute | solution.py:855
  (377 shorter events, 183.3 us)
Async XLA Ops:
  9.6 32.9 %collective-permute-start = (bf16[512,1024]{1,0:T(8,128)(2,1)}, bf16[512,1024]{1,0:T(8,128)(2,1)}, u32[]{:S(2)}, u32[]{:S(2)}) collective-permute-start(bf16[512,1024]{1,0:T(8,128)(2,1)} %part_of.1), channel_id=1, source_target_pairs={{0,4},{4,8},{8,12},{12,16},{16,20},{20,24},{24,28},{28,0},{1,5},{5... | collective-permute-start | bytes 3145736 | tf_op jit(solution)/shard_map/ppermute | solution.py:938
  12.7 32.3 %collective-permute-start.3 = (bf16[1024,512]{1,0:T(8,128)(2,1)S(1)}, bf16[1024,512]{1,0:T(8,128)(2,1)}, u32[]{:S(2)}, u32[]{:S(2)}) collective-permute-start(bf16[1024,512]{1,0:T(8,128)(2,1)S(1)} %packed.3.refs_2_.refs_0_), channel_id=1, source_target_pairs={{0,2},{1,3},{2,0},{3,1},{4,6},{5,7},{6,4},{7,5},{8,10},{9,11},{10,... | collective-permute-start | bytes 3145736 | tf_op jit(solution)/shard_map/ppermute | solution.py:799
  14.3 36.1 %collective-permute-start.2 = (bf16[1024,512]{1,0:T(8,128)(2,1)S(1)}, bf16[1024,512]{1,0:T(8,128)(2,1)}, u32[]{:S(2)}, u32[]{:S(2)}) collective-permute-start(bf16[1024,512]{1,0:T(8,128)(2,1)S(1)} %packed.3.refs_2_.refs_0_), channel_id=1, source_target_pairs={{0,1},{1,0},{2,3},{3,2},{4,5},{5,4},{6,7},{7,6},{8,9},{9,8},{10,11... | collective-permute-start | bytes 3145736 | tf_op jit(solution)/shard_map/ppermute | solution.py:799
  16.2 53.2 %collective-permute-start.6 = (f32[135,256]{1,0:T(8,128)S(1)}, f32[135,256]{1,0:T(8,128)}, u32[]{:S(2)}, u32[]{:S(2)}) collective-permute-start(f32[135,256]{1,0:T(8,128)S(1)} %concatenate.18), channel_id=1, source_target_pairs={{0,2},{1,3},{2,0},{3,1},{4,6},{5,7},{6,4},{7,5},{8,10},{9,11},{10,... | collective-permute-start | bytes 414728 | tf_op jit(solution)/shard_map/ppermute | solution.py:799
  16.8 62.1 %collective-permute-start.5 = (f32[135,256]{1,0:T(8,128)S(1)}, f32[135,256]{1,0:T(8,128)S(1)}, u32[]{:S(2)}, u32[]{:S(2)}) collective-permute-start(f32[135,256]{1,0:T(8,128)S(1)} %concatenate.18), channel_id=1, source_target_pairs={{0,1},{1,0},{2,3},{3,2},{4,5},{5,4},{6,7},{7,6},{8,9},{9,8},{10,11... | collective-permute-start | bytes 414728 | tf_op jit(solution)/shard_map/ppermute | solution.py:799
  21.5 60.7 %all-to-all-start = ((bf16[32,4,16,256]{3,1,2,0:T(4,128)(2,1)}), bf16[32,4,16,256]{3,1,2,0:T(4,128)(2,1)}, u32[]{:S(2)}, u32[]{:S(2)}) async-start(bf16[32,4,16,256]{3,1,2,0:T(4,128)(2,1)} %bitcast.162), calls=%async_computation | async-start | bytes 2097152 | tf_op jit(solution)/shard_map/all_to_all | solution.py:880
  50.4 27.4 %collective-permute-start.9 = (bf16[1024,512]{1,0:T(8,128)(2,1)S(1)}, bf16[1024,512]{1,0:T(8,128)(2,1)S(1)}, u32[]{:S(2)}, u32[]{:S(2)}) collective-permute-start(bf16[1024,512]{1,0:T(8,128)(2,1)S(1)} %packed.4.refs_4_.refs_0_), channel_id=1, source_target_pairs={{0,2},{1,3},{2,0},{3,1},{4,6},{5,7},{6,4},{7,5},{8,10},{9,11},{10,... | collective-permute-start | bytes 3145736 | tf_op jit(solution)/shard_map/ppermute | solution.py:799
  52.7 48.2 %collective-permute-start.8 = (bf16[1024,512]{1,0:T(8,128)(2,1)S(1)}, bf16[1024,512]{1,0:T(8,128)(2,1)}, u32[]{:S(2)}, u32[]{:S(2)}) collective-permute-start(bf16[1024,512]{1,0:T(8,128)(2,1)S(1)} %packed.4.refs_4_.refs_0_), channel_id=1, source_target_pairs={{0,1},{1,0},{2,3},{3,2},{4,5},{5,4},{6,7},{7,6},{8,9},{9,8},{10,11... | collective-permute-start | bytes 3145736 | tf_op jit(solution)/shard_map/ppermute | solution.py:799
  52.9 79.6 %collective-permute-start.12 = (bf16[1024,1024]{1,0:T(8,128)(2,1)}, bf16[1024,1024]{1,0:T(8,128)(2,1)S(1)}, u32[]{:S(2)}, u32[]{:S(2)}) collective-permute-start(bf16[1024,1024]{1,0:T(8,128)(2,1)} %packed.5.refs_4_.refs_0_.refs_1_), channel_id=1, source_target_pairs={{0,2},{1,3},{2,0},{3,1},{4,6},{5,7},{6,4},{7,5},{8,10},{9,11},{10,... | collective-permute-start | bytes 6291464 | tf_op jit(solution)/shard_map/ppermute | solution.py:799
  69.4 69.6 %collective-permute-start.11 = (bf16[1024,1024]{1,0:T(8,128)(2,1)}, bf16[1024,1024]{1,0:T(8,128)(2,1)}, u32[]{:S(2)}, u32[]{:S(2)}) collective-permute-start(bf16[1024,1024]{1,0:T(8,128)(2,1)} %packed.5.refs_4_.refs_0_.refs_1_), channel_id=1, source_target_pairs={{0,1},{1,0},{2,3},{3,2},{4,5},{5,4},{6,7},{7,6},{8,9},{9,8},{10,11... | collective-permute-start | bytes 6291464 | tf_op jit(solution)/shard_map/ppermute | solution.py:799
  94.7 39.9 %all-to-all-start.1 = ((bf16[32,4,16,256]{3,1,2,0:T(4,128)(2,1)}), bf16[32,4,16,256]{3,1,2,0:T(4,128)(2,1)}, u32[]{:S(2)}, u32[]{:S(2)}) async-start(bf16[32,4,16,256]{3,1,2,0:T(4,128)(2,1)} %bitcast.188), calls=%async_computation.1 | async-start | bytes 2097152 | tf_op jit(solution)/shard_map/all_to_all | solution.py:880
  134.1 29.1 %collective-permute-start.14 = (bf16[1024,1024]{1,0:T(8,128)(2,1)}, bf16[1024,1024]{1,0:T(8,128)(2,1)}, u32[]{:S(2)}, u32[]{:S(2)}) collective-permute-start(bf16[1024,1024]{1,0:T(8,128)(2,1)} %wh0.3), channel_id=1, source_target_pairs={{0,1},{1,0},{2,3},{3,2},{4,5},{5,4},{6,7},{7,6},{8,9},{9,8},{10,11... | collective-permute-start | bytes 6291464 | tf_op jit(solution)/shard_map/ppermute | solution.py:799
  134.6 28.6 %collective-permute-start.15 = (bf16[1024,1024]{1,0:T(8,128)(2,1)}, bf16[1024,1024]{1,0:T(8,128)(2,1)}, u32[]{:S(2)}, u32[]{:S(2)}) collective-permute-start(bf16[1024,1024]{1,0:T(8,128)(2,1)} %wo0.3), channel_id=1, source_target_pairs={{0,1},{1,0},{2,3},{3,2},{4,5},{5,4},{6,7},{7,6},{8,9},{9,8},{10,11... | collective-permute-start | bytes 6291464 | tf_op jit(solution)/shard_map/ppermute | solution.py:799
  220.0 43.1 %collective-permute-start.22 = (bf16[4,128,1024]{2,1,0:T(8,128)(2,1)S(1)}, bf16[4,128,1024]{2,1,0:T(8,128)(2,1)S(1)}, u32[]{:S(2)}, u32[]{:S(2)}) collective-permute-start(bf16[4,128,1024]{2,1,0:T(8,128)(2,1)S(1)} %dynamic-slice_bitcast_fusion.1), channel_id=1, source_target_pairs={{0,4},{4,0},{1,5},{5,1},{2,6},{6,2},{3,7},{7,3},{8,12},{12,8},{9,1... | collective-permute-start | bytes 3145736 | tf_op jit(solution)/shard_map/ppermute | solution.py:855
  227.5 39.9 %collective-permute-start.23 = (bf16[4,128,1024]{2,1,0:T(8,128)(2,1)S(1)}, bf16[4,128,1024]{2,1,0:T(8,128)(2,1)S(1)}, u32[]{:S(2)}, u32[]{:S(2)}) collective-permute-start(bf16[4,128,1024]{2,1,0:T(8,128)(2,1)S(1)} %dynamic-slice_bitcast_fusion), channel_id=1, source_target_pairs={{0,4},{4,0},{1,5},{5,1},{2,6},{6,2},{3,7},{7,3},{8,12},{12,8},{9,1... | collective-permute-start | bytes 3145736 | tf_op jit(solution)/shard_map/ppermute | solution.py:855
  231.0 38.4 %collective-permute-start.21 = (bf16[512,1024]{1,0:T(8,128)(2,1)}, bf16[512,1024]{1,0:T(8,128)(2,1)}, u32[]{:S(2)}, u32[]{:S(2)}) collective-permute-start(bf16[512,1024]{1,0:T(8,128)(2,1)} %broadcast_select_fusion.5), channel_id=1, source_target_pairs={{0,2},{1,3},{2,0},{3,1},{4,6},{5,7},{6,4},{7,5},{8,10},{9,11},{10,... | collective-permute-start | bytes 3145736 | tf_op jit(solution)/shard_map/ppermute | solution.py:986
  278.2 119.0 %all-reduce.7.cloned.1.call-start = ((), (), s32[]{:S(2)}) async-start(), calls=%async_computation.4 | async-start | bytes 4194304 | tf_op jit(solution)/shard_map/psum | solution.py:872
  288.6 61.6 %collective-permute-start.26 = (bf16[1024,1024]{1,0:T(8,128)(2,1)}, bf16[1024,1024]{1,0:T(8,128)(2,1)}, u32[]{:S(2)}, u32[]{:S(2)}) collective-permute-start(bf16[1024,1024]{1,0:T(8,128)(2,1)} %self_weights.6.refs_5_), channel_id=1, source_target_pairs={{0,2},{1,3},{2,0},{3,1},{4,6},{5,7},{6,4},{7,5},{8,10},{9,11},{10,... | collective-permute-start | bytes 6291464 | tf_op jit(solution)/shard_map/ppermute | solution.py:799
  294.9 53.6 %all-to-all-start.2 = ((bf16[32,4,16,256]{3,1,2,0:T(4,128)(2,1)}), bf16[32,4,16,256]{3,1,2,0:T(4,128)(2,1)S(1)}, u32[]{:S(2)}, u32[]{:S(2)}) async-start(bf16[32,4,16,256]{3,1,2,0:T(4,128)(2,1)} %bitcast.40), calls=%async_computation.2 | async-start | bytes 2097152 | tf_op jit(solution)/shard_map/all_to_all | solution.py:891
  363.5 33.7 %collective-permute-start.27 = (bf16[1024,1024]{1,0:T(8,128)(2,1)}, bf16[1024,1024]{1,0:T(8,128)(2,1)}, u32[]{:S(2)}, u32[]{:S(2)}) collective-permute-start(bf16[1024,1024]{1,0:T(8,128)(2,1)} %cross_weights.4.refs_8_), channel_id=1, source_target_pairs={{0,1},{1,0},{2,3},{3,2},{4,5},{5,4},{6,7},{7,6},{8,9},{9,8},{10,11... | collective-permute-start | bytes 6291464 | tf_op jit(solution)/shard_map/ppermute | solution.py:799
  375.8 48.0 %collective-permute-start.30 = (bf16[1024,1024]{1,0:T(8,128)(2,1)}, bf16[1024,1024]{1,0:T(8,128)(2,1)}, u32[]{:S(2)}, u32[]{:S(2)}) collective-permute-start(bf16[1024,1024]{1,0:T(8,128)(2,1)} %cross_weights.5.refs_12_), channel_id=1, source_target_pairs={{0,1},{1,0},{2,3},{3,2},{4,5},{5,4},{6,7},{7,6},{8,9},{9,8},{10,11... | collective-permute-start | bytes 6291464 | tf_op jit(solution)/shard_map/ppermute | solution.py:799
  381.4 33.4 %all-to-all-start.3 = ((bf16[32,4,16,256]{3,1,2,0:T(4,128)(2,1)}), bf16[32,4,16,256]{3,1,2,0:T(4,128)(2,1)S(1)}, u32[]{:S(2)}, u32[]{:S(2)}) async-start(bf16[32,4,16,256]{3,1,2,0:T(4,128)(2,1)} %bitcast.53), calls=%async_computation.3 | async-start | bytes 2097152 | tf_op jit(solution)/shard_map/all_to_all | solution.py:891
  385.2 90.4 %all-reduce.9.cloned.1.call-start = ((), (), s32[]{:S(2)}) async-start(), calls=%async_computation.5 | async-start | bytes 2097152 | tf_op jit(solution)/shard_map/psum | solution.py:872
  421.3 27.9 %collective-permute-start.37 = (bf16[4,64,1024]{2,1,0:T(8,128)(2,1)}, bf16[4,64,1024]{2,1,0:T(8,128)(2,1)}, u32[]{:S(2)}, u32[]{:S(2)}) collective-permute-start(bf16[4,64,1024]{2,1,0:T(8,128)(2,1)} %dynamic-slice_bitcast_fusion.2), channel_id=1, source_target_pairs={{0,4},{4,0},{1,5},{5,1},{2,6},{6,2},{3,7},{7,3},{8,12},{12,8},{9,1... | collective-permute-start | bytes 1572872 | tf_op jit(solution)/shard_map/ppermute | solution.py:855
  434.6 43.5 %collective-permute-start.36 = (bf16[4,64,1024]{2,1,0:T(8,128)(2,1)}, bf16[4,64,1024]{2,1,0:T(8,128)(2,1)}, u32[]{:S(2)}, u32[]{:S(2)}) collective-permute-start(bf16[4,64,1024]{2,1,0:T(8,128)(2,1)} %dynamic-slice_bitcast_fusion.3), channel_id=1, source_target_pairs={{0,4},{4,0},{1,5},{5,1},{2,6},{6,2},{3,7},{7,3},{8,12},{12,8},{9,1... | collective-permute-start | bytes 1572872 | tf_op jit(solution)/shard_map/ppermute | solution.py:855
  447.8 38.4 %collective-permute-start.34 = (bf16[4,128,1024]{2,1,0:T(8,128)(2,1)}, bf16[4,128,1024]{2,1,0:T(8,128)(2,1)}, u32[]{:S(2)}, u32[]{:S(2)}) collective-permute-start(bf16[4,128,1024]{2,1,0:T(8,128)(2,1)} %slice_select_fusion.1), channel_id=1, source_target_pairs={{0,4},{4,0},{1,5},{5,1},{2,6},{6,2},{3,7},{7,3},{8,12},{12,8},{9,1... | collective-permute-start | bytes 3145736 | tf_op jit(solution)/shard_map/ppermute | solution.py:855
  451.3 26.8 %collective-permute-start.38 = (bf16[4,64,1024]{2,1,0:T(8,128)(2,1)}, bf16[4,64,1024]{2,1,0:T(8,128)(2,1)}, u32[]{:S(2)}, u32[]{:S(2)}) collective-permute-start(bf16[4,64,1024]{2,1,0:T(8,128)(2,1)} %fusion.16), channel_id=1, source_target_pairs={{0,2},{1,3},{2,0},{3,1},{4,6},{5,7},{6,4},{7,5},{8,10},{9,11},{10,... | collective-permute-start | bytes 1572872 | tf_op jit(solution)/shard_map/ppermute | solution.py:799
  453.5 31.4 %collective-permute-start.35 = (bf16[4,64,1024]{2,1,0:T(8,128)(2,1)}, bf16[4,64,1024]{2,1,0:T(8,128)(2,1)}, u32[]{:S(2)}, u32[]{:S(2)}) collective-permute-start(bf16[4,64,1024]{2,1,0:T(8,128)(2,1)} %copy-done.67), channel_id=1, source_target_pairs={{0,4},{4,0},{1,5},{5,1},{2,6},{6,2},{3,7},{7,3},{8,12},{12,8},{9,1... | collective-permute-start | bytes 1572872 | tf_op jit(solution)/shard_map/ppermute | solution.py:855
  489.5 58.1 %all-reduce.11.cloned.1.call-start = ((), (), s32[]{:S(2)}) async-start(), calls=%async_computation.6 | async-start | bytes 2228224 | tf_op jit(solution)/shard_map/psum | solution.py:872
  493.2 26.4 %collective-permute-start.40 = (bf16[4,128,1024]{2,1,0:T(8,128)(2,1)}, bf16[4,128,1024]{2,1,0:T(8,128)(2,1)}, u32[]{:S(2)}, u32[]{:S(2)}) collective-permute-start(bf16[4,128,1024]{2,1,0:T(8,128)(2,1)} %broadcast_select_fusion.2), channel_id=1, source_target_pairs={{0,4},{4,0},{1,5},{5,1},{2,6},{6,2},{3,7},{7,3},{8,12},{12,8},{9,1... | collective-permute-start | bytes 3145736 | tf_op jit(solution)/shard_map/ppermute | solution.py:855
  495.7 58.6 %collective-permute-start.42 = (bf16[4,128,1024]{2,1,0:T(8,128)(2,1)}, bf16[4,128,1024]{2,1,0:T(8,128)(2,1)S(1)}, u32[]{:S(2)}, u32[]{:S(2)}) collective-permute-start(bf16[4,128,1024]{2,1,0:T(8,128)(2,1)} %slice_select_fusion), channel_id=1, source_target_pairs={{0,4},{4,0},{1,5},{5,1},{2,6},{6,2},{3,7},{7,3},{8,12},{12,8},{9,1... | collective-permute-start | bytes 3145736 | tf_op jit(solution)/shard_map/ppermute | solution.py:855
  548.9 26.6 %collective-permute-start.41 = (bf16[4,136,1024]{2,1,0:T(8,128)(2,1)S(1)}, bf16[4,136,1024]{2,1,0:T(8,128)(2,1)S(1)}, u32[]{:S(2)}, u32[]{:S(2)}) collective-permute-start(bf16[4,136,1024]{2,1,0:T(8,128)(2,1)S(1)} %broadcast_select_fusion.1.own), channel_id=1, source_target_pairs={{0,4},{4,0},{1,5},{5,1},{2,6},{6,2},{3,7},{7,3},{8,12},{12,8},{9,1... | collective-permute-start | bytes 3342344 | tf_op jit(solution)/shard_map/ppermute | solution.py:855
  (94 other events, 903.2 us)
Sparse Core Ops, SparseCore 0:
  283.5 112.7 all-reduce.6
  420.6 53.7 all-reduce.8
  493.3 54.2 all-reduce.10

commit v4 on v3

--- a/solution.py
+++ b/solution.py
@@ -116,6 +116,11 @@
 def softmax_parts(s, axis):
     e = jnp.exp((s - jnp.max(s, axis=axis, keepdims=True)) * SCALE)
     return e * (1.0 / jnp.sum(e, axis=axis, keepdims=True))
+
+
+def head_sets(tp, w, size):
+    heads = [(p, h * HD) for p in range(tp) for h in range(w // HD)]
+    return [heads[i : i + size] for i in range(0, len(heads), size)]
 
 
 def pack_body(counts, *refs):
@@ -319,14 +324,20 @@
         at = [rows_at(idx[g * NB + n], PB) for n in range(NB)]
         lane = lax.broadcasted_iota(jnp.int32, (1, PB), 1)
         live = jnp.concatenate([(lane < lens[g * NB + n]).astype(jnp.int32) for n in range(NB)], axis=1) > 0
-        for p in range(tp):
-            for h in range(w // HD):
-                c = p * w + h * HD
-                k0 = p * 2 * w + h * HD
-                k = jnp.concatenate([kv_b[a, k0 : k0 + HD] for a in at], axis=0)
-                v = jnp.concatenate([kv_b[a, k0 + w : k0 + w + HD] for a in at], axis=0)
-                pr = softmax_parts(jnp.where(live, nt(q[s, c : c + HD], k), NEG), 1)
-                o[s, c : c + HD] = nn(pr.astype(BF), v).astype(BF)
+        for heads in head_sets(tp, w, 8):
+            def part(lo):
+                return [
+                    jnp.concatenate([kv_b[a, p * 2 * w + lo + h : p * 2 * w + lo + h + HD] for a in at], axis=0)
+                    for p, h in heads
+                ]
+
+            qs = [q[s, p * w + h : p * w + h + HD] for p, h in heads]
+            ks, vs = part(0), part(w)
+            ss = [jnp.where(live, nt(x, k), NEG) for x, k in zip(qs, ks)]
+            ps = [softmax_parts(x, 1).astype(BF) for x in ss]
+            outs = [nn(x, v).astype(BF) for x, v in zip(ps, vs)]
+            for (p, h), x in zip(heads, outs):
+                o[s, p * w + h : p * w + h + HD] = x
 
     finish(wo_c)
     acc[...] = nn(o[...], wo_b[...])
@@ -384,13 +395,16 @@
     @pl.loop(0, rows // PB)
     def _(g):
         s = rows_at(g, PB)
-        for p in range(tp):
-            for h in range(w // HD):
-                c = p * w + h * HD
-                k0 = p * 3 * w + h * HD
-                pr = softmax_parts(nt(qkv[s, k0 : k0 + HD], qkv[s, k0 + w : k0 + w + HD]), 1)
-                v = qkv[s, k0 + 2 * w : k0 + 2 * w + HD]
-                o[s, c : c + HD] = nn(pr.astype(BF), v).astype(BF)
+        for heads in head_sets(tp, w, 8):
+            qs, ks, vs = (
+                [qkv[s, p * 3 * w + lo + h : p * 3 * w + lo + h + HD] for p, h in heads]
+                for lo in (0, w, 2 * w)
+            )
+            ss = [nt(x, k) for x, k in zip(qs, ks)]
+            ps = [softmax_parts(x, 1).astype(BF) for x in ss]
+            outs = [nn(x, v).astype(BF) for x, v in zip(ps, vs)]
+            for (p, h), x in zip(heads, outs):
+                o[s, p * w + h : p * w + h + HD] = x
 
     finish(wo_c)
     acc[...] = nn(o[...], wo_b[...])
@@ -544,19 +558,24 @@
     @pl.loop(0, rows // PB)
     def _(g):
         s = rows_at(g, PB)
-        for p in range(tp):
-            for h in range(w // HD):
-                c = p * w + h * HD
-                k0 = p * 3 * w + h * HD
-                k1, k2 = k0 + w, k0 + 2 * w
-                q, k, v = qkv[s, k0 : k0 + HD], qkv[s, k1 : k1 + HD], qkv[s, k2 : k2 + HD]
-                pr = softmax_parts(nt(k, q), 0)
-                do = gso[s, c : c + HD]
-                dp = nt(v, do)
-                ds = (pr * (dp - jnp.sum(dp * pr, axis=0, keepdims=True))).astype(BF)
-                dqkv[s, k0 : k0 + HD] = (tn(ds, k) * SCALE).astype(BF)
-                dqkv[s, k1 : k1 + HD] = (nn(ds, q) * SCALE).astype(BF)
-                dqkv[s, k2 : k2 + HD] = nn(pr.astype(BF), do).astype(BF)
+        for heads in head_sets(tp, w, 8):
+            qs, ks, vs = (
+                [qkv[s, p * 3 * w + lo + h : p * 3 * w + lo + h + HD] for p, h in heads]
+                for lo in (0, w, 2 * w)
+            )
+            dos = [gso[s, p * w + h : p * w + h + HD] for p, h in heads]
+            ss = [nt(k, x) for x, k in zip(qs, ks)]
+            dps = [nt(v, x) for x, v in zip(dos, vs)]
+            prs = [softmax_parts(x, 0) for x in ss]
+            dss = [
+                (x * (y - jnp.sum(y * x, axis=0, keepdims=True))).astype(BF) for x, y in zip(prs, dps)
+            ]
+            dqs = [(tn(x, k) * SCALE).astype(BF) for x, k in zip(dss, ks)]
+            dks = [(nn(x, y) * SCALE).astype(BF) for x, y in zip(dss, qs)]
+            dvs = [nn(x.astype(BF), y).astype(BF) for x, y in zip(prs, dos)]
+            for lo, parts_out in ((0, dqs), (w, dks), (2 * w, dvs)):
+                for (p, h), x in zip(heads, parts_out):
+                    dqkv[s, p * 3 * w + lo + h : p * 3 * w + lo + h + HD] = x
 
     finish(wqkv_c)
     gns[...] = nt(dqkv[...], wqkv_b[...])
@@ -631,24 +650,30 @@
         at = [rows_at(idx[g * NB + n], PB) for n in range(NB)]
         row = lax.broadcasted_iota(jnp.int32, (PB, PB), 0)
         live = jnp.concatenate([(row < lens[g * NB + n]).astype(jnp.int32) for n in range(NB)], axis=0) > 0
-        for p in range(tp):
-            for h in range(w // HD):
-                c = p * w + h * HD
-                k0 = p * 2 * w + h * HD
-                v0 = k0 + w
-                k = jnp.concatenate([kv_b[a, k0 : k0 + HD] for a in at], axis=0)
-                v = jnp.concatenate([kv_b[a, v0 : v0 + HD] for a in at], axis=0)
-                qh = q[s, c : c + HD]
-                do = gco[s, c : c + HD]
-                pr = softmax_parts(jnp.where(live, nt(k, qh), NEG), 0)
-                dp = nt(v, do)
-                ds = (pr * (dp - jnp.sum(dp * pr, axis=0, keepdims=True))).astype(BF)
-                dq[s, c : c + HD] = (tn(ds, k) * SCALE).astype(BF)
-                dk = nn(ds, qh)
-                dv = nn(pr.astype(BF), do)
+        for heads in head_sets(tp, w, 8):
+            def part(lo):
+                return [
+                    jnp.concatenate([kv_b[a, p * 2 * w + lo + h : p * 2 * w + lo + h + HD] for a in at], axis=0)
+                    for p, h in heads
+                ]
+
+            qs, dos = ([r[s, p * w + h : p * w + h + HD] for p, h in heads] for r in (q, gco))
+            ks, vs = part(0), part(w)
+            ss = [jnp.where(live, nt(k, x), NEG) for x, k in zip(qs, ks)]
+            dps = [nt(v, x) for x, v in zip(dos, vs)]
+            prs = [softmax_parts(x, 0) for x in ss]
+            dss = [
+                (x * (y - jnp.sum(y * x, axis=0, keepdims=True))).astype(BF) for x, y in zip(prs, dps)
+            ]
+            dqs = [(tn(x, k) * SCALE).astype(BF) for x, k in zip(dss, ks)]
+            dks = [nn(x, y) for x, y in zip(dss, qs)]
+            dvs = [nn(x.astype(BF), y) for x, y in zip(prs, dos)]
+            for (p, h), x, y, z in zip(heads, dqs, dks, dvs):
+                dq[s, p * w + h : p * w + h + HD] = x
+                k0 = p * 2 * w + h
                 for j, a in enumerate(at):
-                    dacc[a, k0 : k0 + HD] += dk[j * PB : (j + 1) * PB, :]
-                    dacc[a, v0 : v0 + HD] += dv[j * PB : (j + 1) * PB, :]
+                    dacc[a, k0 : k0 + HD] += y[j * PB : (j + 1) * PB, :]
+                    dacc[a, k0 + w : k0 + w + HD] += z[j * PB : (j + 1) * PB, :]
 
     @pl.loop(0, ext // PB)
     def _(i):

time: 597 us -> 596 us (level)
  Pallas kernels: 229 us -> 203 us
  waiting for transfers between devices: 158 us -> 182 us
    pallas_call x1, Pallas kernels: 19 us -> 11 us  [self_forward(): pl.pallas_call(functools.partial(self_forward_body, tp), out_shape=(shape...]
    ppermute x4, waiting for transfers between devices: 12.5 us -> 18.8 us  [swap(): return lax.ppermute(x, 'tp', [(j, j ^ k) for j in range(tp)])]
    pallas_call x1, Pallas kernels: 22.3 us -> 16.2 us  [cross_forward(): pl.pallas_call(functools.partial(cross_forward_body, tp), out_shape=(shap...]
    ppermute x26, waiting for transfers between devices: 25.6 us -> 31.7 us  [flip(): return lax.ppermute(x, axis, [(i, i ^ 1 << bit) for i in range(n)])]
    ppermute x12, waiting for transfers between devices: 73.2 us -> 79.2 us  [flip_x(): return lax.ppermute(v, 'x', [(0, 1), (1, 0)])]
  transfers between devices with their start and end apart: 50 -> 50, of which waited for: 17 -> 18; matrix products, arithmetic and copies ran while one was open for 14% -> 14% of each run, Pallas kernels for 34% -> 30%
where the time goes in v4:
time: 596 us; the launch traced here: 587 us
  Pallas kernels  203 us (34%)
  waiting for transfers between devices  182 us (31%)
  local copies, waits for them, and re-layouts  65.6 us (11%)
  starting transfers between devices  54 us (9%)
  other arithmetic  43.1 us (7%)
  between operations  39.4 us (7%)
    ppermute x12, waiting for transfers between devices, flip_x(): return lax.ppermute(v, 'x', [(0, 1), (1, 0)])  79.2 us
    pallas_call x4, Pallas kernels, cross_weights(): pl.pallas_call(lambda *refs: cross_weights_body(*refs[:n], *refs[-k:]), g...  34.7 us
    ppermute x26, waiting for transfers between devices, flip(): return lax.ppermute(x, axis, [(i, i ^ 1 << bit) for i in range(n)])  31.7 us
    select_n x23, other arithmetic, after(): return jnp.where(ok, x, jnp.zeros_like(x))  29.4 us
    pallas_call x2, Pallas kernels, feed(): pl.pallas_call(feed_body, out_shape=(shape((2, rows, ff), BF), shape((2,...  28.5 us
    pallas_call x1, Pallas kernels, cross_backward(): pl.pallas_call(functools.partial(cross_backward_body, tp), out_shape=(sha...  26.8 us
    psum x3, waiting for transfers between devices, sum_z(): return lax.psum(v, 'z')  25.5 us
    unnamed x163, local copies, waits for them, and re-layouts  19.8 us
  transfers between devices with their start and end apart: 50, of which 18 were waited for; matrix products, arithmetic and copies ran while one was open for 14% of the time, Pallas kernels for 30%

profile of v4, /device:TPU:0, one launch (start us, length us, event | category | flops | bytes accessed | tf_op | source)
XLA Modules:
  0.0 587.3 jit_solution(18241249750939126947)
XLA Ops:
  21.5 5.1 all-to-all-start
  26.5 15.9 %collective-permute-done.came0.refs_6_ = bf16[512,1024]{1,0:T(8,128)(2,1)} collective-permute-done((bf16[512,1024]{1,0:T(8,128)(2,1)}, bf16[512,1024]{1,0:T(8,128)(2,1)}, u32[]{:S(2)}, u32[]{:S(2)}) %collective-permute-start) | collective-permute-done | bytes 1048608 | tf_op jit(solution)/shard_map/ppermute | solution.py:963
  53.3 13.6 %keys_values.1.kv = bf16[2048,2048]{1,0:T(8,128)(2,1)} custom-call(bf16[2048,1024]{1,0:T(8,128)(2,1)} %refs_5_.7, bf16[512,1024]{1,0:T(8,128)(2,1)} %collective-permute-done.came0.refs_6_, bf16[512,1024]{1,0:T(8,128)(2,1)} %collective-permute-done.1.came1.refs_7_, bf16[1024,512]{1,0:T(8,128)(2,1)} %copy-done.11, ...), custom_call_target="tpu_custom_call" | custom-call | flops 15399999488 | bytes 14000000 | tf_op jit(solution)/shard_map/keys_values/pallas_call | solution.py:283
  69.5 8.2 %collective-permute-done.9.refs_2_ = bf16[1024,512]{1,0:T(8,128)(2,1)S(1)} collective-permute-done((bf16[1024,512]{1,0:T(8,128)(2,1)S(1)}, bf16[1024,512]{1,0:T(8,128)(2,1)S(1)}, u32[]{:S(2)}, u32[]{:S(2)}) %collective-permute-start.9) | collective-permute-done | bytes 1048608 | tf_op jit(solution)/shard_map/ppermute | solution.py:824
  94.7 6.1 %all-to-all-start.1 = ((bf16[32,4,16,256]{3,1,2,0:T(4,128)(2,1)}), bf16[32,4,16,256]{3,1,2,0:T(4,128)(2,1)}, u32[]{:S(2)}, u32[]{:S(2)}) async-start(bf16[32,4,16,256]{3,1,2,0:T(4,128)(2,1)} %bitcast.188), calls=%async_computation.1 | async-start | bytes 2097152 | tf_op jit(solution)/shard_map/all_to_all | solution.py:905
  100.9 16.2 %cross_forward.1 = (bf16[512,1024]{1,0:T(8,128)(2,1)}, bf16[512,1024]{1,0:T(8,128)(2,1)}, f32[512,1024]{1,0:T(8,128)}, bf16[512,1024]{1,0:T(8,128)(2,1)}, bf16[512,1024]{1,0:T(8,128)(2,1)}) custom-call(s32[16]{0:T(128)} %compare_select_fusion.1.idx, s32[16]{0:T(128)} %gather_fusion, f32[512,1024]{1,0:T(8,128)} %copy-done.55, f32[1,1024]{1,0:T(1,128)} %bitcast.225, ...), custom_call_target="tpu_custom_call" | custom-call | flops 22000001024 | bytes 20000000 | tf_op jit(solution)/shard_map/cross_forward/pallas_call | solution.py:358
  119.6 13.0 %collective-permute-done.12.refs_2_.refs_3_ = bf16[1024,1024]{1,0:T(8,128)(2,1)S(1)} collective-permute-done((bf16[1024,1024]{1,0:T(8,128)(2,1)}, bf16[1024,1024]{1,0:T(8,128)(2,1)S(1)}, u32[]{:S(2)}, u32[]{:S(2)}) %collective-permute-start.12) | collective-permute-done | bytes 2097184 | tf_op jit(solution)/shard_map/ppermute | solution.py:824
  139.1 11.0 %self_forward.1 = (bf16[512,3072]{1,0:T(8,128)(2,1)S(1)}, bf16[512,1024]{1,0:T(8,128)(2,1)S(1)}, f32[512,1024]{1,0:T(8,128)S(1)}, bf16[512,1024]{1,0:T(8,128)(2,1)S(1)}) custom-call(bf16[512,1024]{1,0:T(8,128)(2,1)S(1)} %copy-done.31, f32[512,1024]{1,0:T(8,128)S(1)} %copy-done.29, f32[1,1024]{1,0:T(1,128)S(1)} %bitcast.179, f32[1,1024]{1,0:T(1,128)S(1)} %bitcast.176, ...), custom_call_target="tpu_custom_call" | custom-call | flops 24199999488 | bytes 22000000 | tf_op jit(solution)/shard_map/self_forward/pallas_call | solution.py:424
  155.2 8.2 %collective-permute-done.16.refs_0_.cot.refs_3_ = bf16[512,1024]{1,0:T(8,128)(2,1)S(1)} collective-permute-done((bf16[512,1024]{1,0:T(8,128)(2,1)S(1)}, bf16[512,1024]{1,0:T(8,128)(2,1)S(1)}, u32[]{:S(2)}, u32[]{:S(2)}) %collective-permute-start.16) | collective-permute-done | bytes 1048608 | tf_op jit(solution)/shard_map/ppermute | solution.py:1011
  163.4 14.1 %feed.2 = (bf16[2,512,1024]{2,1,0:T(8,128)(2,1)S(1)}, bf16[2,512,1024]{2,1,0:T(8,128)(2,1)S(1)}, f32[512,1024]{1,0:T(8,128)S(1)}, f32[512,1024]{1,0:T(8,128)S(1)}, f32[2,1024]{1,0:T(2,128)S(1)}) custom-call(bf16[512,1024]{1,0:T(8,128)(2,1)S(1)} %get-tuple-element.67.nm.refs_2_, bf16[512,1024]{1,0:T(8,128)(2,1)S(1)} %bitcast.171, ...), custom_call_target="tpu_custom_call" | custom-call | flops 16499999744 | bytes 15000000 | tf_op jit(solution)/shard_map/feed/pallas_call | solution.py:475
  180.3 5.3 collective-permute-done.17.nm.refs_3_
  185.5 14.3 %feed.3 = (bf16[2,512,1024]{2,1,0:T(8,128)(2,1)S(1)}, bf16[2,512,1024]{2,1,0:T(8,128)(2,1)S(1)}, bf16[512,1024]{1,0:T(8,128)(2,1)S(1)}, bf16[512,1024]{1,0:T(8,128)(2,1)S(1)}, f32[2,1024]{1,0:T(2,128)S(1)}) custom-call(bf16[512,1024]{1,0:T(8,128)(2,1)S(1)} %collective-permute-done.17.nm.refs_3_, ...), custom_call_target="tpu_custom_call" | custom-call | flops 16499999744 | bytes 15000000 | tf_op jit(solution)/shard_map/feed/pallas_call | solution.py:475
  230.0 5.3 collective-permute-done.18.refs_0_
  235.3 17.2 %self_backward.1 = (bf16[512,1024]{1,0:T(8,128)(2,1)S(1)}, bf16[512,3072]{1,0:T(8,128)(2,1)}, f32[512,1024]{1,0:T(8,128)S(1)}, bf16[512,1024]{1,0:T(8,128)(2,1)S(1)}, f32[8,1024]{1,0:T(8,128)S(1)}) custom-call(bf16[512,1024]{1,0:T(8,128)(2,1)S(1)} %bitcast.174, f32[512,1024]{1,0:T(8,128)S(1)} %copy-done.43, f32[512,1024]{1,0:T(8,128)} %copy-done.7, ...), custom_call_target="tpu_custom_call" | custom-call | flops 29699999744 | bytes 27000000 | tf_op jit(solution)/shard_map/self_backward/pallas_call | solution.py:598
  256.5 9.7 %collective-permute-done.23 = bf16[4,128,1024]{2,1,0:T(8,128)(2,1)S(1)} collective-permute-done((bf16[4,128,1024]{2,1,0:T(8,128)(2,1)S(1)}, bf16[4,128,1024]{2,1,0:T(8,128)(2,1)S(1)}, u32[]{:S(2)}, u32[]{:S(2)}) %collective-permute-start.23) | collective-permute-done | bytes 1048608 | tf_op jit(solution)/shard_map/ppermute | solution.py:880
  282.1 5.2 self_weights.6.refs_5_
  293.0 5.7 all-to-all-start.2
  298.7 5.2 self_weights.7.refs_6_
  304.0 26.8 %cross_backward.1 = (bf16[512,1024]{1,0:T(8,128)(2,1)}, bf16[2048,2048]{1,0:T(8,128)(2,1)}, bf16[512,1024]{1,0:T(8,128)(2,1)}, f32[128,1024]{1,0:T(8,128)}, f32[8,1024]{1,0:T(8,128)}) custom-call(s32[16]{0:T(128)} %compare_select_fusion.1.idx, s32[16]{0:T(128)} %gather_fusion, bf16[512,1024]{1,0:T(8,128)(2,1)} %copy-done.33, f32[512,1024]{1,0:T(8,128)} %copy-done.45, ...), custom_call_target="tpu_custom_call" | custom-call | flops 38499999744 | bytes 35000000 | tf_op jit(solution)/shard_map/cross_backward/pallas_call | solution.py:704
  336.2 10.4 %all-to-all-done.2 = bf16[32,4,16,256]{3,1,2,0:T(4,128)(2,1)S(1)} async-done(((bf16[32,4,16,256]{3,1,2,0:T(4,128)(2,1)}), bf16[32,4,16,256]{3,1,2,0:T(4,128)(2,1)S(1)}, u32[]{:S(2)}, u32[]{:S(2)}) %all-to-all-start.2) | async-done | bytes 1048608 | tf_op jit(solution)/shard_map/all_to_all | solution.py:916
  353.0 8.7 %cross_weights.4.refs_8_ = bf16[1024,1024]{1,0:T(8,128)(2,1)} custom-call(bf16[512,1024]{1,0:T(8,128)(2,1)} %get-tuple-element.64.refs_0_, bf16[512,1024]{1,0:T(8,128)(2,1)} %get-tuple-element.84.refs_1_, bf16[512,1024]{1,0:T(8,128)(2,1)} %get-tuple-element.85.refs_2_, bf16[512,1024]{1,0:T(8,128)(2,1)} %copy-done.33, ...), custom_call_target="tpu_custom_call" | custom-call | flops 8800000000 | bytes 8000000 | tf_op jit(solution)/shard_map/cross_weights/pallas_call | solution.py:800
  364.6 8.4 %cross_weights.5.refs_12_ = bf16[1024,1024]{1,0:T(8,128)(2,1)} custom-call(bf16[512,1024]{1,0:T(8,128)(2,1)} %get-tuple-element.64.refs_0_, bf16[512,1024]{1,0:T(8,128)(2,1)} %get-tuple-element.84.refs_1_, bf16[512,1024]{1,0:T(8,128)(2,1)} %get-tuple-element.85.refs_2_, bf16[512,1024]{1,0:T(8,128)(2,1)} %copy-done.33, ...), custom_call_target="tpu_custom_call" | custom-call | flops 8800000000 | bytes 8000000 | tf_op jit(solution)/shard_map/cross_weights/pallas_call | solution.py:800
  385.6 8.0 %collective-permute-done.28 = bf16[4,64,1024]{2,1,0:T(8,128)(2,1)} collective-permute-done((bf16[4,64,1024]{2,1,0:T(8,128)(2,1)}, bf16[4,64,1024]{2,1,0:T(8,128)(2,1)}, u32[]{:S(2)}, u32[]{:S(2)}) %collective-permute-start.28) | collective-permute-done | bytes 524320 | tf_op jit(solution)/shard_map/ppermute | solution.py:880
  395.6 8.8 %cross_weights.6 = (bf16[512,1024]{1,0:T(8,128)(2,1)}, bf16[512,1024]{1,0:T(8,128)(2,1)}) custom-call(bf16[512,1024]{1,0:T(8,128)(2,1)} %get-tuple-element.64.refs_0_, bf16[512,1024]{1,0:T(8,128)(2,1)} %get-tuple-element.84.refs_1_, bf16[512,1024]{1,0:T(8,128)(2,1)} %get-tuple-element.85.refs_2_, bf16[512,1024]{1,0:T(8,128)(2,1)} %copy-done.33, ...), custom_call_target="tpu_custom_call" | custom-call | flops 8800000000 | bytes 8000000 | tf_op jit(solution)/shard_map/cross_weights/pallas_call | solution.py:800
  422.1 8.8 %cross_weights.7 = (bf16[512,1024]{1,0:T(8,128)(2,1)}, bf16[512,1024]{1,0:T(8,128)(2,1)}) custom-call(bf16[512,1024]{1,0:T(8,128)(2,1)} %get-tuple-element.64.refs_0_, bf16[512,1024]{1,0:T(8,128)(2,1)} %get-tuple-element.84.refs_1_, bf16[512,1024]{1,0:T(8,128)(2,1)} %get-tuple-element.85.refs_2_, bf16[512,1024]{1,0:T(8,128)(2,1)} %copy-done.33, ...), custom_call_target="tpu_custom_call" | custom-call | flops 8800000000 | bytes 8000000 | tf_op jit(solution)/shard_map/cross_weights/pallas_call | solution.py:800
  433.2 7.1 %collective-permute-done.33 = bf16[512,1024]{1,0:T(8,128)(2,1)} collective-permute-done((bf16[512,1024]{1,0:T(8,128)(2,1)}, bf16[512,1024]{1,0:T(8,128)(2,1)}, u32[]{:S(2)}, u32[]{:S(2)}) %collective-permute-start.33) | collective-permute-done | bytes 1048608 | tf_op jit(solution)/shard_map/ppermute | solution.py:824
  453.2 20.6 %collective-permute-done.39 = bf16[4,8,1024]{2,1,0:T(8,128)(2,1)S(1)} collective-permute-done((bf16[4,8,1024]{2,1,0:T(8,128)(2,1)S(1)}, bf16[4,8,1024]{2,1,0:T(8,128)(2,1)S(1)}, u32[]{:S(2)}, u32[]{:S(2)}) %collective-permute-start.39) | collective-permute-done | bytes 65568 | tf_op jit(solution)/shard_map/ppermute | solution.py:880
  478.0 5.2 collective-permute-done.35
  496.1 21.8 %collective-permute-done.40.other = bf16[4,128,1024]{2,1,0:T(8,128)(2,1)} collective-permute-done((bf16[4,128,1024]{2,1,0:T(8,128)(2,1)}, bf16[4,128,1024]{2,1,0:T(8,128)(2,1)}, u32[]{:S(2)}, u32[]{:S(2)}) %collective-permute-start.40) | collective-permute-done | bytes 1048608 | tf_op jit(solution)/shard_map/ppermute | solution.py:880
  520.4 25.4 %all-reduce.11.cloned.1.call-done = bf16[4,136,1024]{2,1,0:T(8,128)(2,1)} async-done(((bf16[4,136,1024]{2,1,0:T(8,128)(2,1)}), bf16[4,136,1024]{2,1,0:T(8,128)(2,1)}) %all-reduce.11.cloned.1.call-update) | async-done | bytes 1114128 | tf_op jit(solution)/shard_map/psum | solution.py:897
  553.5 6.3 %final_feed.1 = (f32[1024,1024]{1,0:T(8,128)}, f32[1024,1024]{1,0:T(8,128)}) custom-call(s32[1]{0:T(128)} %bitcast.75.places, bf16[4,256,1024]{2,1,0:T(8,128)(2,1)} %all-reduce.7.cloned.1.call-done.refs_11_.own, bf16[4,128,1024]{2,1,0:T(8,128)(2,1)} %collective-permute-done.34.other_o, bf16[4,128,1024]{2,1,0:T(8,128)(2,1)} %copy-done.75), custom_call_target="tpu_custom_call" | custom-call | flops 6600000000 | bytes 6000000 | tf_op jit(solution)/shard_map/final_feed/pallas_call | solution.py:237
  559.8 14.0 %collective-permute-done.41.other = bf16[4,136,1024]{2,1,0:T(8,128)(2,1)S(1)} collective-permute-done((bf16[4,136,1024]{2,1,0:T(8,128)(2,1)S(1)}, bf16[4,136,1024]{2,1,0:T(8,128)(2,1)S(1)}, u32[]{:S(2)}, u32[]{:S(2)}) %collective-permute-start.41) | collective-permute-done | bytes 1114144 | tf_op jit(solution)/shard_map/ppermute | solution.py:880
  (377 shorter events, 188.2 us)
Async XLA Ops:
  9.6 32.9 %collective-permute-start = (bf16[512,1024]{1,0:T(8,128)(2,1)}, bf16[512,1024]{1,0:T(8,128)(2,1)}, u32[]{:S(2)}, u32[]{:S(2)}) collective-permute-start(bf16[512,1024]{1,0:T(8,128)(2,1)} %part_of.1), channel_id=1, source_target_pairs={{0,4},{4,8},{8,12},{12,16},{16,20},{20,24},{24,28},{28,0},{1,5},{5... | collective-permute-start | bytes 3145736 | tf_op jit(solution)/shard_map/ppermute | solution.py:963
  12.7 32.3 %collective-permute-start.3 = (bf16[1024,512]{1,0:T(8,128)(2,1)S(1)}, bf16[1024,512]{1,0:T(8,128)(2,1)}, u32[]{:S(2)}, u32[]{:S(2)}) collective-permute-start(bf16[1024,512]{1,0:T(8,128)(2,1)S(1)} %packed.3.refs_2_.refs_0_), channel_id=1, source_target_pairs={{0,2},{1,3},{2,0},{3,1},{4,6},{5,7},{6,4},{7,5},{8,10},{9,11},{10,... | collective-permute-start | bytes 3145736 | tf_op jit(solution)/shard_map/ppermute | solution.py:824
  14.3 36.1 %collective-permute-start.2 = (bf16[1024,512]{1,0:T(8,128)(2,1)S(1)}, bf16[1024,512]{1,0:T(8,128)(2,1)}, u32[]{:S(2)}, u32[]{:S(2)}) collective-permute-start(bf16[1024,512]{1,0:T(8,128)(2,1)S(1)} %packed.3.refs_2_.refs_0_), channel_id=1, source_target_pairs={{0,1},{1,0},{2,3},{3,2},{4,5},{5,4},{6,7},{7,6},{8,9},{9,8},{10,11... | collective-permute-start | bytes 3145736 | tf_op jit(solution)/shard_map/ppermute | solution.py:824
  16.2 53.2 %collective-permute-start.6 = (f32[135,256]{1,0:T(8,128)S(1)}, f32[135,256]{1,0:T(8,128)}, u32[]{:S(2)}, u32[]{:S(2)}) collective-permute-start(f32[135,256]{1,0:T(8,128)S(1)} %concatenate.18), channel_id=1, source_target_pairs={{0,2},{1,3},{2,0},{3,1},{4,6},{5,7},{6,4},{7,5},{8,10},{9,11},{10,... | collective-permute-start | bytes 414728 | tf_op jit(solution)/shard_map/ppermute | solution.py:824
  16.8 62.1 %collective-permute-start.5 = (f32[135,256]{1,0:T(8,128)S(1)}, f32[135,256]{1,0:T(8,128)S(1)}, u32[]{:S(2)}, u32[]{:S(2)}) collective-permute-start(f32[135,256]{1,0:T(8,128)S(1)} %concatenate.18), channel_id=1, source_target_pairs={{0,1},{1,0},{2,3},{3,2},{4,5},{5,4},{6,7},{7,6},{8,9},{9,8},{10,11... | collective-permute-start | bytes 414728 | tf_op jit(solution)/shard_map/ppermute | solution.py:824
  21.5 60.7 %all-to-all-start = ((bf16[32,4,16,256]{3,1,2,0:T(4,128)(2,1)}), bf16[32,4,16,256]{3,1,2,0:T(4,128)(2,1)}, u32[]{:S(2)}, u32[]{:S(2)}) async-start(bf16[32,4,16,256]{3,1,2,0:T(4,128)(2,1)} %bitcast.162), calls=%async_computation | async-start | bytes 2097152 | tf_op jit(solution)/shard_map/all_to_all | solution.py:905
  50.4 27.4 %collective-permute-start.9 = (bf16[1024,512]{1,0:T(8,128)(2,1)S(1)}, bf16[1024,512]{1,0:T(8,128)(2,1)S(1)}, u32[]{:S(2)}, u32[]{:S(2)}) collective-permute-start(bf16[1024,512]{1,0:T(8,128)(2,1)S(1)} %packed.4.refs_4_.refs_0_), channel_id=1, source_target_pairs={{0,2},{1,3},{2,0},{3,1},{4,6},{5,7},{6,4},{7,5},{8,10},{9,11},{10,... | collective-permute-start | bytes 3145736 | tf_op jit(solution)/shard_map/ppermute | solution.py:824
  52.7 48.2 %collective-permute-start.8 = (bf16[1024,512]{1,0:T(8,128)(2,1)S(1)}, bf16[1024,512]{1,0:T(8,128)(2,1)}, u32[]{:S(2)}, u32[]{:S(2)}) collective-permute-start(bf16[1024,512]{1,0:T(8,128)(2,1)S(1)} %packed.4.refs_4_.refs_0_), channel_id=1, source_target_pairs={{0,1},{1,0},{2,3},{3,2},{4,5},{5,4},{6,7},{7,6},{8,9},{9,8},{10,11... | collective-permute-start | bytes 3145736 | tf_op jit(solution)/shard_map/ppermute | solution.py:824
  52.9 79.6 %collective-permute-start.12 = (bf16[1024,1024]{1,0:T(8,128)(2,1)}, bf16[1024,1024]{1,0:T(8,128)(2,1)S(1)}, u32[]{:S(2)}, u32[]{:S(2)}) collective-permute-start(bf16[1024,1024]{1,0:T(8,128)(2,1)} %packed.5.refs_4_.refs_0_.refs_1_), channel_id=1, source_target_pairs={{0,2},{1,3},{2,0},{3,1},{4,6},{5,7},{6,4},{7,5},{8,10},{9,11},{10,... | collective-permute-start | bytes 6291464 | tf_op jit(solution)/shard_map/ppermute | solution.py:824
  69.4 69.6 %collective-permute-start.11 = (bf16[1024,1024]{1,0:T(8,128)(2,1)}, bf16[1024,1024]{1,0:T(8,128)(2,1)}, u32[]{:S(2)}, u32[]{:S(2)}) collective-permute-start(bf16[1024,1024]{1,0:T(8,128)(2,1)} %packed.5.refs_4_.refs_0_.refs_1_), channel_id=1, source_target_pairs={{0,1},{1,0},{2,3},{3,2},{4,5},{5,4},{6,7},{7,6},{8,9},{9,8},{10,11... | collective-permute-start | bytes 6291464 | tf_op jit(solution)/shard_map/ppermute | solution.py:824
  94.7 39.9 %all-to-all-start.1 = ((bf16[32,4,16,256]{3,1,2,0:T(4,128)(2,1)}), bf16[32,4,16,256]{3,1,2,0:T(4,128)(2,1)}, u32[]{:S(2)}, u32[]{:S(2)}) async-start(bf16[32,4,16,256]{3,1,2,0:T(4,128)(2,1)} %bitcast.188), calls=%async_computation.1 | async-start | bytes 2097152 | tf_op jit(solution)/shard_map/all_to_all | solution.py:905
  154.1 31.4 %collective-permute-start.17 = (bf16[512,1024]{1,0:T(8,128)(2,1)S(1)}, bf16[512,1024]{1,0:T(8,128)(2,1)S(1)}, u32[]{:S(2)}, u32[]{:S(2)}) collective-permute-start(bf16[512,1024]{1,0:T(8,128)(2,1)S(1)} %get-tuple-element.67.nm.refs_2_), channel_id=1, source_target_pairs={{0,2},{1,3},{2,0},{3,1},{4,6},{5,7},{6,4},{7,5},{8,10},{9,11},{10,... | collective-permute-start | bytes 3145736 | tf_op jit(solution)/shard_map/ppermute | solution.py:1011
  209.1 26.2 %collective-permute-start.18 = (bf16[512,1024]{1,0:T(8,128)(2,1)}, bf16[512,1024]{1,0:T(8,128)(2,1)S(1)}, u32[]{:S(2)}, u32[]{:S(2)}) collective-permute-start(bf16[512,1024]{1,0:T(8,128)(2,1)} %copy-done.18), channel_id=1, source_target_pairs={{0,2},{1,3},{2,0},{3,1},{4,6},{5,7},{6,4},{7,5},{8,10},{9,11},{10,... | collective-permute-start | bytes 3145736 | tf_op jit(solution)/shard_map/ppermute | solution.py:1011
  218.8 37.2 %collective-permute-start.22 = (bf16[4,128,1024]{2,1,0:T(8,128)(2,1)S(1)}, bf16[4,128,1024]{2,1,0:T(8,128)(2,1)S(1)}, u32[]{:S(2)}, u32[]{:S(2)}) collective-permute-start(bf16[4,128,1024]{2,1,0:T(8,128)(2,1)S(1)} %dynamic-slice_bitcast_fusion.1), channel_id=1, source_target_pairs={{0,4},{4,0},{1,5},{5,1},{2,6},{6,2},{3,7},{7,3},{8,12},{12,8},{9,1... | collective-permute-start | bytes 3145736 | tf_op jit(solution)/shard_map/ppermute | solution.py:880
  226.2 39.9 %collective-permute-start.23 = (bf16[4,128,1024]{2,1,0:T(8,128)(2,1)S(1)}, bf16[4,128,1024]{2,1,0:T(8,128)(2,1)S(1)}, u32[]{:S(2)}, u32[]{:S(2)}) collective-permute-start(bf16[4,128,1024]{2,1,0:T(8,128)(2,1)S(1)} %dynamic-slice_bitcast_fusion), channel_id=1, source_target_pairs={{0,4},{4,0},{1,5},{5,1},{2,6},{6,2},{3,7},{7,3},{8,12},{12,8},{9,1... | collective-permute-start | bytes 3145736 | tf_op jit(solution)/shard_map/ppermute | solution.py:880
  229.7 38.4 %collective-permute-start.21 = (bf16[512,1024]{1,0:T(8,128)(2,1)}, bf16[512,1024]{1,0:T(8,128)(2,1)}, u32[]{:S(2)}, u32[]{:S(2)}) collective-permute-start(bf16[512,1024]{1,0:T(8,128)(2,1)} %broadcast_select_fusion.5), channel_id=1, source_target_pairs={{0,2},{1,3},{2,0},{3,1},{4,6},{5,7},{6,4},{7,5},{8,10},{9,11},{10,... | collective-permute-start | bytes 3145736 | tf_op jit(solution)/shard_map/ppermute | solution.py:1011
  276.9 118.7 %all-reduce.7.cloned.1.call-start = ((), (), s32[]{:S(2)}) async-start(), calls=%async_computation.4 | async-start | bytes 4194304 | tf_op jit(solution)/shard_map/psum | solution.py:897
  287.4 61.1 %collective-permute-start.26 = (bf16[1024,1024]{1,0:T(8,128)(2,1)}, bf16[1024,1024]{1,0:T(8,128)(2,1)}, u32[]{:S(2)}, u32[]{:S(2)}) collective-permute-start(bf16[1024,1024]{1,0:T(8,128)(2,1)} %self_weights.6.refs_5_), channel_id=1, source_target_pairs={{0,2},{1,3},{2,0},{3,1},{4,6},{5,7},{6,4},{7,5},{8,10},{9,11},{10,... | collective-permute-start | bytes 6291464 | tf_op jit(solution)/shard_map/ppermute | solution.py:824
  293.0 53.6 %all-to-all-start.2 = ((bf16[32,4,16,256]{3,1,2,0:T(4,128)(2,1)}), bf16[32,4,16,256]{3,1,2,0:T(4,128)(2,1)S(1)}, u32[]{:S(2)}, u32[]{:S(2)}) async-start(bf16[32,4,16,256]{3,1,2,0:T(4,128)(2,1)} %bitcast.40), calls=%async_computation.2 | async-start | bytes 2097152 | tf_op jit(solution)/shard_map/all_to_all | solution.py:916
  361.7 33.9 %collective-permute-start.27 = (bf16[1024,1024]{1,0:T(8,128)(2,1)}, bf16[1024,1024]{1,0:T(8,128)(2,1)}, u32[]{:S(2)}, u32[]{:S(2)}) collective-permute-start(bf16[1024,1024]{1,0:T(8,128)(2,1)} %cross_weights.4.refs_8_), channel_id=1, source_target_pairs={{0,1},{1,0},{2,3},{3,2},{4,5},{5,4},{6,7},{7,6},{8,9},{9,8},{10,11... | collective-permute-start | bytes 6291464 | tf_op jit(solution)/shard_map/ppermute | solution.py:824
  374.2 47.9 %collective-permute-start.30 = (bf16[1024,1024]{1,0:T(8,128)(2,1)}, bf16[1024,1024]{1,0:T(8,128)(2,1)}, u32[]{:S(2)}, u32[]{:S(2)}) collective-permute-start(bf16[1024,1024]{1,0:T(8,128)(2,1)} %cross_weights.5.refs_12_), channel_id=1, source_target_pairs={{0,1},{1,0},{2,3},{3,2},{4,5},{5,4},{6,7},{7,6},{8,9},{9,8},{10,11... | collective-permute-start | bytes 6291464 | tf_op jit(solution)/shard_map/ppermute | solution.py:824
  379.7 33.4 %all-to-all-start.3 = ((bf16[32,4,16,256]{3,1,2,0:T(4,128)(2,1)}), bf16[32,4,16,256]{3,1,2,0:T(4,128)(2,1)S(1)}, u32[]{:S(2)}, u32[]{:S(2)}) async-start(bf16[32,4,16,256]{3,1,2,0:T(4,128)(2,1)} %bitcast.53), calls=%async_computation.3 | async-start | bytes 2097152 | tf_op jit(solution)/shard_map/all_to_all | solution.py:916
  383.5 90.4 %all-reduce.9.cloned.1.call-start = ((), (), s32[]{:S(2)}) async-start(), calls=%async_computation.5 | async-start | bytes 2097152 | tf_op jit(solution)/shard_map/psum | solution.py:897
  419.7 27.8 %collective-permute-start.37 = (bf16[4,64,1024]{2,1,0:T(8,128)(2,1)}, bf16[4,64,1024]{2,1,0:T(8,128)(2,1)}, u32[]{:S(2)}, u32[]{:S(2)}) collective-permute-start(bf16[4,64,1024]{2,1,0:T(8,128)(2,1)} %dynamic-slice_bitcast_fusion.2), channel_id=1, source_target_pairs={{0,4},{4,0},{1,5},{5,1},{2,6},{6,2},{3,7},{7,3},{8,12},{12,8},{9,1... | collective-permute-start | bytes 1572872 | tf_op jit(solution)/shard_map/ppermute | solution.py:880
  432.8 43.5 %collective-permute-start.36 = (bf16[4,64,1024]{2,1,0:T(8,128)(2,1)}, bf16[4,64,1024]{2,1,0:T(8,128)(2,1)}, u32[]{:S(2)}, u32[]{:S(2)}) collective-permute-start(bf16[4,64,1024]{2,1,0:T(8,128)(2,1)} %dynamic-slice_bitcast_fusion.3), channel_id=1, source_target_pairs={{0,4},{4,0},{1,5},{5,1},{2,6},{6,2},{3,7},{7,3},{8,12},{12,8},{9,1... | collective-permute-start | bytes 1572872 | tf_op jit(solution)/shard_map/ppermute | solution.py:880
  446.1 38.4 %collective-permute-start.34 = (bf16[4,128,1024]{2,1,0:T(8,128)(2,1)}, bf16[4,128,1024]{2,1,0:T(8,128)(2,1)}, u32[]{:S(2)}, u32[]{:S(2)}) collective-permute-start(bf16[4,128,1024]{2,1,0:T(8,128)(2,1)} %slice_select_fusion.1), channel_id=1, source_target_pairs={{0,4},{4,0},{1,5},{5,1},{2,6},{6,2},{3,7},{7,3},{8,12},{12,8},{9,1... | collective-permute-start | bytes 3145736 | tf_op jit(solution)/shard_map/ppermute | solution.py:880
  449.6 26.8 %collective-permute-start.38 = (bf16[4,64,1024]{2,1,0:T(8,128)(2,1)}, bf16[4,64,1024]{2,1,0:T(8,128)(2,1)}, u32[]{:S(2)}, u32[]{:S(2)}) collective-permute-start(bf16[4,64,1024]{2,1,0:T(8,128)(2,1)} %fusion.16), channel_id=1, source_target_pairs={{0,2},{1,3},{2,0},{3,1},{4,6},{5,7},{6,4},{7,5},{8,10},{9,11},{10,... | collective-permute-start | bytes 1572872 | tf_op jit(solution)/shard_map/ppermute | solution.py:824
  451.8 31.4 %collective-permute-start.35 = (bf16[4,64,1024]{2,1,0:T(8,128)(2,1)}, bf16[4,64,1024]{2,1,0:T(8,128)(2,1)}, u32[]{:S(2)}, u32[]{:S(2)}) collective-permute-start(bf16[4,64,1024]{2,1,0:T(8,128)(2,1)} %copy-done.67), channel_id=1, source_target_pairs={{0,4},{4,0},{1,5},{5,1},{2,6},{6,2},{3,7},{7,3},{8,12},{12,8},{9,1... | collective-permute-start | bytes 1572872 | tf_op jit(solution)/shard_map/ppermute | solution.py:880
  487.8 58.0 %all-reduce.11.cloned.1.call-start = ((), (), s32[]{:S(2)}) async-start(), calls=%async_computation.6 | async-start | bytes 2228224 | tf_op jit(solution)/shard_map/psum | solution.py:897
  491.5 26.4 %collective-permute-start.40 = (bf16[4,128,1024]{2,1,0:T(8,128)(2,1)}, bf16[4,128,1024]{2,1,0:T(8,128)(2,1)}, u32[]{:S(2)}, u32[]{:S(2)}) collective-permute-start(bf16[4,128,1024]{2,1,0:T(8,128)(2,1)} %broadcast_select_fusion.2), channel_id=1, source_target_pairs={{0,4},{4,0},{1,5},{5,1},{2,6},{6,2},{3,7},{7,3},{8,12},{12,8},{9,1... | collective-permute-start | bytes 3145736 | tf_op jit(solution)/shard_map/ppermute | solution.py:880
  494.0 58.6 %collective-permute-start.42 = (bf16[4,128,1024]{2,1,0:T(8,128)(2,1)}, bf16[4,128,1024]{2,1,0:T(8,128)(2,1)S(1)}, u32[]{:S(2)}, u32[]{:S(2)}) collective-permute-start(bf16[4,128,1024]{2,1,0:T(8,128)(2,1)} %slice_select_fusion), channel_id=1, source_target_pairs={{0,4},{4,0},{1,5},{5,1},{2,6},{6,2},{3,7},{7,3},{8,12},{12,8},{9,1... | collective-permute-start | bytes 3145736 | tf_op jit(solution)/shard_map/ppermute | solution.py:880
  547.2 26.6 %collective-permute-start.41 = (bf16[4,136,1024]{2,1,0:T(8,128)(2,1)S(1)}, bf16[4,136,1024]{2,1,0:T(8,128)(2,1)S(1)}, u32[]{:S(2)}, u32[]{:S(2)}) collective-permute-start(bf16[4,136,1024]{2,1,0:T(8,128)(2,1)S(1)} %broadcast_select_fusion.1.own), channel_id=1, source_target_pairs={{0,4},{4,0},{1,5},{5,1},{2,6},{6,2},{3,7},{7,3},{8,12},{12,8},{9,1... | collective-permute-start | bytes 3342344 | tf_op jit(solution)/shard_map/ppermute | solution.py:880
  (94 other events, 912.1 us)
Sparse Core Ops, SparseCore 0:
  282.2 112.2 all-reduce.6
  419.0 53.6 all-reduce.8
  491.5 54.2 all-reduce.10

commit v5 on v4

--- a/solution.py
+++ b/solution.py
@@ -1097,9 +1097,9 @@
         if p == tp - 1:
             stage["self"] = over_y(selfs, [emb])[0]
             stage["returned"] = from_groups(after(g0, *late), per)
-            return [stage["self"], restored]
+            return [stage["self"]]
         if p == tp - 3:
-            return []
+            return [restored]
         if p == tp - 2:
             n = stage["self"].shape[0] // 2
             stage["self"] = [over_x(stage["self"][:n], late), over_x(stage["self"][n:], late)]

time: 596 us -> 596 us (level)
  no operation moved by 1% of the time
where the time goes in v5:
time: 596 us; the launch traced here: 587 us
  Pallas kernels  203 us (34%)
  waiting for transfers between devices  182 us (31%)
  local copies, waits for them, and re-layouts  65.6 us (11%)
  starting transfers between devices  54 us (9%)
  other arithmetic  43.1 us (7%)
  between operations  39.4 us (7%)
    ppermute x12, waiting for transfers between devices, flip_x(): return lax.ppermute(v, 'x', [(0, 1), (1, 0)])  79.2 us
    pallas_call x4, Pallas kernels, cross_weights(): pl.pallas_call(lambda *refs: cross_weights_body(*refs[:n], *refs[-k:]), g...  34.7 us
    ppermute x26, waiting for transfers between devices, flip(): return lax.ppermute(x, axis, [(i, i ^ 1 << bit) for i in range(n)])  31.7 us
    select_n x23, other arithmetic, after(): return jnp.where(ok, x, jnp.zeros_like(x))  29.4 us
    pallas_call x2, Pallas kernels, feed(): pl.pallas_call(feed_body, out_shape=(shape((2, rows, ff), BF), shape((2,...  28.5 us
    pallas_call x1, Pallas kernels, cross_backward(): pl.pallas_call(functools.partial(cross_backward_body, tp), out_shape=(sha...  26.8 us
    psum x3, waiting for transfers between devices, sum_z(): return lax.psum(v, 'z')  25.5 us
    unnamed x163, local copies, waits for them, and re-layouts  19.8 us
  transfers between devices with their start and end apart: 50, of which 18 were waited for; matrix products, arithmetic and copies ran while one was open for 14% of the time, Pallas kernels for 30%

profile of v5, /device:TPU:0, one launch (start us, length us, event | category | flops | bytes accessed | tf_op | source)
XLA Modules:
  0.0 587.3 jit_solution(2771996392903050209)
XLA Ops:
  21.5 5.1 all-to-all-start
  26.5 15.9 %collective-permute-done.came0.refs_6_ = bf16[512,1024]{1,0:T(8,128)(2,1)} collective-permute-done((bf16[512,1024]{1,0:T(8,128)(2,1)}, bf16[512,1024]{1,0:T(8,128)(2,1)}, u32[]{:S(2)}, u32[]{:S(2)}) %collective-permute-start) | collective-permute-done | bytes 1048608 | tf_op jit(solution)/shard_map/ppermute | solution.py:963
  53.3 13.6 %keys_values.1.kv = bf16[2048,2048]{1,0:T(8,128)(2,1)} custom-call(bf16[2048,1024]{1,0:T(8,128)(2,1)} %refs_5_.7, bf16[512,1024]{1,0:T(8,128)(2,1)} %collective-permute-done.came0.refs_6_, bf16[512,1024]{1,0:T(8,128)(2,1)} %collective-permute-done.1.came1.refs_7_, bf16[1024,512]{1,0:T(8,128)(2,1)} %copy-done.11, ...), custom_call_target="tpu_custom_call" | custom-call | flops 15399999488 | bytes 14000000 | tf_op jit(solution)/shard_map/keys_values/pallas_call | solution.py:283
  69.5 8.2 %collective-permute-done.9.refs_2_ = bf16[1024,512]{1,0:T(8,128)(2,1)S(1)} collective-permute-done((bf16[1024,512]{1,0:T(8,128)(2,1)S(1)}, bf16[1024,512]{1,0:T(8,128)(2,1)S(1)}, u32[]{:S(2)}, u32[]{:S(2)}) %collective-permute-start.9) | collective-permute-done | bytes 1048608 | tf_op jit(solution)/shard_map/ppermute | solution.py:824
  94.7 6.1 %all-to-all-start.1 = ((bf16[32,4,16,256]{3,1,2,0:T(4,128)(2,1)}), bf16[32,4,16,256]{3,1,2,0:T(4,128)(2,1)}, u32[]{:S(2)}, u32[]{:S(2)}) async-start(bf16[32,4,16,256]{3,1,2,0:T(4,128)(2,1)} %bitcast.188), calls=%async_computation.1 | async-start | bytes 2097152 | tf_op jit(solution)/shard_map/all_to_all | solution.py:905
  100.9 16.2 %cross_forward.1 = (bf16[512,1024]{1,0:T(8,128)(2,1)}, bf16[512,1024]{1,0:T(8,128)(2,1)}, f32[512,1024]{1,0:T(8,128)}, bf16[512,1024]{1,0:T(8,128)(2,1)}, bf16[512,1024]{1,0:T(8,128)(2,1)}) custom-call(s32[16]{0:T(128)} %compare_select_fusion.1.idx, s32[16]{0:T(128)} %gather_fusion, f32[512,1024]{1,0:T(8,128)} %copy-done.55, f32[1,1024]{1,0:T(1,128)} %bitcast.225, ...), custom_call_target="tpu_custom_call" | custom-call | flops 22000001024 | bytes 20000000 | tf_op jit(solution)/shard_map/cross_forward/pallas_call | solution.py:358
  119.6 13.0 %collective-permute-done.12.refs_2_.refs_3_ = bf16[1024,1024]{1,0:T(8,128)(2,1)S(1)} collective-permute-done((bf16[1024,1024]{1,0:T(8,128)(2,1)}, bf16[1024,1024]{1,0:T(8,128)(2,1)S(1)}, u32[]{:S(2)}, u32[]{:S(2)}) %collective-permute-start.12) | collective-permute-done | bytes 2097184 | tf_op jit(solution)/shard_map/ppermute | solution.py:824
  139.1 11.0 %self_forward.1 = (bf16[512,3072]{1,0:T(8,128)(2,1)S(1)}, bf16[512,1024]{1,0:T(8,128)(2,1)S(1)}, f32[512,1024]{1,0:T(8,128)S(1)}, bf16[512,1024]{1,0:T(8,128)(2,1)S(1)}) custom-call(bf16[512,1024]{1,0:T(8,128)(2,1)S(1)} %copy-done.31, f32[512,1024]{1,0:T(8,128)S(1)} %copy-done.29, f32[1,1024]{1,0:T(1,128)S(1)} %bitcast.179, f32[1,1024]{1,0:T(1,128)S(1)} %bitcast.176, ...), custom_call_target="tpu_custom_call" | custom-call | flops 24199999488 | bytes 22000000 | tf_op jit(solution)/shard_map/self_forward/pallas_call | solution.py:424
  155.2 8.2 %collective-permute-done.16.refs_0_.cot.refs_3_ = bf16[512,1024]{1,0:T(8,128)(2,1)S(1)} collective-permute-done((bf16[512,1024]{1,0:T(8,128)(2,1)S(1)}, bf16[512,1024]{1,0:T(8,128)(2,1)S(1)}, u32[]{:S(2)}, u32[]{:S(2)}) %collective-permute-start.16) | collective-permute-done | bytes 1048608 | tf_op jit(solution)/shard_map/ppermute | solution.py:1011
  163.4 14.1 %feed.2 = (bf16[2,512,1024]{2,1,0:T(8,128)(2,1)S(1)}, bf16[2,512,1024]{2,1,0:T(8,128)(2,1)S(1)}, f32[512,1024]{1,0:T(8,128)S(1)}, f32[512,1024]{1,0:T(8,128)S(1)}, f32[2,1024]{1,0:T(2,128)S(1)}) custom-call(bf16[512,1024]{1,0:T(8,128)(2,1)S(1)} %get-tuple-element.67.nm.refs_2_, bf16[512,1024]{1,0:T(8,128)(2,1)S(1)} %bitcast.171, ...), custom_call_target="tpu_custom_call" | custom-call | flops 16499999744 | bytes 15000000 | tf_op jit(solution)/shard_map/feed/pallas_call | solution.py:475
  180.3 5.3 collective-permute-done.17.nm.refs_3_
  185.5 14.3 %feed.3 = (bf16[2,512,1024]{2,1,0:T(8,128)(2,1)S(1)}, bf16[2,512,1024]{2,1,0:T(8,128)(2,1)S(1)}, bf16[512,1024]{1,0:T(8,128)(2,1)S(1)}, bf16[512,1024]{1,0:T(8,128)(2,1)S(1)}, f32[2,1024]{1,0:T(2,128)S(1)}) custom-call(bf16[512,1024]{1,0:T(8,128)(2,1)S(1)} %collective-permute-done.17.nm.refs_3_, ...), custom_call_target="tpu_custom_call" | custom-call | flops 16499999744 | bytes 15000000 | tf_op jit(solution)/shard_map/feed/pallas_call | solution.py:475
  230.0 5.3 collective-permute-done.18.refs_0_
  235.3 17.2 %self_backward.1 = (bf16[512,1024]{1,0:T(8,128)(2,1)S(1)}, bf16[512,3072]{1,0:T(8,128)(2,1)}, f32[512,1024]{1,0:T(8,128)S(1)}, bf16[512,1024]{1,0:T(8,128)(2,1)S(1)}, f32[8,1024]{1,0:T(8,128)S(1)}) custom-call(bf16[512,1024]{1,0:T(8,128)(2,1)S(1)} %bitcast.174, f32[512,1024]{1,0:T(8,128)S(1)} %copy-done.43, f32[512,1024]{1,0:T(8,128)} %copy-done.7, ...), custom_call_target="tpu_custom_call" | custom-call | flops 29699999744 | bytes 27000000 | tf_op jit(solution)/shard_map/self_backward/pallas_call | solution.py:598
  256.5 9.7 %collective-permute-done.23 = bf16[4,128,1024]{2,1,0:T(8,128)(2,1)S(1)} collective-permute-done((bf16[4,128,1024]{2,1,0:T(8,128)(2,1)S(1)}, bf16[4,128,1024]{2,1,0:T(8,128)(2,1)S(1)}, u32[]{:S(2)}, u32[]{:S(2)}) %collective-permute-start.23) | collective-permute-done | bytes 1048608 | tf_op jit(solution)/shard_map/ppermute | solution.py:880
  282.1 5.2 self_weights.6.refs_5_
  293.0 5.7 all-to-all-start.2
  298.7 5.2 self_weights.7.refs_6_
  304.0 26.8 %cross_backward.1 = (bf16[512,1024]{1,0:T(8,128)(2,1)}, bf16[2048,2048]{1,0:T(8,128)(2,1)}, bf16[512,1024]{1,0:T(8,128)(2,1)}, f32[128,1024]{1,0:T(8,128)}, f32[8,1024]{1,0:T(8,128)}) custom-call(s32[16]{0:T(128)} %compare_select_fusion.1.idx, s32[16]{0:T(128)} %gather_fusion, bf16[512,1024]{1,0:T(8,128)(2,1)} %copy-done.33, f32[512,1024]{1,0:T(8,128)} %copy-done.45, ...), custom_call_target="tpu_custom_call" | custom-call | flops 38499999744 | bytes 35000000 | tf_op jit(solution)/shard_map/cross_backward/pallas_call | solution.py:704
  336.2 10.4 %all-to-all-done.2 = bf16[32,4,16,256]{3,1,2,0:T(4,128)(2,1)S(1)} async-done(((bf16[32,4,16,256]{3,1,2,0:T(4,128)(2,1)}), bf16[32,4,16,256]{3,1,2,0:T(4,128)(2,1)S(1)}, u32[]{:S(2)}, u32[]{:S(2)}) %all-to-all-start.2) | async-done | bytes 1048608 | tf_op jit(solution)/shard_map/all_to_all | solution.py:916
  353.0 8.7 %cross_weights.4.refs_9_ = bf16[1024,1024]{1,0:T(8,128)(2,1)} custom-call(bf16[512,1024]{1,0:T(8,128)(2,1)} %get-tuple-element.64.refs_0_, bf16[512,1024]{1,0:T(8,128)(2,1)} %get-tuple-element.84.refs_1_, bf16[512,1024]{1,0:T(8,128)(2,1)} %get-tuple-element.85.refs_2_, bf16[512,1024]{1,0:T(8,128)(2,1)} %copy-done.33, ...), custom_call_target="tpu_custom_call" | custom-call | flops 8800000000 | bytes 8000000 | tf_op jit(solution)/shard_map/cross_weights/pallas_call | solution.py:800
  364.6 8.4 %cross_weights.5.refs_12_ = bf16[1024,1024]{1,0:T(8,128)(2,1)} custom-call(bf16[512,1024]{1,0:T(8,128)(2,1)} %get-tuple-element.64.refs_0_, bf16[512,1024]{1,0:T(8,128)(2,1)} %get-tuple-element.84.refs_1_, bf16[512,1024]{1,0:T(8,128)(2,1)} %get-tuple-element.85.refs_2_, bf16[512,1024]{1,0:T(8,128)(2,1)} %copy-done.33, ...), custom_call_target="tpu_custom_call" | custom-call | flops 8800000000 | bytes 8000000 | tf_op jit(solution)/shard_map/cross_weights/pallas_call | solution.py:800
  385.6 8.0 %collective-permute-done.28 = bf16[4,64,1024]{2,1,0:T(8,128)(2,1)} collective-permute-done((bf16[4,64,1024]{2,1,0:T(8,128)(2,1)}, bf16[4,64,1024]{2,1,0:T(8,128)(2,1)}, u32[]{:S(2)}, u32[]{:S(2)}) %collective-permute-start.28) | collective-permute-done | bytes 524320 | tf_op jit(solution)/shard_map/ppermute | solution.py:880
  395.6 8.8 %cross_weights.6 = (bf16[512,1024]{1,0:T(8,128)(2,1)}, bf16[512,1024]{1,0:T(8,128)(2,1)}) custom-call(bf16[512,1024]{1,0:T(8,128)(2,1)} %get-tuple-element.64.refs_0_, bf16[512,1024]{1,0:T(8,128)(2,1)} %get-tuple-element.84.refs_1_, bf16[512,1024]{1,0:T(8,128)(2,1)} %get-tuple-element.85.refs_2_, bf16[512,1024]{1,0:T(8,128)(2,1)} %copy-done.33, ...), custom_call_target="tpu_custom_call" | custom-call | flops 8800000000 | bytes 8000000 | tf_op jit(solution)/shard_map/cross_weights/pallas_call | solution.py:800
  422.1 8.8 %cross_weights.7 = (bf16[512,1024]{1,0:T(8,128)(2,1)}, bf16[512,1024]{1,0:T(8,128)(2,1)}) custom-call(bf16[512,1024]{1,0:T(8,128)(2,1)} %get-tuple-element.64.refs_0_, bf16[512,1024]{1,0:T(8,128)(2,1)} %get-tuple-element.84.refs_1_, bf16[512,1024]{1,0:T(8,128)(2,1)} %get-tuple-element.85.refs_2_, bf16[512,1024]{1,0:T(8,128)(2,1)} %copy-done.33, ...), custom_call_target="tpu_custom_call" | custom-call | flops 8800000000 | bytes 8000000 | tf_op jit(solution)/shard_map/cross_weights/pallas_call | solution.py:800
  433.2 7.1 %collective-permute-done.33 = bf16[512,1024]{1,0:T(8,128)(2,1)} collective-permute-done((bf16[512,1024]{1,0:T(8,128)(2,1)}, bf16[512,1024]{1,0:T(8,128)(2,1)}, u32[]{:S(2)}, u32[]{:S(2)}) %collective-permute-start.33) | collective-permute-done | bytes 1048608 | tf_op jit(solution)/shard_map/ppermute | solution.py:824
  453.2 20.6 %collective-permute-done.39 = bf16[4,8,1024]{2,1,0:T(8,128)(2,1)S(1)} collective-permute-done((bf16[4,8,1024]{2,1,0:T(8,128)(2,1)S(1)}, bf16[4,8,1024]{2,1,0:T(8,128)(2,1)S(1)}, u32[]{:S(2)}, u32[]{:S(2)}) %collective-permute-start.39) | collective-permute-done | bytes 65568 | tf_op jit(solution)/shard_map/ppermute | solution.py:880
  478.0 5.2 collective-permute-done.35
  496.1 21.8 %collective-permute-done.40.other = bf16[4,128,1024]{2,1,0:T(8,128)(2,1)} collective-permute-done((bf16[4,128,1024]{2,1,0:T(8,128)(2,1)}, bf16[4,128,1024]{2,1,0:T(8,128)(2,1)}, u32[]{:S(2)}, u32[]{:S(2)}) %collective-permute-start.40) | collective-permute-done | bytes 1048608 | tf_op jit(solution)/shard_map/ppermute | solution.py:880
  520.4 25.4 %all-reduce.11.cloned.1.call-done = bf16[4,136,1024]{2,1,0:T(8,128)(2,1)} async-done(((bf16[4,136,1024]{2,1,0:T(8,128)(2,1)}), bf16[4,136,1024]{2,1,0:T(8,128)(2,1)}) %all-reduce.11.cloned.1.call-update) | async-done | bytes 1114128 | tf_op jit(solution)/shard_map/psum | solution.py:897
  553.5 6.3 %final_feed.1 = (f32[1024,1024]{1,0:T(8,128)}, f32[1024,1024]{1,0:T(8,128)}) custom-call(s32[1]{0:T(128)} %bitcast.75.places, bf16[4,256,1024]{2,1,0:T(8,128)(2,1)} %all-reduce.7.cloned.1.call-done.refs_11_.own, bf16[4,128,1024]{2,1,0:T(8,128)(2,1)} %collective-permute-done.34.other_o, bf16[4,128,1024]{2,1,0:T(8,128)(2,1)} %copy-done.75), custom_call_target="tpu_custom_call" | custom-call | flops 6600000000 | bytes 6000000 | tf_op jit(solution)/shard_map/final_feed/pallas_call | solution.py:237
  559.8 14.0 %collective-permute-done.41.other = bf16[4,136,1024]{2,1,0:T(8,128)(2,1)S(1)} collective-permute-done((bf16[4,136,1024]{2,1,0:T(8,128)(2,1)S(1)}, bf16[4,136,1024]{2,1,0:T(8,128)(2,1)S(1)}, u32[]{:S(2)}, u32[]{:S(2)}) %collective-permute-start.41) | collective-permute-done | bytes 1114144 | tf_op jit(solution)/shard_map/ppermute | solution.py:880
  (377 shorter events, 188.2 us)
Async XLA Ops:
  9.6 32.9 %collective-permute-start = (bf16[512,1024]{1,0:T(8,128)(2,1)}, bf16[512,1024]{1,0:T(8,128)(2,1)}, u32[]{:S(2)}, u32[]{:S(2)}) collective-permute-start(bf16[512,1024]{1,0:T(8,128)(2,1)} %part_of.1), channel_id=1, source_target_pairs={{0,4},{4,8},{8,12},{12,16},{16,20},{20,24},{24,28},{28,0},{1,5},{5... | collective-permute-start | bytes 3145736 | tf_op jit(solution)/shard_map/ppermute | solution.py:963
  12.7 32.3 %collective-permute-start.3 = (bf16[1024,512]{1,0:T(8,128)(2,1)S(1)}, bf16[1024,512]{1,0:T(8,128)(2,1)}, u32[]{:S(2)}, u32[]{:S(2)}) collective-permute-start(bf16[1024,512]{1,0:T(8,128)(2,1)S(1)} %packed.3.refs_2_.refs_0_), channel_id=1, source_target_pairs={{0,2},{1,3},{2,0},{3,1},{4,6},{5,7},{6,4},{7,5},{8,10},{9,11},{10,... | collective-permute-start | bytes 3145736 | tf_op jit(solution)/shard_map/ppermute | solution.py:824
  14.3 36.1 %collective-permute-start.2 = (bf16[1024,512]{1,0:T(8,128)(2,1)S(1)}, bf16[1024,512]{1,0:T(8,128)(2,1)}, u32[]{:S(2)}, u32[]{:S(2)}) collective-permute-start(bf16[1024,512]{1,0:T(8,128)(2,1)S(1)} %packed.3.refs_2_.refs_0_), channel_id=1, source_target_pairs={{0,1},{1,0},{2,3},{3,2},{4,5},{5,4},{6,7},{7,6},{8,9},{9,8},{10,11... | collective-permute-start | bytes 3145736 | tf_op jit(solution)/shard_map/ppermute | solution.py:824
  16.2 53.2 %collective-permute-start.6 = (f32[135,256]{1,0:T(8,128)S(1)}, f32[135,256]{1,0:T(8,128)}, u32[]{:S(2)}, u32[]{:S(2)}) collective-permute-start(f32[135,256]{1,0:T(8,128)S(1)} %concatenate.18), channel_id=1, source_target_pairs={{0,2},{1,3},{2,0},{3,1},{4,6},{5,7},{6,4},{7,5},{8,10},{9,11},{10,... | collective-permute-start | bytes 414728 | tf_op jit(solution)/shard_map/ppermute | solution.py:824
  16.8 62.1 %collective-permute-start.5 = (f32[135,256]{1,0:T(8,128)S(1)}, f32[135,256]{1,0:T(8,128)S(1)}, u32[]{:S(2)}, u32[]{:S(2)}) collective-permute-start(f32[135,256]{1,0:T(8,128)S(1)} %concatenate.18), channel_id=1, source_target_pairs={{0,1},{1,0},{2,3},{3,2},{4,5},{5,4},{6,7},{7,6},{8,9},{9,8},{10,11... | collective-permute-start | bytes 414728 | tf_op jit(solution)/shard_map/ppermute | solution.py:824
  21.5 60.7 %all-to-all-start = ((bf16[32,4,16,256]{3,1,2,0:T(4,128)(2,1)}), bf16[32,4,16,256]{3,1,2,0:T(4,128)(2,1)}, u32[]{:S(2)}, u32[]{:S(2)}) async-start(bf16[32,4,16,256]{3,1,2,0:T(4,128)(2,1)} %bitcast.162), calls=%async_computation | async-start | bytes 2097152 | tf_op jit(solution)/shard_map/all_to_all | solution.py:905
  50.4 27.4 %collective-permute-start.9 = (bf16[1024,512]{1,0:T(8,128)(2,1)S(1)}, bf16[1024,512]{1,0:T(8,128)(2,1)S(1)}, u32[]{:S(2)}, u32[]{:S(2)}) collective-permute-start(bf16[1024,512]{1,0:T(8,128)(2,1)S(1)} %packed.4.refs_4_.refs_0_), channel_id=1, source_target_pairs={{0,2},{1,3},{2,0},{3,1},{4,6},{5,7},{6,4},{7,5},{8,10},{9,11},{10,... | collective-permute-start | bytes 3145736 | tf_op jit(solution)/shard_map/ppermute | solution.py:824
  52.7 48.2 %collective-permute-start.8 = (bf16[1024,512]{1,0:T(8,128)(2,1)S(1)}, bf16[1024,512]{1,0:T(8,128)(2,1)}, u32[]{:S(2)}, u32[]{:S(2)}) collective-permute-start(bf16[1024,512]{1,0:T(8,128)(2,1)S(1)} %packed.4.refs_4_.refs_0_), channel_id=1, source_target_pairs={{0,1},{1,0},{2,3},{3,2},{4,5},{5,4},{6,7},{7,6},{8,9},{9,8},{10,11... | collective-permute-start | bytes 3145736 | tf_op jit(solution)/shard_map/ppermute | solution.py:824
  52.9 79.6 %collective-permute-start.12 = (bf16[1024,1024]{1,0:T(8,128)(2,1)}, bf16[1024,1024]{1,0:T(8,128)(2,1)S(1)}, u32[]{:S(2)}, u32[]{:S(2)}) collective-permute-start(bf16[1024,1024]{1,0:T(8,128)(2,1)} %packed.5.refs_4_.refs_0_.refs_1_), channel_id=1, source_target_pairs={{0,2},{1,3},{2,0},{3,1},{4,6},{5,7},{6,4},{7,5},{8,10},{9,11},{10,... | collective-permute-start | bytes 6291464 | tf_op jit(solution)/shard_map/ppermute | solution.py:824
  69.4 69.6 %collective-permute-start.11 = (bf16[1024,1024]{1,0:T(8,128)(2,1)}, bf16[1024,1024]{1,0:T(8,128)(2,1)}, u32[]{:S(2)}, u32[]{:S(2)}) collective-permute-start(bf16[1024,1024]{1,0:T(8,128)(2,1)} %packed.5.refs_4_.refs_0_.refs_1_), channel_id=1, source_target_pairs={{0,1},{1,0},{2,3},{3,2},{4,5},{5,4},{6,7},{7,6},{8,9},{9,8},{10,11... | collective-permute-start | bytes 6291464 | tf_op jit(solution)/shard_map/ppermute | solution.py:824
  94.7 39.9 %all-to-all-start.1 = ((bf16[32,4,16,256]{3,1,2,0:T(4,128)(2,1)}), bf16[32,4,16,256]{3,1,2,0:T(4,128)(2,1)}, u32[]{:S(2)}, u32[]{:S(2)}) async-start(bf16[32,4,16,256]{3,1,2,0:T(4,128)(2,1)} %bitcast.188), calls=%async_computation.1 | async-start | bytes 2097152 | tf_op jit(solution)/shard_map/all_to_all | solution.py:905
  154.1 31.4 %collective-permute-start.17 = (bf16[512,1024]{1,0:T(8,128)(2,1)S(1)}, bf16[512,1024]{1,0:T(8,128)(2,1)S(1)}, u32[]{:S(2)}, u32[]{:S(2)}) collective-permute-start(bf16[512,1024]{1,0:T(8,128)(2,1)S(1)} %get-tuple-element.67.nm.refs_2_), channel_id=1, source_target_pairs={{0,2},{1,3},{2,0},{3,1},{4,6},{5,7},{6,4},{7,5},{8,10},{9,11},{10,... | collective-permute-start | bytes 3145736 | tf_op jit(solution)/shard_map/ppermute | solution.py:1011
  209.1 26.2 %collective-permute-start.18 = (bf16[512,1024]{1,0:T(8,128)(2,1)}, bf16[512,1024]{1,0:T(8,128)(2,1)S(1)}, u32[]{:S(2)}, u32[]{:S(2)}) collective-permute-start(bf16[512,1024]{1,0:T(8,128)(2,1)} %copy-done.18), channel_id=1, source_target_pairs={{0,2},{1,3},{2,0},{3,1},{4,6},{5,7},{6,4},{7,5},{8,10},{9,11},{10,... | collective-permute-start | bytes 3145736 | tf_op jit(solution)/shard_map/ppermute | solution.py:1011
  218.8 37.2 %collective-permute-start.22 = (bf16[4,128,1024]{2,1,0:T(8,128)(2,1)S(1)}, bf16[4,128,1024]{2,1,0:T(8,128)(2,1)S(1)}, u32[]{:S(2)}, u32[]{:S(2)}) collective-permute-start(bf16[4,128,1024]{2,1,0:T(8,128)(2,1)S(1)} %dynamic-slice_bitcast_fusion.1), channel_id=1, source_target_pairs={{0,4},{4,0},{1,5},{5,1},{2,6},{6,2},{3,7},{7,3},{8,12},{12,8},{9,1... | collective-permute-start | bytes 3145736 | tf_op jit(solution)/shard_map/ppermute | solution.py:880
  226.2 39.9 %collective-permute-start.23 = (bf16[4,128,1024]{2,1,0:T(8,128)(2,1)S(1)}, bf16[4,128,1024]{2,1,0:T(8,128)(2,1)S(1)}, u32[]{:S(2)}, u32[]{:S(2)}) collective-permute-start(bf16[4,128,1024]{2,1,0:T(8,128)(2,1)S(1)} %dynamic-slice_bitcast_fusion), channel_id=1, source_target_pairs={{0,4},{4,0},{1,5},{5,1},{2,6},{6,2},{3,7},{7,3},{8,12},{12,8},{9,1... | collective-permute-start | bytes 3145736 | tf_op jit(solution)/shard_map/ppermute | solution.py:880
  229.7 38.4 %collective-permute-start.21 = (bf16[512,1024]{1,0:T(8,128)(2,1)}, bf16[512,1024]{1,0:T(8,128)(2,1)}, u32[]{:S(2)}, u32[]{:S(2)}) collective-permute-start(bf16[512,1024]{1,0:T(8,128)(2,1)} %broadcast_select_fusion.5), channel_id=1, source_target_pairs={{0,2},{1,3},{2,0},{3,1},{4,6},{5,7},{6,4},{7,5},{8,10},{9,11},{10,... | collective-permute-start | bytes 3145736 | tf_op jit(solution)/shard_map/ppermute | solution.py:1011
  276.9 118.7 %all-reduce.7.cloned.1.call-start = ((), (), s32[]{:S(2)}) async-start(), calls=%async_computation.4 | async-start | bytes 4194304 | tf_op jit(solution)/shard_map/psum | solution.py:897
  287.4 61.1 %collective-permute-start.26 = (bf16[1024,1024]{1,0:T(8,128)(2,1)}, bf16[1024,1024]{1,0:T(8,128)(2,1)}, u32[]{:S(2)}, u32[]{:S(2)}) collective-permute-start(bf16[1024,1024]{1,0:T(8,128)(2,1)} %self_weights.6.refs_5_), channel_id=1, source_target_pairs={{0,2},{1,3},{2,0},{3,1},{4,6},{5,7},{6,4},{7,5},{8,10},{9,11},{10,... | collective-permute-start | bytes 6291464 | tf_op jit(solution)/shard_map/ppermute | solution.py:824
  293.0 53.6 %all-to-all-start.2 = ((bf16[32,4,16,256]{3,1,2,0:T(4,128)(2,1)}), bf16[32,4,16,256]{3,1,2,0:T(4,128)(2,1)S(1)}, u32[]{:S(2)}, u32[]{:S(2)}) async-start(bf16[32,4,16,256]{3,1,2,0:T(4,128)(2,1)} %bitcast.40), calls=%async_computation.2 | async-start | bytes 2097152 | tf_op jit(solution)/shard_map/all_to_all | solution.py:916
  361.7 33.9 %collective-permute-start.27 = (bf16[1024,1024]{1,0:T(8,128)(2,1)}, bf16[1024,1024]{1,0:T(8,128)(2,1)}, u32[]{:S(2)}, u32[]{:S(2)}) collective-permute-start(bf16[1024,1024]{1,0:T(8,128)(2,1)} %cross_weights.4.refs_9_), channel_id=1, source_target_pairs={{0,1},{1,0},{2,3},{3,2},{4,5},{5,4},{6,7},{7,6},{8,9},{9,8},{10,11... | collective-permute-start | bytes 6291464 | tf_op jit(solution)/shard_map/ppermute | solution.py:824
  374.2 47.9 %collective-permute-start.30 = (bf16[1024,1024]{1,0:T(8,128)(2,1)}, bf16[1024,1024]{1,0:T(8,128)(2,1)}, u32[]{:S(2)}, u32[]{:S(2)}) collective-permute-start(bf16[1024,1024]{1,0:T(8,128)(2,1)} %cross_weights.5.refs_12_), channel_id=1, source_target_pairs={{0,1},{1,0},{2,3},{3,2},{4,5},{5,4},{6,7},{7,6},{8,9},{9,8},{10,11... | collective-permute-start | bytes 6291464 | tf_op jit(solution)/shard_map/ppermute | solution.py:824
  379.7 33.4 %all-to-all-start.3 = ((bf16[32,4,16,256]{3,1,2,0:T(4,128)(2,1)}), bf16[32,4,16,256]{3,1,2,0:T(4,128)(2,1)S(1)}, u32[]{:S(2)}, u32[]{:S(2)}) async-start(bf16[32,4,16,256]{3,1,2,0:T(4,128)(2,1)} %bitcast.53), calls=%async_computation.3 | async-start | bytes 2097152 | tf_op jit(solution)/shard_map/all_to_all | solution.py:916
  383.5 90.4 %all-reduce.9.cloned.1.call-start = ((), (), s32[]{:S(2)}) async-start(), calls=%async_computation.5 | async-start | bytes 2097152 | tf_op jit(solution)/shard_map/psum | solution.py:897
  419.7 27.8 %collective-permute-start.37 = (bf16[4,64,1024]{2,1,0:T(8,128)(2,1)}, bf16[4,64,1024]{2,1,0:T(8,128)(2,1)}, u32[]{:S(2)}, u32[]{:S(2)}) collective-permute-start(bf16[4,64,1024]{2,1,0:T(8,128)(2,1)} %dynamic-slice_bitcast_fusion.2), channel_id=1, source_target_pairs={{0,4},{4,0},{1,5},{5,1},{2,6},{6,2},{3,7},{7,3},{8,12},{12,8},{9,1... | collective-permute-start | bytes 1572872 | tf_op jit(solution)/shard_map/ppermute | solution.py:880
  432.8 43.5 %collective-permute-start.36 = (bf16[4,64,1024]{2,1,0:T(8,128)(2,1)}, bf16[4,64,1024]{2,1,0:T(8,128)(2,1)}, u32[]{:S(2)}, u32[]{:S(2)}) collective-permute-start(bf16[4,64,1024]{2,1,0:T(8,128)(2,1)} %dynamic-slice_bitcast_fusion.3), channel_id=1, source_target_pairs={{0,4},{4,0},{1,5},{5,1},{2,6},{6,2},{3,7},{7,3},{8,12},{12,8},{9,1... | collective-permute-start | bytes 1572872 | tf_op jit(solution)/shard_map/ppermute | solution.py:880
  446.1 38.4 %collective-permute-start.34 = (bf16[4,128,1024]{2,1,0:T(8,128)(2,1)}, bf16[4,128,1024]{2,1,0:T(8,128)(2,1)}, u32[]{:S(2)}, u32[]{:S(2)}) collective-permute-start(bf16[4,128,1024]{2,1,0:T(8,128)(2,1)} %slice_select_fusion.1), channel_id=1, source_target_pairs={{0,4},{4,0},{1,5},{5,1},{2,6},{6,2},{3,7},{7,3},{8,12},{12,8},{9,1... | collective-permute-start | bytes 3145736 | tf_op jit(solution)/shard_map/ppermute | solution.py:880
  449.6 26.8 %collective-permute-start.38 = (bf16[4,64,1024]{2,1,0:T(8,128)(2,1)}, bf16[4,64,1024]{2,1,0:T(8,128)(2,1)}, u32[]{:S(2)}, u32[]{:S(2)}) collective-permute-start(bf16[4,64,1024]{2,1,0:T(8,128)(2,1)} %fusion.16), channel_id=1, source_target_pairs={{0,2},{1,3},{2,0},{3,1},{4,6},{5,7},{6,4},{7,5},{8,10},{9,11},{10,... | collective-permute-start | bytes 1572872 | tf_op jit(solution)/shard_map/ppermute | solution.py:824
  451.8 31.4 %collective-permute-start.35 = (bf16[4,64,1024]{2,1,0:T(8,128)(2,1)}, bf16[4,64,1024]{2,1,0:T(8,128)(2,1)}, u32[]{:S(2)}, u32[]{:S(2)}) collective-permute-start(bf16[4,64,1024]{2,1,0:T(8,128)(2,1)} %copy-done.67), channel_id=1, source_target_pairs={{0,4},{4,0},{1,5},{5,1},{2,6},{6,2},{3,7},{7,3},{8,12},{12,8},{9,1... | collective-permute-start | bytes 1572872 | tf_op jit(solution)/shard_map/ppermute | solution.py:880
  487.8 58.0 %all-reduce.11.cloned.1.call-start = ((), (), s32[]{:S(2)}) async-start(), calls=%async_computation.6 | async-start | bytes 2228224 | tf_op jit(solution)/shard_map/psum | solution.py:897
  491.5 26.4 %collective-permute-start.40 = (bf16[4,128,1024]{2,1,0:T(8,128)(2,1)}, bf16[4,128,1024]{2,1,0:T(8,128)(2,1)}, u32[]{:S(2)}, u32[]{:S(2)}) collective-permute-start(bf16[4,128,1024]{2,1,0:T(8,128)(2,1)} %broadcast_select_fusion.2), channel_id=1, source_target_pairs={{0,4},{4,0},{1,5},{5,1},{2,6},{6,2},{3,7},{7,3},{8,12},{12,8},{9,1... | collective-permute-start | bytes 3145736 | tf_op jit(solution)/shard_map/ppermute | solution.py:880
  494.0 58.6 %collective-permute-start.42 = (bf16[4,128,1024]{2,1,0:T(8,128)(2,1)}, bf16[4,128,1024]{2,1,0:T(8,128)(2,1)S(1)}, u32[]{:S(2)}, u32[]{:S(2)}) collective-permute-start(bf16[4,128,1024]{2,1,0:T(8,128)(2,1)} %slice_select_fusion), channel_id=1, source_target_pairs={{0,4},{4,0},{1,5},{5,1},{2,6},{6,2},{3,7},{7,3},{8,12},{12,8},{9,1... | collective-permute-start | bytes 3145736 | tf_op jit(solution)/shard_map/ppermute | solution.py:880
  547.2 26.6 %collective-permute-start.41 = (bf16[4,136,1024]{2,1,0:T(8,128)(2,1)S(1)}, bf16[4,136,1024]{2,1,0:T(8,128)(2,1)S(1)}, u32[]{:S(2)}, u32[]{:S(2)}) collective-permute-start(bf16[4,136,1024]{2,1,0:T(8,128)(2,1)S(1)} %broadcast_select_fusion.1.own), channel_id=1, source_target_pairs={{0,4},{4,0},{1,5},{5,1},{2,6},{6,2},{3,7},{7,3},{8,12},{12,8},{9,1... | collective-permute-start | bytes 3342344 | tf_op jit(solution)/shard_map/ppermute | solution.py:880
  (94 other events, 912.1 us)
Sparse Core Ops, SparseCore 0:
  282.2 112.2 all-reduce.6
  419.0 53.6 all-reduce.8
  491.5 54.2 all-reduce.10
